TPU v7x, 32 devices: a whole 2x2x4 slice. The times are simulated.
32 devices in a mesh: mem: 2 (over x), par: 16 (over z, y, core).
Axes of the slice: x: 2, y: 2, z: 4, core: 2. Of those that a mesh axis runs over, the one named last changes fastest.
Arguments:
- operator: float32 [32768, 512], P('par'), may hold values from -0.046875 to 0.046875
- ensemble: float32 [256, 32768], P('mem', 'par'), may hold values from -6 to 6
- noise: float32 [256, 512], P('mem'), may hold values from -6 to 6
- observations: float32 [16384], replicated, may hold values from -6 to 6
- variances: float32 [16384], replicated, may hold values from 0.25 to 4
- rows: int32 [512], replicated, may hold values from 0 to 16383
Outputs:
- updated: float32 [256, 32768], P('mem', 'par')
Inputs may be any that keep to these rules, and one draw needn't show every extreme that they name: `rows`: indices into the observations; they may repeat.
All inputs are finite; a program needn't handle non-finite values.
Results may differ from a plain program's by a relative error of at most 0.00017.
Values sent between devices are 32-bit elements; how exact they have to be, the bound alone decides.
No kernel may reach another device: no remote copies, remote signals or barrier semaphores. Data moves between devices by JAX's collectives and lax.ppermute only.
A program may use at most 64 MiB of HBM per device.

v0:
```python
import jax
import jax.numpy as jnp
from jax import lax
from jax.sharding import PartitionSpec as P


def cholesky_solve(matrix, right):
    factor = jnp.linalg.cholesky(matrix)
    inner = lax.linalg.triangular_solve(factor, right, left_side=True, lower=True)
    return lax.linalg.triangular_solve(factor, inner, left_side=True, lower=True, transpose_a=True)


def per_device(operator, ensemble, noise, observations, variances, rows):
    highest = lax.Precision.HIGHEST
    own_members = ensemble.shape[0]
    member_index = lax.axis_index("mem")
    partial_fwd = jnp.dot(ensemble, operator, precision=highest, preferred_element_type=jnp.float32)
    forward = lax.psum(partial_fwd, "par")
    obs_rows = jnp.take(observations, rows)
    var_rows = jnp.take(variances, rows)
    residual = obs_rows[None, :] + jnp.sqrt(var_rows)[None, :] * noise - forward
    all_forward, all_residual = (
        lax.all_gather(forward, "mem", axis=0, tiled=True),
        lax.all_gather(residual, "mem", axis=0, tiled=True),
    )
    spread = all_forward - jnp.mean(all_forward, axis=0, keepdims=True)
    weighted = spread / var_rows[None, :]
    gram_part = jnp.dot(weighted, spread.T, precision=highest, preferred_element_type=jnp.float32)
    cross_part = jnp.dot(
        weighted, all_residual.T, precision=highest, preferred_element_type=jnp.float32
    )
    members = all_forward.shape[0]
    gram = gram_part + (members - 1) * jnp.eye(members, dtype=jnp.float32)
    weights = cholesky_solve(gram, cross_part)
    gathered = lax.all_gather(ensemble, "mem", axis=0, tiled=True)
    deviation = gathered - jnp.mean(gathered, axis=0, keepdims=True)
    own_columns = lax.dynamic_slice_in_dim(weights, member_index * own_members, own_members, 1)
    change = jnp.dot(
        own_columns.T, deviation, precision=highest, preferred_element_type=jnp.float32
    )
    return ensemble + change


def solution(mesh):
    return jax.shard_map(
        per_device,
        mesh=mesh,
        in_specs=(P("par", None), P("mem", "par"), P("mem", None), P(), P(), P()),
        out_specs=P("mem", "par"),
        check_vma=False,
    )
```

profile of v0, /device:TPU:0, one launch (start us, length us, event | category | flops | bytes accessed | tf_op | source)
XLA Modules:
  0.0 198.3 jit_solution(7675143033784119858)
XLA Ops:
  7.4 5.7 %fusion.27 = f32[128,512]{1,0:T(8,128)} fusion(f32[128,2048]{1,0:T(8,128)} %param.9, f32[2048,512]{1,0:T(8,128)} %param.8), kind=kOutput, calls=%fused_computation.62 | convolution fusion | flops 1610612736 | bytes 5505024 | tf_op jit(solution)/shard_map/dot_general | solution.py:17
  13.1 0.5 all-gather.2.cloned.1.call-update
  13.7 3.1 %gather_fusion = f32[512]{0:T(512)S(1)} fusion(f32[16384]{0:T(1024)S(1)} %copy-done, s32[1024]{0:T(1024)S(1)} %pad_clamp_fusion), kind=kCustom, calls=%fused_computation.clone | custom fusion | bytes 6144 | tf_op jit(solution)/shard_map/jit(_take)/gather | solution.py:20
  16.9 3.1 %gather_fusion.1 = f32[512]{0:T(512)S(1)} fusion(f32[16384]{0:T(1024)S(1)} %copy-done.1, s32[1024]{0:T(1024)S(1)} %pad_clamp_fusion), kind=kCustom, calls=%fused_computation.1.clone | custom fusion | bytes 6144 | tf_op jit(solution)/shard_map/jit(_take)/gather | solution.py:19
  20.1 84.6 %all-reduce.3.cloned.1.call-done = f32[128,512]{1,0:T(8,128)} async-done(((f32[128,512]{1,0:T(8,128)}), f32[128,512]{1,0:T(8,128)}) %all-reduce.3.cloned.1.call-update) | async-done | bytes 262160 | tf_op jit(solution)/shard_map/psum | solution.py:18
  104.7 9.8 %all_gather.9 = f32[256,512]{1,0:T(8,128)S(1)} all-gather(f32[128,512]{1,0:T(8,128)} %all-reduce.3.cloned.1.call-done), channel_id=1, replica_groups=mesh['mem'=2,'par'=16] {'mem'}, dimensions={0}, use_global_device_ids=true | all-gather | bytes 786432 | tf_op jit(solution)/shard_map/all_gather | solution.py:23
  114.6 0.6 fusion.2
  115.5 11.7 %cholesky.49 = f32[128,128]{1,0:T(8,128)S(1)} custom-call(f32[128,128]{1,0:T(8,128)S(1)} %cholesky.115), custom_call_target="Cholesky" | custom-call | tf_op jit(solution)/shard_map/jit(cholesky)/cholesky | solution.py:8
  127.2 9.8 %custom-call.16 = f32[1,128,128]{1,2,0:T(8,128)S(1)} custom-call(f32[1,128,128]{2,1,0:T(8,128)S(1)} %get-tuple-element.29), custom_call_target="InvertDiagBlocksLowerTriangular" | custom-call | tf_op jit(solution)/shard_map/jit(cholesky)/cholesky | solution.py:8
  137.5 11.7 %cholesky.103 = f32[128,128]{1,0:T(8,128)S(1)} custom-call(f32[128,128]{1,0:T(8,128)S(1)} %convolution_subtract_fusion.2), custom_call_target="Cholesky" | custom-call | tf_op jit(solution)/shard_map/jit(cholesky)/cholesky | solution.py:8
  149.3 0.7 compare_reduce_fusion
  151.3 4.1 %while.1 = (s32[]{:T(128)}, f32[256,256]{1,0:T(8,128)S(1)}, s32[2,2]{1,0:T(2,128)S(1)}, f32[2,128,128]{2,1,0:T(8,128)S(1)}, s32[]{:T(128)}) while((s32[]{:T(128)}, f32[256,256]{1,0:T(8,128)S(1)}, s32[2,2]{1,0:T(2,128)S(1)}, f32[2,128,128]{2,1,0:T(8,128)S(1)}, s32[]{:T(128)}) %tuple.26), condition=%wide.while_cond, body=%wide.while_body.sunk | while | flops 2 | bytes 131181 | solution.py:10
  151.5 0.6 fusion.39
  152.1 1.4 bitcast_dynamic-update-slice_fusion.2
  153.5 0.6 fusion.39
  154.1 1.4 bitcast_dynamic-update-slice_fusion.2
  155.5 19.7 %custom-call.17 = f32[2,128,128]{1,2,0:T(8,128)S(1)} custom-call(f32[2,128,128]{2,1,0:T(8,128)S(1)} %get-tuple-element.13), custom_call_target="InvertDiagBlocksLowerTriangular" | custom-call | tf_op jit(solution)/shard_map/triangular_solve | solution.py:10
  175.2 8.6 %all_gather.10 = f32[256,512]{1,0:T(8,128)S(1)} all-gather(f32[128,512]{1,0:T(8,128)S(1)} %add_subtract_fusion), channel_id=1, replica_groups=mesh['mem'=2,'par'=16] {'mem'}, dimensions={0}, use_global_device_ids=true | all-gather | bytes 786432 | tf_op jit(solution)/shard_map/all_gather | solution.py:24
  183.9 0.6 fusion.4
  185.1 0.3 fusion.20
  185.7 0.3 convolution_subtract_fusion
  186.3 1.9 reduce_sum.19
  188.2 0.3 copy-done.3
  188.5 2.3 %convolution_add_fusion = f32[128,2048]{1,0:T(8,128)} fusion(f32[128,2048]{1,0:T(8,128)S(1)} %copy-done.2, f32[256,2048]{1,0:T(8,128)S(1)} %copy-done.3, f32[2048]{0:T(1024)S(1)} %broadcast_multiply_fusion, s32[]{:T(128)S(6)} %select_n.15, f32[128,256]{1,0:T(8,128)S(1)} %fusion.18, f32[128,256]{1,0:T(8,128)S(1)} %fusion.19), kind=kOutput, calls=%fused_computation.4 | convolution fusion | flops 806125568 | bytes 4464644 | tf_op jit(solution)/shard_map/dot_general | solution.py:38
  (42 shorter events, 2.2 us)
Async XLA Ops:
  7.4 6.4 %copy-start = (f32[16384]{0:T(1024)S(1)}, f32[16384]{0:T(1024)}, u32[]{:S(2)}) copy-start(f32[16384]{0:T(1024)} %param.12) | copy-start | bytes 196612
  7.4 6.3 %copy-start.6 = (s32[512]{0:T(512)S(1)}, s32[512]{0:T(512)}, u32[]{:S(2)}) copy-start(s32[512]{0:T(512)} %param.13) | copy-start | bytes 6148
  7.4 97.3 %all-reduce.3.cloned.1.call-start = ((), (), s32[]{:S(2)}) async-start(), calls=%async_computation | async-start | bytes 524288 | tf_op jit(solution)/shard_map/psum | solution.py:18
  13.1 3.8 %copy-start.1 = (f32[16384]{0:T(1024)S(1)}, f32[16384]{0:T(1024)}, u32[]{:S(2)}) copy-start(f32[16384]{0:T(1024)} %param.11) | copy-start | bytes 196612
  13.1 173.2 %all-gather.2.cloned.1.call-start = ((), (), s32[]{:S(2)}) async-start(), calls=%async_computation.1 | async-start | bytes 3145728 | tf_op jit(solution)/shard_map/all_gather | solution.py:35
  115.2 59.9 %copy-start.4 = (f32[128,512]{1,0:T(8,128)S(1)}, f32[128,512]{1,0:T(8,128)}, u32[]{:S(2)}) copy-start(f32[128,512]{1,0:T(8,128)} %all-reduce.3.cloned.1.call-done) | copy-start | bytes 786436
  115.2 59.9 %copy-start.5 = (f32[128,512]{1,0:T(8,128)S(1)}, f32[128,512]{1,0:T(8,128)}, u32[]{:S(2)}) copy-start(f32[128,512]{1,0:T(8,128)} %param.10) | copy-start | bytes 786436
  184.5 3.7 %copy-start.2 = (f32[128,2048]{1,0:T(8,128)S(1)}, f32[128,2048]{1,0:T(8,128)}, u32[]{:S(2)}) copy-start(f32[128,2048]{1,0:T(8,128)} %param.9) | copy-start | bytes 3145732
  186.3 2.2 %copy-start.3 = (f32[256,2048]{1,0:T(8,128)S(1)}, f32[256,2048]{1,0:T(8,128)}, u32[]{:S(2)}) copy-start(f32[256,2048]{1,0:T(8,128)} %all-gather.2.cloned.1.call-done) | copy-start | bytes 6291460
Sparse Core Ops, SparseCore 0:
  13.2 91.4 all-reduce.2
Sparse Core Ops, SparseCore 1:
  15.1 35.7 all-gather.1
where the time goes:
time: 198 us
  waiting for transfers between devices  85.2 us (43%)
  other arithmetic  55.7 us (28%)
  blocking collectives  18.4 us (9%)
  between operations  16.4 us (8%)
  matrix products  11.5 us (6%)
  local copies, waits for them, and re-layouts  10.8 us (5%)
    psum x1, waiting for transfers between devices, per_device(): forward = lax.psum(partial_fwd, 'par')  84.6 us
    another operation x6, other arithmetic, cholesky_solve(): factor = jnp.linalg.cholesky(matrix)  34 us
    another operation x3, other arithmetic, cholesky_solve(): lax.linalg.triangular_solve(factor, inner, left_side=True, lower=True, tr...  19.7 us
    all_gather x1, blocking collectives, per_device(): lax.all_gather(forward, 'mem', axis=0, tiled=True)  9.8 us
    all_gather x1, blocking collectives, per_device(): lax.all_gather(residual, 'mem', axis=0, tiled=True)  8.65 us
    dot_general x1, matrix products, per_device(): jnp.dot(ensemble, operator, precision=highest, preferred_element_type=jnp...  5.69 us
  transfers between devices with their start and end apart: 2, of which 1 were waited for; matrix products, arithmetic and copies ran while one was open for 34% of the time, Pallas kernels for 0%

commit v1 on v0

v1 whole, which is shorter than its diff:
```python
import functools

import jax
import jax.numpy as jnp
from jax import lax
from jax.experimental import pallas as pl
from jax.experimental.pallas import tpu as pltpu
from jax.sharding import PartitionSpec as P

f32 = jnp.float32
HIGHEST = lax.Precision.HIGHEST
SUB, LANE = 8, 128
VMEM = pl.BlockSpec(memory_space=pltpu.VMEM)
SMEM = pl.BlockSpec(memory_space=pltpu.SMEM)
ANY = pl.BlockSpec(memory_space=pl.ANY)


def dot(a, b, dims, precision=HIGHEST):
    return lax.dot_general(a, b, (dims, ((), ())), precision=precision, preferred_element_type=f32)


def add_all(terms):
    terms = list(terms)
    while len(terms) > 1:
        pairs = [terms[i] + terms[i + 1] for i in range(0, len(terms) - 1, 2)]
        terms = pairs + ([terms[-1]] if len(terms) % 2 else [])
    return terms[0]


def small_inverse(e):
    n = len(e)

    def at(m, i, k):
        return m[min(i, k)][max(i, k)]

    if n == 2:
        a, b, c = e[0][0], e[0][1], e[1][1]
        d = 1.0 / (a * c - b * b)
        return [[c * d, -(b * d)], [None, a * d]]
    m = n // 2
    span = range(m)
    top = small_inverse([[at(e, i, k) for k in span] for i in span])
    side = [[at(e, i, m + k) for k in span] for i in span]
    t = [[add_all(at(top, i, l) * side[l][k] for l in span) for k in span] for i in span]
    rest = [
        [at(e, m + i, m + k) - add_all(side[l][i] * t[l][k] for l in span) if i <= k else None for k in span]
        for i in span
    ]
    low = small_inverse(rest)
    u = [[add_all(t[i][l] * at(low, l, k) for l in span) for k in span] for i in span]
    out = [[None] * n for _ in range(n)]
    for i in span:
        for k in span:
            if i <= k:
                out[i][k] = top[i][k] + add_all(u[i][l] * t[k][l] for l in span)
                out[m + i][m + k] = low[i][k]
            out[i][m + k] = -u[i][k]
    return out


def across(v, k):
    return jnp.broadcast_to(v[:, k : k + 1], v.shape)


def down(v, i):
    return jnp.broadcast_to(v[i : i + 1, :], v.shape)


def block_inverse(matrix):
    lane = lax.broadcasted_iota(jnp.int32, (SUB, LANE), 1)
    sub = lax.broadcasted_iota(jnp.int32, (SUB, LANE), 0)
    n = LANE // SUB
    m = [matrix[SUB * i : SUB * (i + 1), :] for i in range(n)]
    for j in range(n):
        at = SUB * j
        here = (lane >= at) & (lane < at + SUB)
        cols = [across(m[j], at + k) for k in range(SUB)]
        inv = small_inverse([[down(cols[k], i) if i <= k else None for k in range(SUB)] for i in range(SUB)])
        row = jnp.where(here, (lane - at == sub).astype(f32), m[j])
        rows = [down(row, k) for k in range(SUB)]
        new = [add_all(inv[min(i, k)][max(i, k)] * rows[k] for k in range(SUB)) for i in range(SUB)]
        for d in range(1, n):
            i = (j + d) % n
            drop = add_all(across(m[i], at + k) * new[k] for k in range(SUB))
            m[i] = jnp.where(here, 0.0, m[i]) - drop
        done = new[0]
        for i in range(1, SUB):
            done = jnp.where(sub == i, new[i], done)
        m[j] = done
    return jnp.concatenate(m, axis=0)


def forward_kernel(bits, ens, op, keep, send, acc):
    step = pl.program_id(0)

    @pl.when(step == 0)
    def _():
        acc[...] = jnp.zeros_like(acc)

    acc[...] += dot(ens[...], op[...], ((1,), (0,)))

    @pl.when(step == pl.num_programs(0) - 1)
    def _():
        half = keep.shape[0]
        mine = pl.multiple_of(bits[0] * half, SUB)
        other = pl.multiple_of((1 - bits[0]) * half, SUB)
        keep[...] = acc[pl.ds(mine, half), :]
        send[...] = acc[pl.ds(other, half), :]


def forward(ens, op, bits):
    members, params = ens.shape
    rows = op.shape[1]
    steps = 4 if params % (4 * LANE) == 0 else 1
    depth = params // steps
    half = jax.ShapeDtypeStruct((members // 2, rows), f32)
    whole = pl.BlockSpec((members // 2, rows), lambda i: (0, 0))
    return pl.pallas_call(
        forward_kernel,
        grid=(steps,),
        out_shape=(half, half),
        in_specs=[
            SMEM,
            pl.BlockSpec((members, depth), lambda i: (0, i)),
            pl.BlockSpec((depth, rows), lambda i: (i, 0)),
        ],
        out_specs=(whole, whole),
        scratch_shapes=[pltpu.VMEM((members, rows), f32)],
        cost_estimate=pl.CostEstimate(
            flops=2 * members * params * rows, bytes_accessed=4 * (members * params + params * rows), transcendentals=0
        ),
        name="forward",
    )(bits, ens, op)


def lookup_kernel(rows, obs, var, noise, target, inverse_var):
    index = rows[...]
    high = lax.shift_right_logical(index, 7)
    low = lax.bitwise_and(index, LANE - 1)
    count = index.shape[1]
    blocks = obs.shape[0]
    pick_high = (lax.broadcasted_iota(jnp.int32, (blocks, count), 0) == high).astype(f32)
    pick_low = (lax.broadcasted_iota(jnp.int32, (LANE, count), 0) == low).astype(f32)
    obs_rows = jnp.sum(dot(obs[...], pick_high, ((0,), (0,))) * pick_low, axis=0, keepdims=True)
    var_rows = jnp.sum(dot(var[...], pick_high, ((0,), (0,))) * pick_low, axis=0, keepdims=True)
    target[...] = obs_rows + jnp.sqrt(var_rows) * noise[...]
    inverse_var[...] = jnp.broadcast_to(1.0 / var_rows, inverse_var.shape)


def lookup(rows, obs, var, noise):
    count = rows.shape[0]
    return pl.pallas_call(
        lookup_kernel,
        out_shape=(
            jax.ShapeDtypeStruct(noise.shape, f32),
            jax.ShapeDtypeStruct((SUB, count), f32),
        ),
        in_specs=[VMEM] * 4,
        out_specs=(VMEM, VMEM),
        cost_estimate=pl.CostEstimate(flops=2 * obs.shape[0] * LANE * count * 12, bytes_accessed=1 << 20, transcendentals=0),
        name="lookup",
    )(rows.reshape(1, count), obs.reshape(-1, LANE), var.reshape(-1, LANE), noise)


def solve_kernel(places, own, bits, *refs):
    count = len(places)
    pieces = refs[:count]
    target, inverse_var = refs[count : count + 2]
    weights = refs[count + 2]
    fwd = refs[count + 3]
    rows = pieces[0].shape[0]
    for piece, (far, dy, dc) in zip(pieces, places):
        core = bits[0] if dc == 0 else 1 - bits[0]
        side = bits[1] if dy == 0 else 1 - bits[1]
        fwd[pl.ds(pl.multiple_of(far * own + (core * 2 + side) * rows, SUB), rows), :] = piece[...]
    members = fwd.shape[0]
    spread = fwd[...] - jnp.mean(fwd[...], axis=0, keepdims=True)
    weighted = spread * inverse_var[0:1, :]
    gram = dot(weighted, spread, ((1,), (1,)))
    cross = dot(weighted, target[...] - fwd[0:own, :], ((1,), (1,)))
    blocks = members // LANE
    eye = (
        lax.broadcasted_iota(jnp.int32, (LANE, LANE), 0) == lax.broadcasted_iota(jnp.int32, (LANE, LANE), 1)
    ).astype(f32) * (members - 1)
    cut = lambda i: slice(i * LANE, (i + 1) * LANE)
    g = [[gram[cut(i), cut(k)] + (eye if i == k else 0.0) for k in range(blocks)] for i in range(blocks)]
    c = [cross[cut(i), :] for i in range(blocks)]
    t = [[None] * blocks for _ in range(blocks)]
    for j in range(blocks):
        inv = block_inverse(g[j][j])
        c[j] = dot(inv, c[j], ((1,), (0,)))
        for k in range(j + 1, blocks):
            t[j][k] = dot(inv, g[j][k], ((1,), (0,)))
        for i in range(j + 1, blocks):
            c[i] = c[i] - dot(g[i][j], c[j], ((1,), (0,)))
            for k in range(j + 1, blocks):
                g[i][k] = g[i][k] - dot(g[i][j], t[j][k], ((1,), (0,)))
    for j in reversed(range(blocks)):
        for k in range(j + 1, blocks):
            c[j] = c[j] - dot(t[j][k], c[k], ((1,), (0,)))
    w = jnp.concatenate(c, axis=0)
    weights[...] = (w - jnp.mean(w, axis=0, keepdims=True)).T


def solve(pieces, places, target, inverse_var, bits, members):
    own, rows = target.shape
    return pl.pallas_call(
        functools.partial(solve_kernel, places, own),
        out_shape=jax.ShapeDtypeStruct((own, members), f32),
        in_specs=[SMEM] + [VMEM] * (len(pieces) + 2),
        out_specs=VMEM,
        scratch_shapes=[pltpu.VMEM((members, rows), f32)],
        cost_estimate=pl.CostEstimate(flops=2 * members * members * rows * 12, bytes_accessed=1 << 20, transcendentals=0),
        name="solve",
    )(bits, *pieces, target, inverse_var)


def update_kernel(weights, *refs):
    out = refs[-1]
    ens = refs[:-1]
    own = ens[0].shape[0]
    total = ens[0][...]
    for far, part in enumerate(ens):
        total = total + dot(weights[:, far * own : (far + 1) * own], part[...], ((1,), (0,)))
    out[...] = total


def update(weights, ens):
    own, params = ens[0].shape
    steps = 4 if params % (4 * LANE) == 0 else 1
    block = pl.BlockSpec((own, params // steps), lambda i: (0, i))
    return pl.pallas_call(
        update_kernel,
        grid=(steps,),
        out_shape=jax.ShapeDtypeStruct((own, params), f32),
        in_specs=[pl.BlockSpec(weights.shape, lambda i: (0, 0))] + [block] * len(ens),
        out_specs=block,
        cost_estimate=pl.CostEstimate(
            flops=2 * own * weights.shape[1] * params, bytes_accessed=4 * params * (own + weights.shape[1]), transcendentals=0
        ),
        name="update",
    )(weights, *ens)


def per_device(n_mem, n_par, operator, ensemble, noise, observations, variances, rows):
    index = lax.axis_index("par")
    core, side = index % 2, (index // 2) % 2
    bits = jnp.stack([core, side]).astype(jnp.int32)

    def swap(x, far, near):
        pairs = [
            (m * n_par + p, (m ^ far) * n_par + (p ^ near)) for m in range(n_mem) for p in range(n_par)
        ]
        return lax.ppermute(x, ("mem", "par"), pairs)

    ens = [ensemble] + [swap(ensemble, far, 0) for far in range(1, n_mem)]
    keep, send = forward(ensemble, operator, bits)
    part = keep + swap(send, 0, 1)
    size = part.shape[0] // 2
    total = lax.dynamic_slice_in_dim(part, side * size, size, 0) + swap(
        lax.dynamic_slice_in_dim(part, (1 - side) * size, size, 0), 0, 2
    )
    stride = 4
    while stride < n_par:
        ways = min(4, n_par // stride)
        total = add_all([total] + [swap(total, 0, d * stride) for d in range(1, ways)])
        stride *= ways
    target, inverse_var = lookup(rows, observations, variances, noise)
    places = [(far, dy, 0) for far in range(n_mem) for dy in range(2)]
    pieces = [total if (far, dy) == (0, 0) else swap(total, far, 2 * dy) for far, dy, _ in places]
    pieces += [swap(piece, 0, 1) for piece in pieces]
    places += [(far, dy, 1) for far, dy, _ in places]
    members = ensemble.shape[0] * n_mem
    weights = solve(pieces, places, target, inverse_var, bits, members)
    return update(weights, ens)


def solution(mesh):
    return jax.shard_map(
        functools.partial(per_device, mesh.shape["mem"], mesh.shape["par"]),
        mesh=mesh,
        in_specs=(P("par", None), P("mem", "par"), P("mem", None), P(), P(), P()),
        out_specs=P("mem", "par"),
        check_vma=False,
    )
```

time: 198 us -> 57.7 us (0.29)
  waiting for transfers between devices: 85.2 us -> 10.8 us
  other arithmetic: 55.7 us -> 1.6 us
  Pallas kernels: 0 us -> 29.5 us
  blocking collectives: 18.4 us -> 0 us
  between operations: 16.4 us -> 0.14 us
  starting transfers between devices: 0.05 us -> 13.6 us
  matrix products: 11.5 us -> 0 us
  local copies, waits for them, and re-layouts: 10.8 us -> 1.67 us
    psum x1 -> x0, waiting for transfers between devices: 84.6 us -> none  [per_device(): forward = lax.psum(partial_fwd, 'par')]
    another operation x9 -> x1, other arithmetic: 53.7 us -> 0.65 us  [per_device(): bits = jnp.stack([core, side]).astype(jnp.int32)]
    pallas_call x0 -> x4, Pallas kernels: none -> 29.5 us  [the longest x1 17 us: solve(): pl.pallas_call(functools.partial(solve_kernel, places, own), out_shape=ja...]
    all_gather x2 -> x0, blocking collectives: 18.4 us -> none  [the longest x1 9.8 us: per_device(): lax.all_gather(forward, 'mem', axis=0, tiled=True)]
    ppermute x0 -> x13, starting transfers between devices: none -> 13.6 us  [swap(): return lax.ppermute(x, ('mem', 'par'), pairs)]
    ppermute x0 -> x13, waiting for transfers between devices: none -> 10.8 us  [swap(): return lax.ppermute(x, ('mem', 'par'), pairs)]
    dot_general x4 -> x0, matrix products: 9.26 us -> none  [the longest x1 5.69 us: per_device(): jnp.dot(ensemble, operator, precision=highest, preferred_element_type=jnp...]
    gather x2 -> x0, local copies, waits for them, and re-layouts: 6.29 us -> none  [the longest x1 3.14 us: per_device(): var_rows = jnp.take(variances, rows)]
  transfers between devices with their start and end apart: 2 -> 13, of which waited for: 1 -> 6; matrix products, arithmetic and copies ran while one was open for 34% -> 0% of each run, Pallas kernels for 0% -> 34%
where the time goes in v1:
time: 57.7 us; the launch traced here: 57.4 us
  Pallas kernels  29.5 us (51%)
  starting transfers between devices  13.6 us (24%)
  waiting for transfers between devices  10.8 us (19%)
  local copies, waits for them, and re-layouts  1.67 us (3%)
  other arithmetic  1.6 us (3%)
    pallas_call x1, Pallas kernels, solve(): pl.pallas_call(functools.partial(solve_kernel, places, own), out_shape=ja...  17 us
    ppermute x13, starting transfers between devices, swap(): return lax.ppermute(x, ('mem', 'par'), pairs)  13.6 us
    ppermute x13, waiting for transfers between devices, swap(): return lax.ppermute(x, ('mem', 'par'), pairs)  10.8 us
    pallas_call x1, Pallas kernels, forward(): pl.pallas_call(forward_kernel, grid=(steps,), out_shape=(half, half), in_...  5.48 us
    pallas_call x1, Pallas kernels, update(): pl.pallas_call(update_kernel, grid=(steps,), out_shape=jax.ShapeDtypeStru...  4.67 us
    pallas_call x1, Pallas kernels, lookup(): pl.pallas_call(lookup_kernel, out_shape=(jax.ShapeDtypeStruct(noise.shape...  2.44 us
    unnamed x20, local copies, waits for them, and re-layouts  1.65 us
  transfers between devices with their start and end apart: 13, of which 6 were waited for; matrix products, arithmetic and copies ran while one was open for 0% of the time, Pallas kernels for 34%

profile of v1, /device:TPU:0, one launch (start us, length us, event | category | flops | bytes accessed | tf_op | source)
XLA Modules:
  0.0 57.4 jit_solution(203756352289794155)
XLA Ops:
  0.0 0.6 %pad_add_fusion.bits = s32[2]{0:T(128)} fusion(s32[1]{0:T(128)} %bitcast.1, s32[1]{0:T(128)} %bitcast), kind=kLoop, calls=%fused_computation.2 | loop fusion | flops 2 | bytes 16 | tf_op jit(solution)/shard_map/stack | solution.py:248
  0.6 5.5 %forward.1 = (f32[64,512]{1,0:T(8,128)}, f32[64,512]{1,0:T(8,128)}) custom-call(s32[2]{0:T(128)} %pad_add_fusion.bits, f32[128,2048]{1,0:T(8,128)} %refs_0_.1, f32[2048,512]{1,0:T(8,128)} %op.1), custom_call_target="tpu_custom_call" | custom-call | flops 268435456 | bytes 5242880 | tf_op jit(solution)/shard_map/forward/pallas_call | solution.py:118
  6.1 0.5 collective-permute-start
  6.6 1.2 %collective-permute-done = f32[64,512]{1,0:T(8,128)S(1)} collective-permute-done((f32[64,512]{1,0:T(8,128)}, f32[64,512]{1,0:T(8,128)S(1)}, u32[]{:S(2)}, u32[]{:S(2)}) %collective-permute-start) | collective-permute-done | bytes 131104 | tf_op jit(solution)/shard_map/ppermute | solution.py:254
  7.8 0.9 %add.31 = f32[64,512]{1,0:T(8,128)S(1)} add(f32[64,512]{1,0:T(8,128)} %get-tuple-element.9, f32[64,512]{1,0:T(8,128)S(1)} %collective-permute-done) | non-fusion elementwise | flops 32768 | bytes 393216 | tf_op jit(solution)/shard_map/add | solution.py:258
  8.7 2.9 %collective-permute-start.1 = (f32[32,512]{1,0:T(8,128)S(1)}, f32[32,512]{1,0:T(8,128)S(1)}, u32[]{:S(2)}, u32[]{:S(2)}) collective-permute-start(f32[32,512]{1,0:T(8,128)S(1)} %constant_dynamic-slice_fusion), channel_id=1, source_target_pairs={{0,2},{1,3},{2,0},{3,1},{4,6},{5,7},{6,4},{7,5},{8,10},{9,11},{10,... | collective-permute-start | bytes 196616 | tf_op jit(solution)/shard_map/ppermute | solution.py:254
  11.7 2.4 %collective-permute-done.1 = f32[32,512]{1,0:T(8,128)S(1)} collective-permute-done((f32[32,512]{1,0:T(8,128)S(1)}, f32[32,512]{1,0:T(8,128)S(1)}, u32[]{:S(2)}, u32[]{:S(2)}) %collective-permute-start.1) | collective-permute-done | bytes 65568 | tf_op jit(solution)/shard_map/ppermute | solution.py:254
  14.1 4.0 %collective-permute-start.4 = (f32[32,512]{1,0:T(8,128)S(1)}, f32[32,512]{1,0:T(8,128)S(1)}, u32[]{:S(2)}, u32[]{:S(2)}) collective-permute-start(f32[32,512]{1,0:T(8,128)S(1)} %dynamic-slice_add_fusion), channel_id=1, source_target_pairs={{0,12},{1,13},{2,14},{3,15},{4,8},{5,9},{6,10},{7,11},{8,4},{9,5},... | collective-permute-start | bytes 196616 | tf_op jit(solution)/shard_map/ppermute | solution.py:254
  18.1 0.6 %collective-permute-start.2 = (f32[32,512]{1,0:T(8,128)S(1)}, f32[32,512]{1,0:T(8,128)S(1)}, u32[]{:S(2)}, u32[]{:S(2)}) collective-permute-start(f32[32,512]{1,0:T(8,128)S(1)} %dynamic-slice_add_fusion), channel_id=1, source_target_pairs={{0,4},{1,5},{2,6},{3,7},{4,0},{5,1},{6,2},{7,3},{8,12},{9,13},{10,... | collective-permute-start | bytes 196616 | tf_op jit(solution)/shard_map/ppermute | solution.py:254
  18.7 2.1 %collective-permute-done.4 = f32[32,512]{1,0:T(8,128)S(1)} collective-permute-done((f32[32,512]{1,0:T(8,128)S(1)}, f32[32,512]{1,0:T(8,128)S(1)}, u32[]{:S(2)}, u32[]{:S(2)}) %collective-permute-start.4) | collective-permute-done | bytes 65568 | tf_op jit(solution)/shard_map/ppermute | solution.py:254
  20.8 2.6 %collective-permute-done.3 = f32[32,512]{1,0:T(8,128)S(1)} collective-permute-done((f32[32,512]{1,0:T(8,128)S(1)}, f32[32,512]{1,0:T(8,128)S(1)}, u32[]{:S(2)}, u32[]{:S(2)}) %collective-permute-start.3) | collective-permute-done | bytes 65568 | tf_op jit(solution)/shard_map/ppermute | solution.py:254
  23.5 2.5 %collective-permute-start.7 = (f32[32,512]{1,0:T(8,128)S(1)}, f32[32,512]{1,0:T(8,128)S(1)}, u32[]{:S(2)}, u32[]{:S(2)}) collective-permute-start(f32[32,512]{1,0:T(8,128)S(1)} %add_add_fusion.refs_0_), channel_id=1, source_target_pairs={{0,18},{1,19},{2,16},{3,17},{4,22},{5,23},{6,20},{7,21},{8,26},{9,... | collective-permute-start | bytes 196616 | tf_op jit(solution)/shard_map/ppermute | solution.py:254
  26.0 0.5 collective-permute-start.6
  26.5 0.5 collective-permute-start.5
  27.1 1.5 %collective-permute-start.12 = (f32[128,2048]{1,0:T(8,128)S(1)}, f32[128,2048]{1,0:T(8,128)S(1)}, u32[]{:S(2)}, u32[]{:S(2)}) collective-permute-start(f32[128,2048]{1,0:T(8,128)S(1)} %copy-done), channel_id=1, source_target_pairs={{0,16},{1,17},{2,18},{3,19},{4,20},{5,21},{6,22},{7,23},{8,24},{9,... | collective-permute-start | bytes 3145736 | tf_op jit(solution)/shard_map/ppermute | solution.py:254
  28.5 0.6 collective-permute-done.7.refs_3_
  29.1 1.9 %collective-permute-done.6.refs_2_ = f32[32,512]{1,0:T(8,128)S(1)} collective-permute-done((f32[32,512]{1,0:T(8,128)S(1)}, f32[32,512]{1,0:T(8,128)S(1)}, u32[]{:S(2)}, u32[]{:S(2)}) %collective-permute-start.6) | collective-permute-done | bytes 65568 | tf_op jit(solution)/shard_map/ppermute | solution.py:254
  31.1 0.5 collective-permute-start.9
  31.6 2.4 %lookup.1 = (f32[128,512]{1,0:T(8,128)}, f32[8,512]{1,0:T(8,128)}) custom-call(s32[1,512]{1,0:T(1,128)} %bitcast.7, f32[128,128]{1,0:T(8,128)} %bitcast.5, f32[128,128]{1,0:T(8,128)} %bitcast.6, f32[128,512]{1,0:T(8,128)} %noise.1), custom_call_target="tpu_custom_call" | custom-call | flops 25769803776 | bytes 1048576 | tf_op jit(solution)/shard_map/lookup/pallas_call | solution.py:152
  34.1 0.5 copy-done.6
  34.7 0.1 copy-done.8
  34.7 17.0 %solve.1.weights = f32[128,256]{1,0:T(8,128)} custom-call(s32[2]{0:T(128)} %pad_add_fusion.bits, f32[32,512]{1,0:T(8,128)} %copy-done.2, f32[32,512]{1,0:T(8,128)} %copy-done.5, f32[32,512]{1,0:T(8,128)} %copy-done.4, f32[32,512]{1,0:T(8,128)} %copy-done.3, f32[32,512]{1,0:T(8,128)} %copy-done.6, f32[32,512]{1,0:T(8,128)} %copy-done.9, f32[32,512]{1,0:T(8,128)} %copy-done.8, ...), custom_call_target="tpu_custom_call" | custom-call | flops 805306368 | bytes 1048576 | tf_op jit(solution)/shard_map/solve/pallas_call | solution.py:207
  51.7 1.0 %copy-done.1 = f32[128,2048]{1,0:T(8,128)} copy-done((f32[128,2048]{1,0:T(8,128)}, f32[128,2048]{1,0:T(8,128)S(1)}, u32[]{:S(2)}) %copy-start.1) | copy-done | bytes 1048600
  52.7 4.7 %update.1 = f32[128,2048]{1,0:T(8,128)} custom-call(f32[128,256]{1,0:T(8,128)} %solve.1.weights, f32[128,2048]{1,0:T(8,128)} %refs_0_.1, f32[128,2048]{1,0:T(8,128)} %copy-done.1), custom_call_target="tpu_custom_call" | custom-call | flops 134217728 | bytes 3145728 | tf_op jit(solution)/shard_map/update/pallas_call | solution.py:232
  (31 shorter events, 0.1 us)
Async XLA Ops:
  0.0 27.1 %copy-start = (f32[128,2048]{1,0:T(8,128)S(1)}, f32[128,2048]{1,0:T(8,128)}, u32[]{:S(2)}) copy-start(f32[128,2048]{1,0:T(8,128)} %refs_0_.1) | copy-start | bytes 3145732
  6.1 1.6 %collective-permute-start = (f32[64,512]{1,0:T(8,128)}, f32[64,512]{1,0:T(8,128)S(1)}, u32[]{:S(2)}, u32[]{:S(2)}) collective-permute-start(f32[64,512]{1,0:T(8,128)} %get-tuple-element.10), channel_id=1, source_target_pairs={{0,1},{1,0},{2,3},{3,2},{4,5},{5,4},{6,7},{7,6},{8,9},{9,8},{10,11... | collective-permute-start | bytes 393224 | tf_op jit(solution)/shard_map/ppermute | solution.py:254
  8.7 5.3 %collective-permute-start.1 = (f32[32,512]{1,0:T(8,128)S(1)}, f32[32,512]{1,0:T(8,128)S(1)}, u32[]{:S(2)}, u32[]{:S(2)}) collective-permute-start(f32[32,512]{1,0:T(8,128)S(1)} %constant_dynamic-slice_fusion), channel_id=1, source_target_pairs={{0,2},{1,3},{2,0},{3,1},{4,6},{5,7},{6,4},{7,5},{8,10},{9,11},{10,... | collective-permute-start | bytes 196616 | tf_op jit(solution)/shard_map/ppermute | solution.py:254
  14.1 6.7 %collective-permute-start.4 = (f32[32,512]{1,0:T(8,128)S(1)}, f32[32,512]{1,0:T(8,128)S(1)}, u32[]{:S(2)}, u32[]{:S(2)}) collective-permute-start(f32[32,512]{1,0:T(8,128)S(1)} %dynamic-slice_add_fusion), channel_id=1, source_target_pairs={{0,12},{1,13},{2,14},{3,15},{4,8},{5,9},{6,10},{7,11},{8,4},{9,5},... | collective-permute-start | bytes 196616 | tf_op jit(solution)/shard_map/ppermute | solution.py:254
  18.1 5.4 %collective-permute-start.3 = (f32[32,512]{1,0:T(8,128)S(1)}, f32[32,512]{1,0:T(8,128)S(1)}, u32[]{:S(2)}, u32[]{:S(2)}) collective-permute-start(f32[32,512]{1,0:T(8,128)S(1)} %dynamic-slice_add_fusion), channel_id=1, source_target_pairs={{0,8},{1,9},{2,10},{3,11},{4,12},{5,13},{6,14},{7,15},{8,0},{9,1},... | collective-permute-start | bytes 196616 | tf_op jit(solution)/shard_map/ppermute | solution.py:254
  18.1 5.4 %collective-permute-start.2 = (f32[32,512]{1,0:T(8,128)S(1)}, f32[32,512]{1,0:T(8,128)S(1)}, u32[]{:S(2)}, u32[]{:S(2)}) collective-permute-start(f32[32,512]{1,0:T(8,128)S(1)} %dynamic-slice_add_fusion), channel_id=1, source_target_pairs={{0,4},{1,5},{2,6},{3,7},{4,0},{5,1},{6,2},{7,3},{8,12},{9,13},{10,... | collective-permute-start | bytes 196616 | tf_op jit(solution)/shard_map/ppermute | solution.py:254
  23.5 10.5 %copy-start.2 = (f32[32,512]{1,0:T(8,128)}, f32[32,512]{1,0:T(8,128)S(1)}, u32[]{:S(2)}) copy-start(f32[32,512]{1,0:T(8,128)S(1)} %add_add_fusion.refs_0_) | copy-start | bytes 196612
  23.5 5.6 %collective-permute-start.7 = (f32[32,512]{1,0:T(8,128)S(1)}, f32[32,512]{1,0:T(8,128)S(1)}, u32[]{:S(2)}, u32[]{:S(2)}) collective-permute-start(f32[32,512]{1,0:T(8,128)S(1)} %add_add_fusion.refs_0_), channel_id=1, source_target_pairs={{0,18},{1,19},{2,16},{3,17},{4,22},{5,23},{6,20},{7,21},{8,26},{9,... | collective-permute-start | bytes 196616 | tf_op jit(solution)/shard_map/ppermute | solution.py:254
  26.0 5.0 %collective-permute-start.6 = (f32[32,512]{1,0:T(8,128)S(1)}, f32[32,512]{1,0:T(8,128)S(1)}, u32[]{:S(2)}, u32[]{:S(2)}) collective-permute-start(f32[32,512]{1,0:T(8,128)S(1)} %add_add_fusion.refs_0_), channel_id=1, source_target_pairs={{0,16},{1,17},{2,18},{3,19},{4,20},{5,21},{6,22},{7,23},{8,24},{9,... | collective-permute-start | bytes 196616 | tf_op jit(solution)/shard_map/ppermute | solution.py:254
  26.5 4.5 %collective-permute-start.5 = (f32[32,512]{1,0:T(8,128)S(1)}, f32[32,512]{1,0:T(8,128)S(1)}, u32[]{:S(2)}, u32[]{:S(2)}) collective-permute-start(f32[32,512]{1,0:T(8,128)S(1)} %add_add_fusion.refs_0_), channel_id=1, source_target_pairs={{0,2},{1,3},{2,0},{3,1},{4,6},{5,7},{6,4},{7,5},{8,10},{9,11},{10,... | collective-permute-start | bytes 196616 | tf_op jit(solution)/shard_map/ppermute | solution.py:254
  27.1 24.7 %collective-permute-start.12 = (f32[128,2048]{1,0:T(8,128)S(1)}, f32[128,2048]{1,0:T(8,128)S(1)}, u32[]{:S(2)}, u32[]{:S(2)}) collective-permute-start(f32[128,2048]{1,0:T(8,128)S(1)} %copy-done), channel_id=1, source_target_pairs={{0,16},{1,17},{2,18},{3,19},{4,20},{5,21},{6,22},{7,23},{8,24},{9,... | collective-permute-start | bytes 3145736 | tf_op jit(solution)/shard_map/ppermute | solution.py:254
  28.5 5.5 %collective-permute-start.8 = (f32[32,512]{1,0:T(8,128)S(1)}, f32[32,512]{1,0:T(8,128)S(1)}, u32[]{:S(2)}, u32[]{:S(2)}) collective-permute-start(f32[32,512]{1,0:T(8,128)S(1)} %add_add_fusion.refs_0_), channel_id=1, source_target_pairs={{0,1},{1,0},{2,3},{3,2},{4,5},{5,4},{6,7},{7,6},{8,9},{9,8},{10,11... | collective-permute-start | bytes 196616 | tf_op jit(solution)/shard_map/ppermute | solution.py:254
  29.1 4.9 %copy-start.3 = (f32[32,512]{1,0:T(8,128)}, f32[32,512]{1,0:T(8,128)S(1)}, u32[]{:S(2)}) copy-start(f32[32,512]{1,0:T(8,128)S(1)} %collective-permute-done.7.refs_3_) | copy-start | bytes 196612
  29.1 4.9 %collective-permute-start.11 = (f32[32,512]{1,0:T(8,128)S(1)}, f32[32,512]{1,0:T(8,128)S(1)}, u32[]{:S(2)}, u32[]{:S(2)}) collective-permute-start(f32[32,512]{1,0:T(8,128)S(1)} %collective-permute-done.7.refs_3_), channel_id=1, source_target_pairs={{0,1},{1,0},{2,3},{3,2},{4,5},{5,4},{6,7},{7,6},{8,9},{9,8},{10,11... | collective-permute-start | bytes 196616 | tf_op jit(solution)/shard_map/ppermute | solution.py:254
  31.0 3.0 %copy-start.4 = (f32[32,512]{1,0:T(8,128)}, f32[32,512]{1,0:T(8,128)S(1)}, u32[]{:S(2)}) copy-start(f32[32,512]{1,0:T(8,128)S(1)} %collective-permute-done.6.refs_2_) | copy-start | bytes 196612
  31.0 3.0 %collective-permute-start.10 = (f32[32,512]{1,0:T(8,128)S(1)}, f32[32,512]{1,0:T(8,128)S(1)}, u32[]{:S(2)}, u32[]{:S(2)}) collective-permute-start(f32[32,512]{1,0:T(8,128)S(1)} %collective-permute-done.6.refs_2_), channel_id=1, source_target_pairs={{0,1},{1,0},{2,3},{3,2},{4,5},{5,4},{6,7},{7,6},{8,9},{9,8},{10,11... | collective-permute-start | bytes 196616 | tf_op jit(solution)/shard_map/ppermute | solution.py:254
  31.0 3.0 %copy-start.5 = (f32[32,512]{1,0:T(8,128)}, f32[32,512]{1,0:T(8,128)S(1)}, u32[]{:S(2)}) copy-start(f32[32,512]{1,0:T(8,128)S(1)} %collective-permute-done.5.refs_1_) | copy-start | bytes 196612
  31.1 3.0 %collective-permute-start.9 = (f32[32,512]{1,0:T(8,128)S(1)}, f32[32,512]{1,0:T(8,128)S(1)}, u32[]{:S(2)}, u32[]{:S(2)}) collective-permute-start(f32[32,512]{1,0:T(8,128)S(1)} %collective-permute-done.5.refs_1_), channel_id=1, source_target_pairs={{0,1},{1,0},{2,3},{3,2},{4,5},{5,4},{6,7},{7,6},{8,9},{9,8},{10,11... | collective-permute-start | bytes 196616 | tf_op jit(solution)/shard_map/ppermute | solution.py:254
  34.0 0.6 %copy-start.6 = (f32[32,512]{1,0:T(8,128)}, f32[32,512]{1,0:T(8,128)S(1)}, u32[]{:S(2)}) copy-start(f32[32,512]{1,0:T(8,128)S(1)} %collective-permute-done.8.refs_4_) | copy-start | bytes 196612
  34.0 0.6 %copy-start.7 = (f32[32,512]{1,0:T(8,128)}, f32[32,512]{1,0:T(8,128)S(1)}, u32[]{:S(2)}) copy-start(f32[32,512]{1,0:T(8,128)S(1)} %collective-permute-done.11.refs_7_) | copy-start | bytes 196612
  34.1 0.7 %copy-start.8 = (f32[32,512]{1,0:T(8,128)}, f32[32,512]{1,0:T(8,128)S(1)}, u32[]{:S(2)}) copy-start(f32[32,512]{1,0:T(8,128)S(1)} %collective-permute-done.10.refs_6_) | copy-start | bytes 196612
  34.1 0.6 %copy-start.9 = (f32[32,512]{1,0:T(8,128)}, f32[32,512]{1,0:T(8,128)S(1)}, u32[]{:S(2)}) copy-start(f32[32,512]{1,0:T(8,128)S(1)} %collective-permute-done.9.refs_5_) | copy-start | bytes 196612
  51.7 1.0 %copy-start.1 = (f32[128,2048]{1,0:T(8,128)}, f32[128,2048]{1,0:T(8,128)S(1)}, u32[]{:S(2)}) copy-start(f32[128,2048]{1,0:T(8,128)S(1)} %collective-permute-done.12.refs_1_) | copy-start | bytes 3145732

commit v2 on v1

--- a/solution.py
+++ b/solution.py
@@ -11,8 +11,7 @@
 HIGHEST = lax.Precision.HIGHEST
 SUB, LANE = 8, 128
 VMEM = pl.BlockSpec(memory_space=pltpu.VMEM)
-SMEM = pl.BlockSpec(memory_space=pltpu.SMEM)
-ANY = pl.BlockSpec(memory_space=pl.ANY)
+VMEM_LIMIT = 20 << 20
 
 
 def dot(a, b, dims, precision=HIGHEST):
@@ -90,7 +89,12 @@
     return jnp.concatenate(m, axis=0)
 
 
-def forward_kernel(bits, ens, op, keep, send, acc):
+def own_bits():
+    index = lax.axis_index("par")
+    return lax.bitwise_and(index, 1), lax.bitwise_and(lax.shift_right_logical(index, 1), 1)
+
+
+def forward_kernel(ens, op, keep, send, acc):
     step = pl.program_id(0)
 
     @pl.when(step == 0)
@@ -102,13 +106,14 @@
     @pl.when(step == pl.num_programs(0) - 1)
     def _():
         half = keep.shape[0]
-        mine = pl.multiple_of(bits[0] * half, SUB)
-        other = pl.multiple_of((1 - bits[0]) * half, SUB)
+        core, _ = own_bits()
+        mine = pl.multiple_of(core * half, SUB)
+        other = pl.multiple_of((1 - core) * half, SUB)
         keep[...] = acc[pl.ds(mine, half), :]
         send[...] = acc[pl.ds(other, half), :]
 
 
-def forward(ens, op, bits):
+def forward(ens, op):
     members, params = ens.shape
     rows = op.shape[1]
     steps = 4 if params % (4 * LANE) == 0 else 1
@@ -120,7 +125,6 @@
         grid=(steps,),
         out_shape=(half, half),
         in_specs=[
-            SMEM,
             pl.BlockSpec((members, depth), lambda i: (0, i)),
             pl.BlockSpec((depth, rows), lambda i: (i, 0)),
         ],
@@ -129,8 +133,9 @@
         cost_estimate=pl.CostEstimate(
             flops=2 * members * params * rows, bytes_accessed=4 * (members * params + params * rows), transcendentals=0
         ),
+        compiler_params=pltpu.CompilerParams(vmem_limit_bytes=VMEM_LIMIT),
         name="forward",
-    )(bits, ens, op)
+    )(ens, op)
 
 
 def lookup_kernel(rows, obs, var, noise, target, inverse_var):
@@ -158,11 +163,13 @@
         in_specs=[VMEM] * 4,
         out_specs=(VMEM, VMEM),
         cost_estimate=pl.CostEstimate(flops=2 * obs.shape[0] * LANE * count * 12, bytes_accessed=1 << 20, transcendentals=0),
+        compiler_params=pltpu.CompilerParams(vmem_limit_bytes=VMEM_LIMIT),
         name="lookup",
     )(rows.reshape(1, count), obs.reshape(-1, LANE), var.reshape(-1, LANE), noise)
 
 
-def solve_kernel(places, own, bits, *refs):
+def solve_kernel(places, own, *refs):
+    own_core, own_side = own_bits()
     count = len(places)
     pieces = refs[:count]
     target, inverse_var = refs[count : count + 2]
@@ -170,8 +177,8 @@
     fwd = refs[count + 3]
     rows = pieces[0].shape[0]
     for piece, (far, dy, dc) in zip(pieces, places):
-        core = bits[0] if dc == 0 else 1 - bits[0]
-        side = bits[1] if dy == 0 else 1 - bits[1]
+        core = own_core if dc == 0 else 1 - own_core
+        side = own_side if dy == 0 else 1 - own_side
         fwd[pl.ds(pl.multiple_of(far * own + (core * 2 + side) * rows, SUB), rows), :] = piece[...]
     members = fwd.shape[0]
     spread = fwd[...] - jnp.mean(fwd[...], axis=0, keepdims=True)
@@ -202,17 +209,18 @@
     weights[...] = (w - jnp.mean(w, axis=0, keepdims=True)).T
 
 
-def solve(pieces, places, target, inverse_var, bits, members):
+def solve(pieces, places, target, inverse_var, members):
     own, rows = target.shape
     return pl.pallas_call(
         functools.partial(solve_kernel, places, own),
         out_shape=jax.ShapeDtypeStruct((own, members), f32),
-        in_specs=[SMEM] + [VMEM] * (len(pieces) + 2),
+        in_specs=[VMEM] * (len(pieces) + 2),
         out_specs=VMEM,
         scratch_shapes=[pltpu.VMEM((members, rows), f32)],
-        cost_estimate=pl.CostEstimate(flops=2 * members * members * rows * 12, bytes_accessed=1 << 20, transcendentals=0),
+        cost_estimate=pl.CostEstimate(flops=1, bytes_accessed=1, transcendentals=0),
+        compiler_params=pltpu.CompilerParams(vmem_limit_bytes=VMEM_LIMIT),
         name="solve",
-    )(bits, *pieces, target, inverse_var)
+    )(*pieces, target, inverse_var)
 
 
 def update_kernel(weights, *refs):
@@ -238,14 +246,14 @@
         cost_estimate=pl.CostEstimate(
             flops=2 * own * weights.shape[1] * params, bytes_accessed=4 * params * (own + weights.shape[1]), transcendentals=0
         ),
+        compiler_params=pltpu.CompilerParams(vmem_limit_bytes=VMEM_LIMIT),
         name="update",
     )(weights, *ens)
 
 
 def per_device(n_mem, n_par, operator, ensemble, noise, observations, variances, rows):
     index = lax.axis_index("par")
-    core, side = index % 2, (index // 2) % 2
-    bits = jnp.stack([core, side]).astype(jnp.int32)
+    side = lax.bitwise_and(lax.shift_right_logical(index, 1), 1)
 
     def swap(x, far, near):
         pairs = [
@@ -254,24 +262,27 @@
         return lax.ppermute(x, ("mem", "par"), pairs)
 
     ens = [ensemble] + [swap(ensemble, far, 0) for far in range(1, n_mem)]
-    keep, send = forward(ensemble, operator, bits)
+    keep, send = forward(ensemble, operator)
     part = keep + swap(send, 0, 1)
     size = part.shape[0] // 2
     total = lax.dynamic_slice_in_dim(part, side * size, size, 0) + swap(
         lax.dynamic_slice_in_dim(part, (1 - side) * size, size, 0), 0, 2
     )
+    target, inverse_var = lookup(rows, observations, variances, noise)
     stride = 4
     while stride < n_par:
         ways = min(4, n_par // stride)
-        total = add_all([total] + [swap(total, 0, d * stride) for d in range(1, ways)])
+        terms = [total] + [swap(total, 0, d * stride) for d in range(1, ways)]
+        if stride == 4:
+            terms, target, inverse_var = lax.optimization_barrier((terms, target, inverse_var))
+        total = add_all(terms)
         stride *= ways
-    target, inverse_var = lookup(rows, observations, variances, noise)
     places = [(far, dy, 0) for far in range(n_mem) for dy in range(2)]
     pieces = [total if (far, dy) == (0, 0) else swap(total, far, 2 * dy) for far, dy, _ in places]
     pieces += [swap(piece, 0, 1) for piece in pieces]
     places += [(far, dy, 1) for far, dy, _ in places]
     members = ensemble.shape[0] * n_mem
-    weights = solve(pieces, places, target, inverse_var, bits, members)
+    weights = solve(pieces, places, target, inverse_var, members)
     return update(weights, ens)
 
 

time: 57.7 us -> 58.5 us (1.014)
  waiting for transfers between devices: 10.8 us -> 19.2 us
  Pallas kernels: 29.5 us -> 21.9 us
  local copies, waits for them, and re-layouts: 1.67 us -> 3.44 us
  other arithmetic: 1.6 us -> 0.05 us
    ppermute x13, waiting for transfers between devices: 10.8 us -> 19.2 us  [swap(): return lax.ppermute(x, ('mem', 'par'), pairs)]
    pallas_call x1, Pallas kernels: 5.48 us -> 2.82 us  [forward(): pl.pallas_call(forward_kernel, grid=(steps,), out_shape=(half, half), in_...]
    pallas_call x1, Pallas kernels: 17 us -> 15.1 us  [solve(): pl.pallas_call(functools.partial(solve_kernel, places, own), out_shape=ja...]
    unnamed x20 -> x14, local copies, waits for them, and re-layouts: 1.65 us -> 3.43 us
    pallas_call x1, Pallas kernels: 2.44 us -> 0.68 us  [lookup(): pl.pallas_call(lookup_kernel, out_shape=(jax.ShapeDtypeStruct(noise.shape...]
    pallas_call x1, Pallas kernels: 4.67 us -> 3.3 us  [update(): pl.pallas_call(update_kernel, grid=(steps,), out_shape=jax.ShapeDtypeStru...]
    add x1, other arithmetic: 0.92 us -> 0.02 us  [per_device(): part = keep + swap(send, 0, 1)]
    another operation x1 -> x0, other arithmetic: 0.65 us -> none  [per_device(): bits = jnp.stack([core, side]).astype(jnp.int32)]
  transfers between devices with their start and end apart: 13 -> 13, of which waited for: 6 -> 8; matrix products, arithmetic and copies ran while one was open for 0% -> 0% of each run, Pallas kernels for 34% -> 27%
where the time goes in v2:
time: 58.5 us; the launch traced here: 58.3 us
  Pallas kernels  21.9 us (37%)
  waiting for transfers between devices  19.2 us (33%)
  starting transfers between devices  13.7 us (23%)
  local copies, waits for them, and re-layouts  3.44 us (6%)
    ppermute x13, waiting for transfers between devices, swap(): return lax.ppermute(x, ('mem', 'par'), pairs)  19.2 us
    pallas_call x1, Pallas kernels, solve(): pl.pallas_call(functools.partial(solve_kernel, places, own), out_shape=ja...  15.1 us
    ppermute x13, starting transfers between devices, swap(): return lax.ppermute(x, ('mem', 'par'), pairs)  13.7 us
    unnamed x14, local copies, waits for them, and re-layouts  3.43 us
    pallas_call x1, Pallas kernels, update(): pl.pallas_call(update_kernel, grid=(steps,), out_shape=jax.ShapeDtypeStru...  3.3 us
    pallas_call x1, Pallas kernels, forward(): pl.pallas_call(forward_kernel, grid=(steps,), out_shape=(half, half), in_...  2.82 us
  transfers between devices with their start and end apart: 13, of which 8 were waited for; matrix products, arithmetic and copies ran while one was open for 0% of the time, Pallas kernels for 27%

profile of v2, /device:TPU:0, one launch (start us, length us, event | category | flops | bytes accessed | tf_op | source)
XLA Modules:
  0.0 58.3 jit_solution(2570797092105319374)
XLA Ops:
  0.0 1.2 %copy-done = f32[128,2048]{1,0:T(8,128)S(1)} copy-done((f32[128,2048]{1,0:T(8,128)S(1)}, f32[128,2048]{1,0:T(8,128)}, u32[]{:S(2)}) %copy-start) | copy-done | bytes 1048600
  1.2 2.2 %copy-done.2 = f32[2048,512]{1,0:T(8,128)S(1)} copy-done((f32[2048,512]{1,0:T(8,128)S(1)}, f32[2048,512]{1,0:T(8,128)}, u32[]{:S(2)}) %copy-start.2) | copy-done | bytes 4194328
  3.4 2.8 %forward.1 = (f32[64,512]{1,0:T(8,128)S(1)}, f32[64,512]{1,0:T(8,128)S(1)}) custom-call(f32[128,2048]{1,0:T(8,128)S(1)} %copy-done, f32[2048,512]{1,0:T(8,128)S(1)} %copy-done.2), custom_call_target="tpu_custom_call" | custom-call | flops 268435456 | bytes 5242880 | tf_op jit(solution)/shard_map/forward/pallas_call | solution.py:123
  6.3 0.5 collective-permute-start
  6.8 1.0 %collective-permute-done = f32[64,512]{1,0:T(8,128)S(1)} collective-permute-done((f32[64,512]{1,0:T(8,128)S(1)}, f32[64,512]{1,0:T(8,128)S(1)}, u32[]{:S(2)}, u32[]{:S(2)}) %collective-permute-start) | collective-permute-done | bytes 131104 | tf_op jit(solution)/shard_map/ppermute | solution.py:262
  7.8 2.9 %collective-permute-start.1 = (f32[32,512]{1,0:T(8,128)S(1)}, f32[32,512]{1,0:T(8,128)S(1)}, u32[]{:S(2)}, u32[]{:S(2)}) collective-permute-start(f32[32,512]{1,0:T(8,128)S(1)} %constant_dynamic-slice_fusion), channel_id=1, source_target_pairs={{0,2},{1,3},{2,0},{3,1},{4,6},{5,7},{6,4},{7,5},{8,10},{9,11},{10,... | collective-permute-start | bytes 196616 | tf_op jit(solution)/shard_map/ppermute | solution.py:262
  10.8 1.5 %collective-permute-start.12 = (f32[128,2048]{1,0:T(8,128)S(1)}, f32[128,2048]{1,0:T(8,128)S(1)}, u32[]{:S(2)}, u32[]{:S(2)}) collective-permute-start(f32[128,2048]{1,0:T(8,128)S(1)} %copy-done.1), channel_id=1, source_target_pairs={{0,16},{1,17},{2,18},{3,19},{4,20},{5,21},{6,22},{7,23},{8,24},{9,... | collective-permute-start | bytes 3145736 | tf_op jit(solution)/shard_map/ppermute | solution.py:262
  12.3 0.9 %collective-permute-done.1 = f32[32,512]{1,0:T(8,128)S(1)} collective-permute-done((f32[32,512]{1,0:T(8,128)S(1)}, f32[32,512]{1,0:T(8,128)S(1)}, u32[]{:S(2)}, u32[]{:S(2)}) %collective-permute-start.1) | collective-permute-done | bytes 65568 | tf_op jit(solution)/shard_map/ppermute | solution.py:262
  13.2 4.0 %collective-permute-start.4 = (f32[32,512]{1,0:T(8,128)S(1)}, f32[32,512]{1,0:T(8,128)S(1)}, u32[]{:S(2)}, u32[]{:S(2)}) collective-permute-start(f32[32,512]{1,0:T(8,128)S(1)} %dynamic-slice_add_fusion), channel_id=1, source_target_pairs={{0,12},{1,13},{2,14},{3,15},{4,8},{5,9},{6,10},{7,11},{8,4},{9,5},... | collective-permute-start | bytes 196616 | tf_op jit(solution)/shard_map/ppermute | solution.py:262
  17.2 0.6 %collective-permute-start.2 = (f32[32,512]{1,0:T(8,128)S(1)}, f32[32,512]{1,0:T(8,128)S(1)}, u32[]{:S(2)}, u32[]{:S(2)}) collective-permute-start(f32[32,512]{1,0:T(8,128)S(1)} %dynamic-slice_add_fusion), channel_id=1, source_target_pairs={{0,4},{1,5},{2,6},{3,7},{4,0},{5,1},{6,2},{7,3},{8,12},{9,13},{10,... | collective-permute-start | bytes 196616 | tf_op jit(solution)/shard_map/ppermute | solution.py:262
  17.8 0.7 %lookup.1 = (f32[128,512]{1,0:T(8,128)S(1)}, f32[8,512]{1,0:T(8,128)S(1)}) custom-call(s32[1,512]{1,0:T(1,128)S(1)} %bitcast.5, f32[128,128]{1,0:T(8,128)S(1)} %bitcast.3, f32[128,128]{1,0:T(8,128)S(1)} %bitcast.4, f32[128,512]{1,0:T(8,128)S(1)} %copy-done.3), custom_call_target="tpu_custom_call" | custom-call | flops 25769803776 | bytes 1048576 | tf_op jit(solution)/shard_map/lookup/pallas_call | solution.py:157
  18.5 1.4 %collective-permute-done.4 = f32[32,512]{1,0:T(8,128)S(1)} collective-permute-done((f32[32,512]{1,0:T(8,128)S(1)}, f32[32,512]{1,0:T(8,128)S(1)}, u32[]{:S(2)}, u32[]{:S(2)}) %collective-permute-start.4) | collective-permute-done | bytes 65568 | tf_op jit(solution)/shard_map/ppermute | solution.py:262
  19.9 2.6 %collective-permute-done.3 = f32[32,512]{1,0:T(8,128)S(1)} collective-permute-done((f32[32,512]{1,0:T(8,128)S(1)}, f32[32,512]{1,0:T(8,128)S(1)}, u32[]{:S(2)}, u32[]{:S(2)}) %collective-permute-start.3) | collective-permute-done | bytes 65568 | tf_op jit(solution)/shard_map/ppermute | solution.py:262
  22.6 0.0 collective-permute-done.2
  22.6 2.5 %collective-permute-start.7 = (f32[32,512]{1,0:T(8,128)S(1)}, f32[32,512]{1,0:T(8,128)S(1)}, u32[]{:S(2)}, u32[]{:S(2)}) collective-permute-start(f32[32,512]{1,0:T(8,128)S(1)} %add_add_fusion.refs_0_), channel_id=1, source_target_pairs={{0,18},{1,19},{2,16},{3,17},{4,22},{5,23},{6,20},{7,21},{8,26},{9,... | collective-permute-start | bytes 196616 | tf_op jit(solution)/shard_map/ppermute | solution.py:262
  25.1 0.5 collective-permute-start.6
  25.6 0.5 collective-permute-start.5
  26.1 11.5 %collective-permute-done.7.refs_3_ = f32[32,512]{1,0:T(8,128)S(1)} collective-permute-done((f32[32,512]{1,0:T(8,128)S(1)}, f32[32,512]{1,0:T(8,128)S(1)}, u32[]{:S(2)}, u32[]{:S(2)}) %collective-permute-start.7) | collective-permute-done | bytes 65568 | tf_op jit(solution)/shard_map/ppermute | solution.py:262
  37.6 0.9 %collective-permute-done.6.refs_2_ = f32[32,512]{1,0:T(8,128)S(1)} collective-permute-done((f32[32,512]{1,0:T(8,128)S(1)}, f32[32,512]{1,0:T(8,128)S(1)}, u32[]{:S(2)}, u32[]{:S(2)}) %collective-permute-start.6) | collective-permute-done | bytes 65568 | tf_op jit(solution)/shard_map/ppermute | solution.py:262
  38.5 0.5 collective-permute-start.9
  39.0 0.7 %collective-permute-done.10.refs_6_ = f32[32,512]{1,0:T(8,128)S(1)} collective-permute-done((f32[32,512]{1,0:T(8,128)S(1)}, f32[32,512]{1,0:T(8,128)S(1)}, u32[]{:S(2)}, u32[]{:S(2)}) %collective-permute-start.10) | collective-permute-done | bytes 65568 | tf_op jit(solution)/shard_map/ppermute | solution.py:262
  39.8 0.2 collective-permute-done.9.refs_5_
  39.9 15.1 %solve.1.weights = f32[128,256]{1,0:T(8,128)S(1)} custom-call(f32[32,512]{1,0:T(8,128)S(1)} %add_add_fusion.refs_0_, f32[32,512]{1,0:T(8,128)S(1)} %collective-permute-done.5.refs_1_, f32[32,512]{1,0:T(8,128)S(1)} %collective-permute-done.6.refs_2_, f32[32,512]{1,0:T(8,128)S(1)} %collective-permute-done.7.refs_3_, ...), custom_call_target="tpu_custom_call" | custom-call | flops 1 | bytes 1 | tf_op jit(solution)/shard_map/solve/pallas_call | solution.py:214
  55.0 3.3 %update.1 = f32[128,2048]{1,0:T(8,128)} custom-call(f32[128,256]{1,0:T(8,128)S(1)} %solve.1.weights, f32[128,2048]{1,0:T(8,128)S(1)} %copy-done.1, f32[128,2048]{1,0:T(8,128)S(1)} %collective-permute-done.12.refs_1_), custom_call_target="tpu_custom_call" | custom-call | flops 134217728 | bytes 3145728 | tf_op jit(solution)/shard_map/update/pallas_call | solution.py:240
  (24 shorter events, 0.1 us)
Async XLA Ops:
  0.0 1.2 %copy-start = (f32[128,2048]{1,0:T(8,128)S(1)}, f32[128,2048]{1,0:T(8,128)}, u32[]{:S(2)}) copy-start(f32[128,2048]{1,0:T(8,128)} %refs_0_.1) | copy-start | bytes 3145732
  1.2 2.2 %copy-start.2 = (f32[2048,512]{1,0:T(8,128)S(1)}, f32[2048,512]{1,0:T(8,128)}, u32[]{:S(2)}) copy-start(f32[2048,512]{1,0:T(8,128)} %op.1) | copy-start | bytes 12582916
  3.4 7.3 %copy-start.1 = (f32[128,2048]{1,0:T(8,128)S(1)}, f32[128,2048]{1,0:T(8,128)}, u32[]{:S(2)}) copy-start(f32[128,2048]{1,0:T(8,128)} %refs_0_.1) | copy-start | bytes 3145732
  3.4 14.4 %copy-start.3 = (f32[128,512]{1,0:T(8,128)S(1)}, f32[128,512]{1,0:T(8,128)}, u32[]{:S(2)}) copy-start(f32[128,512]{1,0:T(8,128)} %noise.1) | copy-start | bytes 786436
  3.4 14.4 %copy-start.4 = (f32[16384]{0:T(1024)S(1)}, f32[16384]{0:T(1024)}, u32[]{:S(2)}) copy-start(f32[16384]{0:T(1024)} %param.9) | copy-start | bytes 196612
  3.4 14.4 %copy-start.5 = (f32[16384]{0:T(1024)S(1)}, f32[16384]{0:T(1024)}, u32[]{:S(2)}) copy-start(f32[16384]{0:T(1024)} %param.10) | copy-start | bytes 196612
  3.4 14.4 %copy-start.6 = (s32[512]{0:T(512)S(1)}, s32[512]{0:T(512)}, u32[]{:S(2)}) copy-start(s32[512]{0:T(512)} %param.11) | copy-start | bytes 6148
  6.3 1.5 %collective-permute-start = (f32[64,512]{1,0:T(8,128)S(1)}, f32[64,512]{1,0:T(8,128)S(1)}, u32[]{:S(2)}, u32[]{:S(2)}) collective-permute-start(f32[64,512]{1,0:T(8,128)S(1)} %get-tuple-element.16), channel_id=1, source_target_pairs={{0,1},{1,0},{2,3},{3,2},{4,5},{5,4},{6,7},{7,6},{8,9},{9,8},{10,11... | collective-permute-start | bytes 393224 | tf_op jit(solution)/shard_map/ppermute | solution.py:262
  7.8 5.3 %collective-permute-start.1 = (f32[32,512]{1,0:T(8,128)S(1)}, f32[32,512]{1,0:T(8,128)S(1)}, u32[]{:S(2)}, u32[]{:S(2)}) collective-permute-start(f32[32,512]{1,0:T(8,128)S(1)} %constant_dynamic-slice_fusion), channel_id=1, source_target_pairs={{0,2},{1,3},{2,0},{3,1},{4,6},{5,7},{6,4},{7,5},{8,10},{9,11},{10,... | collective-permute-start | bytes 196616 | tf_op jit(solution)/shard_map/ppermute | solution.py:262
  10.8 44.2 %collective-permute-start.12 = (f32[128,2048]{1,0:T(8,128)S(1)}, f32[128,2048]{1,0:T(8,128)S(1)}, u32[]{:S(2)}, u32[]{:S(2)}) collective-permute-start(f32[128,2048]{1,0:T(8,128)S(1)} %copy-done.1), channel_id=1, source_target_pairs={{0,16},{1,17},{2,18},{3,19},{4,20},{5,21},{6,22},{7,23},{8,24},{9,... | collective-permute-start | bytes 3145736 | tf_op jit(solution)/shard_map/ppermute | solution.py:262
  13.2 6.7 %collective-permute-start.4 = (f32[32,512]{1,0:T(8,128)S(1)}, f32[32,512]{1,0:T(8,128)S(1)}, u32[]{:S(2)}, u32[]{:S(2)}) collective-permute-start(f32[32,512]{1,0:T(8,128)S(1)} %dynamic-slice_add_fusion), channel_id=1, source_target_pairs={{0,12},{1,13},{2,14},{3,15},{4,8},{5,9},{6,10},{7,11},{8,4},{9,5},... | collective-permute-start | bytes 196616 | tf_op jit(solution)/shard_map/ppermute | solution.py:262
  17.2 5.4 %collective-permute-start.3 = (f32[32,512]{1,0:T(8,128)S(1)}, f32[32,512]{1,0:T(8,128)S(1)}, u32[]{:S(2)}, u32[]{:S(2)}) collective-permute-start(f32[32,512]{1,0:T(8,128)S(1)} %dynamic-slice_add_fusion), channel_id=1, source_target_pairs={{0,8},{1,9},{2,10},{3,11},{4,12},{5,13},{6,14},{7,15},{8,0},{9,1},... | collective-permute-start | bytes 196616 | tf_op jit(solution)/shard_map/ppermute | solution.py:262
  17.2 5.4 %collective-permute-start.2 = (f32[32,512]{1,0:T(8,128)S(1)}, f32[32,512]{1,0:T(8,128)S(1)}, u32[]{:S(2)}, u32[]{:S(2)}) collective-permute-start(f32[32,512]{1,0:T(8,128)S(1)} %dynamic-slice_add_fusion), channel_id=1, source_target_pairs={{0,4},{1,5},{2,6},{3,7},{4,0},{5,1},{6,2},{7,3},{8,12},{9,13},{10,... | collective-permute-start | bytes 196616 | tf_op jit(solution)/shard_map/ppermute | solution.py:262
  22.6 15.0 %collective-permute-start.7 = (f32[32,512]{1,0:T(8,128)S(1)}, f32[32,512]{1,0:T(8,128)S(1)}, u32[]{:S(2)}, u32[]{:S(2)}) collective-permute-start(f32[32,512]{1,0:T(8,128)S(1)} %add_add_fusion.refs_0_), channel_id=1, source_target_pairs={{0,18},{1,19},{2,16},{3,17},{4,22},{5,23},{6,20},{7,21},{8,26},{9,... | collective-permute-start | bytes 196616 | tf_op jit(solution)/shard_map/ppermute | solution.py:262
  25.1 13.4 %collective-permute-start.6 = (f32[32,512]{1,0:T(8,128)S(1)}, f32[32,512]{1,0:T(8,128)S(1)}, u32[]{:S(2)}, u32[]{:S(2)}) collective-permute-start(f32[32,512]{1,0:T(8,128)S(1)} %add_add_fusion.refs_0_), channel_id=1, source_target_pairs={{0,16},{1,17},{2,18},{3,19},{4,20},{5,21},{6,22},{7,23},{8,24},{9,... | collective-permute-start | bytes 196616 | tf_op jit(solution)/shard_map/ppermute | solution.py:262
  25.6 12.9 %collective-permute-start.5 = (f32[32,512]{1,0:T(8,128)S(1)}, f32[32,512]{1,0:T(8,128)S(1)}, u32[]{:S(2)}, u32[]{:S(2)}) collective-permute-start(f32[32,512]{1,0:T(8,128)S(1)} %add_add_fusion.refs_0_), channel_id=1, source_target_pairs={{0,2},{1,3},{2,0},{3,1},{4,6},{5,7},{6,4},{7,5},{8,10},{9,11},{10,... | collective-permute-start | bytes 196616 | tf_op jit(solution)/shard_map/ppermute | solution.py:262
  26.1 12.9 %collective-permute-start.8 = (f32[32,512]{1,0:T(8,128)S(1)}, f32[32,512]{1,0:T(8,128)S(1)}, u32[]{:S(2)}, u32[]{:S(2)}) collective-permute-start(f32[32,512]{1,0:T(8,128)S(1)} %add_add_fusion.refs_0_), channel_id=1, source_target_pairs={{0,1},{1,0},{2,3},{3,2},{4,5},{5,4},{6,7},{7,6},{8,9},{9,8},{10,11... | collective-permute-start | bytes 196616 | tf_op jit(solution)/shard_map/ppermute | solution.py:262
  37.6 1.4 %collective-permute-start.11 = (f32[32,512]{1,0:T(8,128)S(1)}, f32[32,512]{1,0:T(8,128)S(1)}, u32[]{:S(2)}, u32[]{:S(2)}) collective-permute-start(f32[32,512]{1,0:T(8,128)S(1)} %collective-permute-done.7.refs_3_), channel_id=1, source_target_pairs={{0,1},{1,0},{2,3},{3,2},{4,5},{5,4},{6,7},{7,6},{8,9},{9,8},{10,11... | collective-permute-start | bytes 196616 | tf_op jit(solution)/shard_map/ppermute | solution.py:262
  38.5 1.3 %collective-permute-start.10 = (f32[32,512]{1,0:T(8,128)S(1)}, f32[32,512]{1,0:T(8,128)S(1)}, u32[]{:S(2)}, u32[]{:S(2)}) collective-permute-start(f32[32,512]{1,0:T(8,128)S(1)} %collective-permute-done.6.refs_2_), channel_id=1, source_target_pairs={{0,1},{1,0},{2,3},{3,2},{4,5},{5,4},{6,7},{7,6},{8,9},{9,8},{10,11... | collective-permute-start | bytes 196616 | tf_op jit(solution)/shard_map/ppermute | solution.py:262
  38.5 1.4 %collective-permute-start.9 = (f32[32,512]{1,0:T(8,128)S(1)}, f32[32,512]{1,0:T(8,128)S(1)}, u32[]{:S(2)}, u32[]{:S(2)}) collective-permute-start(f32[32,512]{1,0:T(8,128)S(1)} %collective-permute-done.5.refs_1_), channel_id=1, source_target_pairs={{0,1},{1,0},{2,3},{3,2},{4,5},{5,4},{6,7},{7,6},{8,9},{9,8},{10,11... | collective-permute-start | bytes 196616 | tf_op jit(solution)/shard_map/ppermute | solution.py:262

commit v3 on v2

--- a/solution.py
+++ b/solution.py
@@ -11,7 +11,9 @@
 HIGHEST = lax.Precision.HIGHEST
 SUB, LANE = 8, 128
 VMEM = pl.BlockSpec(memory_space=pltpu.VMEM)
+HBM = pl.BlockSpec(memory_space=pltpu.HBM)
 VMEM_LIMIT = 20 << 20
+PARTS, EARLY = 8, 3
 
 
 def dot(a, b, dims, precision=HIGHEST):
@@ -94,48 +96,63 @@
     return lax.bitwise_and(index, 1), lax.bitwise_and(lax.shift_right_logical(index, 1), 1)
 
 
-def forward_kernel(ens, op, keep, send, acc):
-    step = pl.program_id(0)
-
-    @pl.when(step == 0)
-    def _():
-        acc[...] = jnp.zeros_like(acc)
-
-    acc[...] += dot(ens[...], op[...], ((1,), (0,)))
-
-    @pl.when(step == pl.num_programs(0) - 1)
-    def _():
-        half = keep.shape[0]
-        core, _ = own_bits()
-        mine = pl.multiple_of(core * half, SUB)
-        other = pl.multiple_of((1 - core) * half, SUB)
-        keep[...] = acc[pl.ds(mine, half), :]
-        send[...] = acc[pl.ds(other, half), :]
+def dot3(a, b, dims):
+    parts = []
+    for x in (a, b):
+        high = x.astype(jnp.bfloat16)
+        parts.append((high, (x - high.astype(f32)).astype(jnp.bfloat16)))
+    (ah, al), (bh, bl) = parts
+    mul = lambda x, y: lax.dot_general(x, y, (dims, ((), ())), preferred_element_type=f32)
+    return mul(ah, bh) + (mul(ah, bl) + mul(al, bh))
+
+
+def own_bits():
+    index = lax.axis_index("par")
+    return lax.bitwise_and(index, 1), lax.bitwise_and(lax.shift_right_logical(index, 1), 1)
+
+
+def forward_kernel(steps, ens, op, keep, send, ens_buf, op_buf, acc, sems):
+    depth = op.shape[0] // steps
+    cut = lambda i: pl.ds(i * depth, depth)
+    copies = [pltpu.make_async_copy(ens, ens_buf, sems.at[steps])]
+    copies += [pltpu.make_async_copy(op.at[cut(i), :], op_buf.at[cut(i), :], sems.at[i]) for i in range(steps)]
+    for copy in copies:
+        copy.start()
+    copies[0].wait()
+    total = None
+    for i in range(steps):
+        copies[i + 1].wait()
+        term = dot3(ens_buf[:, cut(i)], op_buf[cut(i), :], ((1,), (0,)))
+        total = term if total is None else total + term
+    acc[...] = total
+    half = keep.shape[0]
+    core, _ = own_bits()
+    keep[...] = acc[pl.ds(pl.multiple_of(core * half, SUB), half), :]
+    send[...] = acc[pl.ds(pl.multiple_of((1 - core) * half, SUB), half), :]
 
 
 def forward(ens, op):
     members, params = ens.shape
     rows = op.shape[1]
-    steps = 4 if params % (4 * LANE) == 0 else 1
-    depth = params // steps
+    steps = 8 if params % (8 * LANE) == 0 else 1
     half = jax.ShapeDtypeStruct((members // 2, rows), f32)
-    whole = pl.BlockSpec((members // 2, rows), lambda i: (0, 0))
     return pl.pallas_call(
-        forward_kernel,
-        grid=(steps,),
+        functools.partial(forward_kernel, steps),
         out_shape=(half, half),
-        in_specs=[
-            pl.BlockSpec((members, depth), lambda i: (0, i)),
-            pl.BlockSpec((depth, rows), lambda i: (i, 0)),
+        in_specs=[HBM, HBM],
+        out_specs=(VMEM, VMEM),
+        scratch_shapes=[
+            pltpu.VMEM(ens.shape, f32),
+            pltpu.VMEM(op.shape, f32),
+            pltpu.VMEM((members, rows), f32),
+            pltpu.SemaphoreType.DMA((steps + 1,)),
         ],
-        out_specs=(whole, whole),
-        scratch_shapes=[pltpu.VMEM((members, rows), f32)],
         cost_estimate=pl.CostEstimate(
             flops=2 * members * params * rows, bytes_accessed=4 * (members * params + params * rows), transcendentals=0
         ),
         compiler_params=pltpu.CompilerParams(vmem_limit_bytes=VMEM_LIMIT),
         name="forward",
-    )(ens, op)
+    )(pltpu.with_memory_space_constraint(ens, pltpu.HBM), pltpu.with_memory_space_constraint(op, pltpu.HBM))
 
 
 def lookup_kernel(rows, obs, var, noise, target, inverse_var):
@@ -223,32 +240,43 @@
     )(*pieces, target, inverse_var)
 
 
-def update_kernel(weights, *refs):
-    out = refs[-1]
-    ens = refs[:-1]
-    own = ens[0].shape[0]
-    total = ens[0][...]
-    for far, part in enumerate(ens):
-        total = total + dot(weights[:, far * own : (far + 1) * own], part[...], ((1,), (0,)))
-    out[...] = total
-
-
-def update(weights, ens):
-    own, params = ens[0].shape
-    steps = 4 if params % (4 * LANE) == 0 else 1
-    block = pl.BlockSpec((own, params // steps), lambda i: (0, i))
+def update_kernel(fars, weights, own_ens, *refs):
+    halves = refs[: 2 * fars]
+    out, buf, sems = refs[2 * fars :]
+    own, params = own_ens.shape
+    steps = sems.shape[0]
+    width = params // steps
+    copies = []
+    for i in range(steps):
+        cols = slice(i * width, (i + 1) * width)
+        half, at = (0, i) if i * width < halves[0].shape[1] else (1, i - halves[0].shape[1] // width)
+        part = own_ens[:, cols]
+        total = part + dot3(weights[:, :own], part, ((1,), (0,)))
+        for far in range(fars):
+            w = weights[:, (far + 1) * own : (far + 2) * own]
+            total = total + dot3(w, halves[2 * far + half][:, at * width : (at + 1) * width], ((1,), (0,)))
+        buf[:, cols] = total
+        copies.append(pltpu.make_async_copy(buf.at[:, cols], out.at[:, cols], sems.at[i]))
+        copies[-1].start()
+    for copy in copies:
+        copy.wait()
+
+
+def update(weights, own_ens, halves):
+    own, params = own_ens.shape
+    steps = PARTS
     return pl.pallas_call(
-        update_kernel,
-        grid=(steps,),
+        functools.partial(update_kernel, len(halves) // 2),
         out_shape=jax.ShapeDtypeStruct((own, params), f32),
-        in_specs=[pl.BlockSpec(weights.shape, lambda i: (0, 0))] + [block] * len(ens),
-        out_specs=block,
+        in_specs=[VMEM] * (2 + len(halves)),
+        out_specs=HBM,
+        scratch_shapes=[pltpu.VMEM((own, params), f32), pltpu.SemaphoreType.DMA((steps,))],
         cost_estimate=pl.CostEstimate(
             flops=2 * own * weights.shape[1] * params, bytes_accessed=4 * params * (own + weights.shape[1]), transcendentals=0
         ),
         compiler_params=pltpu.CompilerParams(vmem_limit_bytes=VMEM_LIMIT),
         name="update",
-    )(weights, *ens)
+    )(weights, own_ens, *halves)
 
 
 def per_device(n_mem, n_par, operator, ensemble, noise, observations, variances, rows):
@@ -261,7 +289,8 @@
         ]
         return lax.ppermute(x, ("mem", "par"), pairs)
 
-    ens = [ensemble] + [swap(ensemble, far, 0) for far in range(1, n_mem)]
+    mid = ensemble.shape[1] // PARTS * EARLY
+    early = [swap(ensemble[:, :mid], far, 0) for far in range(1, n_mem)]
     keep, send = forward(ensemble, operator)
     part = keep + swap(send, 0, 1)
     size = part.shape[0] // 2
@@ -274,16 +303,18 @@
         ways = min(4, n_par // stride)
         terms = [total] + [swap(total, 0, d * stride) for d in range(1, ways)]
         if stride == 4:
-            terms, target, inverse_var = lax.optimization_barrier((terms, target, inverse_var))
+            terms, target, inverse_var, early = lax.optimization_barrier((terms, target, inverse_var, early))
         total = add_all(terms)
         stride *= ways
     places = [(far, dy, 0) for far in range(n_mem) for dy in range(2)]
     pieces = [total if (far, dy) == (0, 0) else swap(total, far, 2 * dy) for far, dy, _ in places]
+    rest, pieces = lax.optimization_barrier((ensemble[:, mid:], pieces))
+    late = [swap(rest, far, 0) for far in range(1, n_mem)]
     pieces += [swap(piece, 0, 1) for piece in pieces]
     places += [(far, dy, 1) for far, dy, _ in places]
     members = ensemble.shape[0] * n_mem
     weights = solve(pieces, places, target, inverse_var, members)
-    return update(weights, ens)
+    return update(weights, ensemble, [half for pair in zip(early, late) for half in pair])
 
 
 def solution(mesh):

time: 58.5 us -> 47.5 us (0.81)
  waiting for transfers between devices: 19.2 us -> 10.4 us
  local copies, waits for them, and re-layouts: 3.44 us -> 0.1 us
  starting transfers between devices: 13.7 us -> 15.7 us
  Pallas kernels: 21.9 us -> 20.8 us
    ppermute x13 -> x14, waiting for transfers between devices: 19.2 us -> 10.4 us  [swap(): return lax.ppermute(x, ('mem', 'par'), pairs)]
    unnamed x14 -> x10, local copies, waits for them, and re-layouts: 3.43 us -> 0.02 us
    ppermute x13 -> x14, starting transfers between devices: 13.7 us -> 15.7 us  [swap(): return lax.ppermute(x, ('mem', 'par'), pairs)]
    pallas_call x2, Pallas kernels: 6.12 us -> 4.87 us  [the longest x1 3.09 us: forward(): pl.pallas_call(functools.partial(forward_kernel, steps), out_shape=(half,...]
  transfers between devices with their start and end apart: 13 -> 14, of which waited for: 8 -> 11; matrix products, arithmetic and copies ran while one was open for 0% -> 0% of each run, Pallas kernels for 27% -> 34%
where the time goes in v3:
time: 47.5 us; the launch traced here: 47.4 us
  Pallas kernels  20.8 us (44%)
  starting transfers between devices  15.7 us (33%)
  waiting for transfers between devices  10.4 us (22%)
    ppermute x14, starting transfers between devices, swap(): return lax.ppermute(x, ('mem', 'par'), pairs)  15.7 us
    pallas_call x1, Pallas kernels, solve(): pl.pallas_call(functools.partial(solve_kernel, places, own), out_shape=ja...  15.3 us
    ppermute x14, waiting for transfers between devices, swap(): return lax.ppermute(x, ('mem', 'par'), pairs)  10.4 us
    pallas_call x1, Pallas kernels, forward(): pl.pallas_call(functools.partial(forward_kernel, steps), out_shape=(half,...  3.09 us
    pallas_call x1, Pallas kernels, update(): pl.pallas_call(functools.partial(update_kernel, len(halves) // 2), out_sh...  1.78 us
  transfers between devices with their start and end apart: 14, of which 11 were waited for; matrix products, arithmetic and copies ran while one was open for 0% of the time, Pallas kernels for 34%

profile of v3, /device:TPU:0, one launch (start us, length us, event | category | flops | bytes accessed | tf_op | source)
XLA Modules:
  0.0 47.4 jit_solution(10308444958562060719)
XLA Ops:
  0.0 3.1 %forward.1 = (f32[64,512]{1,0:T(8,128)S(1)}, f32[64,512]{1,0:T(8,128)S(1)}) custom-call(f32[128,2048]{1,0:T(8,128)} %own_ens.1, f32[2048,512]{1,0:T(8,128)} %op.1), custom_call_target="tpu_custom_call" | custom-call | flops 268435456 | bytes 5242880 | tf_op jit(solution)/shard_map/forward/pallas_call | solution.py:139
  3.1 0.5 %collective-permute-start = (f32[64,512]{1,0:T(8,128)S(1)}, f32[64,512]{1,0:T(8,128)S(1)}, u32[]{:S(2)}, u32[]{:S(2)}) collective-permute-start(f32[64,512]{1,0:T(8,128)S(1)} %get-tuple-element.22), channel_id=1, source_target_pairs={{0,1},{1,0},{2,3},{3,2},{4,5},{5,4},{6,7},{7,6},{8,9},{9,8},{10,11... | collective-permute-start | bytes 393224 | tf_op jit(solution)/shard_map/ppermute | solution.py:290
  3.7 1.0 %collective-permute-done = f32[64,512]{1,0:T(8,128)S(1)} collective-permute-done((f32[64,512]{1,0:T(8,128)S(1)}, f32[64,512]{1,0:T(8,128)S(1)}, u32[]{:S(2)}, u32[]{:S(2)}) %collective-permute-start) | collective-permute-done | bytes 131104 | tf_op jit(solution)/shard_map/ppermute | solution.py:290
  4.7 2.9 %collective-permute-start.1 = (f32[32,512]{1,0:T(8,128)S(1)}, f32[32,512]{1,0:T(8,128)S(1)}, u32[]{:S(2)}, u32[]{:S(2)}) collective-permute-start(f32[32,512]{1,0:T(8,128)S(1)} %constant_dynamic-slice_fusion), channel_id=1, source_target_pairs={{0,2},{1,3},{2,0},{3,1},{4,6},{5,7},{6,4},{7,5},{8,10},{9,11},{10,... | collective-permute-start | bytes 196616 | tf_op jit(solution)/shard_map/ppermute | solution.py:290
  7.7 1.6 %collective-permute-start.5 = (f32[128,768]{1,0:T(8,128)S(1)}, f32[128,768]{1,0:T(8,128)S(1)}, u32[]{:S(2)}, u32[]{:S(2)}) collective-permute-start(f32[128,768]{1,0:T(8,128)S(1)} %slice.7), channel_id=1, source_target_pairs={{0,16},{1,17},{2,18},{3,19},{4,20},{5,21},{6,22},{7,23},{8,24},{9,... | collective-permute-start | bytes 1179656 | tf_op jit(solution)/shard_map/ppermute | solution.py:290
  9.2 0.8 %collective-permute-done.1 = f32[32,512]{1,0:T(8,128)S(1)} collective-permute-done((f32[32,512]{1,0:T(8,128)S(1)}, f32[32,512]{1,0:T(8,128)S(1)}, u32[]{:S(2)}, u32[]{:S(2)}) %collective-permute-start.1) | collective-permute-done | bytes 65568 | tf_op jit(solution)/shard_map/ppermute | solution.py:290
  10.0 4.0 %collective-permute-start.4 = (f32[32,512]{1,0:T(8,128)S(1)}, f32[32,512]{1,0:T(8,128)S(1)}, u32[]{:S(2)}, u32[]{:S(2)}) collective-permute-start(f32[32,512]{1,0:T(8,128)S(1)} %dynamic-slice_add_fusion), channel_id=1, source_target_pairs={{0,12},{1,13},{2,14},{3,15},{4,8},{5,9},{6,10},{7,11},{8,4},{9,5},... | collective-permute-start | bytes 196616 | tf_op jit(solution)/shard_map/ppermute | solution.py:290
  14.0 0.6 %collective-permute-start.2 = (f32[32,512]{1,0:T(8,128)S(1)}, f32[32,512]{1,0:T(8,128)S(1)}, u32[]{:S(2)}, u32[]{:S(2)}) collective-permute-start(f32[32,512]{1,0:T(8,128)S(1)} %dynamic-slice_add_fusion), channel_id=1, source_target_pairs={{0,4},{1,5},{2,6},{3,7},{4,0},{5,1},{6,2},{7,3},{8,12},{9,13},{10,... | collective-permute-start | bytes 196616 | tf_op jit(solution)/shard_map/ppermute | solution.py:290
  14.7 0.7 %lookup.1 = (f32[128,512]{1,0:T(8,128)S(1)}, f32[8,512]{1,0:T(8,128)S(1)}) custom-call(s32[1,512]{1,0:T(1,128)S(1)} %bitcast.5, f32[128,128]{1,0:T(8,128)S(1)} %bitcast.3, f32[128,128]{1,0:T(8,128)S(1)} %bitcast.4, f32[128,512]{1,0:T(8,128)S(1)} %copy-done.1), custom_call_target="tpu_custom_call" | custom-call | flops 25769803776 | bytes 1048576 | tf_op jit(solution)/shard_map/lookup/pallas_call | solution.py:174
  15.4 1.4 %collective-permute-done.4 = f32[32,512]{1,0:T(8,128)S(1)} collective-permute-done((f32[32,512]{1,0:T(8,128)S(1)}, f32[32,512]{1,0:T(8,128)S(1)}, u32[]{:S(2)}, u32[]{:S(2)}) %collective-permute-start.4) | collective-permute-done | bytes 65568 | tf_op jit(solution)/shard_map/ppermute | solution.py:290
  16.8 2.6 %collective-permute-done.3 = f32[32,512]{1,0:T(8,128)S(1)} collective-permute-done((f32[32,512]{1,0:T(8,128)S(1)}, f32[32,512]{1,0:T(8,128)S(1)}, u32[]{:S(2)}, u32[]{:S(2)}) %collective-permute-start.3) | collective-permute-done | bytes 65568 | tf_op jit(solution)/shard_map/ppermute | solution.py:290
  19.4 2.5 %collective-permute-start.8 = (f32[32,512]{1,0:T(8,128)S(1)}, f32[32,512]{1,0:T(8,128)S(1)}, u32[]{:S(2)}, u32[]{:S(2)}) collective-permute-start(f32[32,512]{1,0:T(8,128)S(1)} %add_add_fusion.refs_0_), channel_id=1, source_target_pairs={{0,18},{1,19},{2,16},{3,17},{4,22},{5,23},{6,20},{7,21},{8,26},{9,... | collective-permute-start | bytes 196616 | tf_op jit(solution)/shard_map/ppermute | solution.py:290
  22.0 0.5 %collective-permute-start.7 = (f32[32,512]{1,0:T(8,128)S(1)}, f32[32,512]{1,0:T(8,128)S(1)}, u32[]{:S(2)}, u32[]{:S(2)}) collective-permute-start(f32[32,512]{1,0:T(8,128)S(1)} %add_add_fusion.refs_0_), channel_id=1, source_target_pairs={{0,16},{1,17},{2,18},{3,19},{4,20},{5,21},{6,22},{7,23},{8,24},{9,... | collective-permute-start | bytes 196616 | tf_op jit(solution)/shard_map/ppermute | solution.py:290
  22.5 0.5 %collective-permute-start.6 = (f32[32,512]{1,0:T(8,128)S(1)}, f32[32,512]{1,0:T(8,128)S(1)}, u32[]{:S(2)}, u32[]{:S(2)}) collective-permute-start(f32[32,512]{1,0:T(8,128)S(1)} %add_add_fusion.refs_0_), channel_id=1, source_target_pairs={{0,2},{1,3},{2,0},{3,1},{4,6},{5,7},{6,4},{7,5},{8,10},{9,11},{10,... | collective-permute-start | bytes 196616 | tf_op jit(solution)/shard_map/ppermute | solution.py:290
  23.0 1.6 %collective-permute-done.8.refs_3_ = f32[32,512]{1,0:T(8,128)S(1)} collective-permute-done((f32[32,512]{1,0:T(8,128)S(1)}, f32[32,512]{1,0:T(8,128)S(1)}, u32[]{:S(2)}, u32[]{:S(2)}) %collective-permute-start.8) | collective-permute-done | bytes 65568 | tf_op jit(solution)/shard_map/ppermute | solution.py:290
  24.7 1.6 %collective-permute-done.7.refs_2_ = f32[32,512]{1,0:T(8,128)S(1)} collective-permute-done((f32[32,512]{1,0:T(8,128)S(1)}, f32[32,512]{1,0:T(8,128)S(1)}, u32[]{:S(2)}, u32[]{:S(2)}) %collective-permute-start.7) | collective-permute-done | bytes 65568 | tf_op jit(solution)/shard_map/ppermute | solution.py:290
  26.3 0.5 %collective-permute-done.6.refs_1_ = f32[32,512]{1,0:T(8,128)S(1)} collective-permute-done((f32[32,512]{1,0:T(8,128)S(1)}, f32[32,512]{1,0:T(8,128)S(1)}, u32[]{:S(2)}, u32[]{:S(2)}) %collective-permute-start.6) | collective-permute-done | bytes 65568 | tf_op jit(solution)/shard_map/ppermute | solution.py:290
  26.8 1.5 %collective-permute-start.13 = (f32[128,1280]{1,0:T(8,128)S(1)}, f32[128,1280]{1,0:T(8,128)S(1)}, u32[]{:S(2)}, u32[]{:S(2)}) collective-permute-start(f32[128,1280]{1,0:T(8,128)S(1)} %slice.6), channel_id=1, source_target_pairs={{0,16},{1,17},{2,18},{3,19},{4,20},{5,21},{6,22},{7,23},{8,24},{9,... | collective-permute-start | bytes 1966088 | tf_op jit(solution)/shard_map/ppermute | solution.py:290
  28.3 0.5 %collective-permute-start.10 = (f32[32,512]{1,0:T(8,128)S(1)}, f32[32,512]{1,0:T(8,128)S(1)}, u32[]{:S(2)}, u32[]{:S(2)}) collective-permute-start(f32[32,512]{1,0:T(8,128)S(1)} %collective-permute-done.6.refs_1_), channel_id=1, source_target_pairs={{0,1},{1,0},{2,3},{3,2},{4,5},{5,4},{6,7},{7,6},{8,9},{9,8},{10,11... | collective-permute-start | bytes 196616 | tf_op jit(solution)/shard_map/ppermute | solution.py:290
  28.8 0.5 %collective-permute-start.12 = (f32[32,512]{1,0:T(8,128)S(1)}, f32[32,512]{1,0:T(8,128)S(1)}, u32[]{:S(2)}, u32[]{:S(2)}) collective-permute-start(f32[32,512]{1,0:T(8,128)S(1)} %collective-permute-done.8.refs_3_), channel_id=1, source_target_pairs={{0,1},{1,0},{2,3},{3,2},{4,5},{5,4},{6,7},{7,6},{8,9},{9,8},{10,11... | collective-permute-start | bytes 196616 | tf_op jit(solution)/shard_map/ppermute | solution.py:290
  29.3 0.2 collective-permute-done.9.refs_4_
  29.7 0.4 collective-permute-done.11.refs_6_
  30.2 15.3 %solve.1.weights = f32[128,256]{1,0:T(8,128)S(1)} custom-call(f32[32,512]{1,0:T(8,128)S(1)} %add_add_fusion.refs_0_, f32[32,512]{1,0:T(8,128)S(1)} %collective-permute-done.6.refs_1_, f32[32,512]{1,0:T(8,128)S(1)} %collective-permute-done.7.refs_2_, f32[32,512]{1,0:T(8,128)S(1)} %collective-permute-done.8.refs_3_, ...), custom_call_target="tpu_custom_call" | custom-call | flops 1 | bytes 1 | tf_op jit(solution)/shard_map/solve/pallas_call | solution.py:231
  45.4 1.8 %update.1 = f32[128,2048]{1,0:T(8,128)} custom-call(f32[128,256]{1,0:T(8,128)S(1)} %solve.1.weights, f32[128,2048]{1,0:T(8,128)S(1)} %copy-done, f32[128,768]{1,0:T(8,128)S(1)} %collective-permute-done.5.refs_0_, f32[128,1280]{1,0:T(8,128)S(1)} %collective-permute-done.13.refs_1_), custom_call_target="tpu_custom_call" | custom-call | flops 134217728 | bytes 3145728 | tf_op jit(solution)/shard_map/update/pallas_call | solution.py:268
  (24 shorter events, 0.5 us)
Async XLA Ops:
  0.0 7.6 %copy-start = (f32[128,2048]{1,0:T(8,128)S(1)}, f32[128,2048]{1,0:T(8,128)}, u32[]{:S(2)}) copy-start(f32[128,2048]{1,0:T(8,128)} %own_ens.1) | copy-start | bytes 3145732
  0.0 14.7 %copy-start.4 = (s32[512]{0:T(512)S(1)}, s32[512]{0:T(512)}, u32[]{:S(2)}) copy-start(s32[512]{0:T(512)} %param.11) | copy-start | bytes 6148
  0.0 14.7 %copy-start.3 = (f32[16384]{0:T(1024)S(1)}, f32[16384]{0:T(1024)}, u32[]{:S(2)}) copy-start(f32[16384]{0:T(1024)} %param.10) | copy-start | bytes 196612
  0.0 14.7 %copy-start.2 = (f32[16384]{0:T(1024)S(1)}, f32[16384]{0:T(1024)}, u32[]{:S(2)}) copy-start(f32[16384]{0:T(1024)} %param.9) | copy-start | bytes 196612
  0.0 14.7 %copy-start.1 = (f32[128,512]{1,0:T(8,128)S(1)}, f32[128,512]{1,0:T(8,128)}, u32[]{:S(2)}) copy-start(f32[128,512]{1,0:T(8,128)} %noise.1) | copy-start | bytes 786436
  3.1 1.5 %collective-permute-start = (f32[64,512]{1,0:T(8,128)S(1)}, f32[64,512]{1,0:T(8,128)S(1)}, u32[]{:S(2)}, u32[]{:S(2)}) collective-permute-start(f32[64,512]{1,0:T(8,128)S(1)} %get-tuple-element.22), channel_id=1, source_target_pairs={{0,1},{1,0},{2,3},{3,2},{4,5},{5,4},{6,7},{7,6},{8,9},{9,8},{10,11... | collective-permute-start | bytes 393224 | tf_op jit(solution)/shard_map/ppermute | solution.py:290
  4.7 5.3 %collective-permute-start.1 = (f32[32,512]{1,0:T(8,128)S(1)}, f32[32,512]{1,0:T(8,128)S(1)}, u32[]{:S(2)}, u32[]{:S(2)}) collective-permute-start(f32[32,512]{1,0:T(8,128)S(1)} %constant_dynamic-slice_fusion), channel_id=1, source_target_pairs={{0,2},{1,3},{2,0},{3,1},{4,6},{5,7},{6,4},{7,5},{8,10},{9,11},{10,... | collective-permute-start | bytes 196616 | tf_op jit(solution)/shard_map/ppermute | solution.py:290
  7.7 11.8 %collective-permute-start.5 = (f32[128,768]{1,0:T(8,128)S(1)}, f32[128,768]{1,0:T(8,128)S(1)}, u32[]{:S(2)}, u32[]{:S(2)}) collective-permute-start(f32[128,768]{1,0:T(8,128)S(1)} %slice.7), channel_id=1, source_target_pairs={{0,16},{1,17},{2,18},{3,19},{4,20},{5,21},{6,22},{7,23},{8,24},{9,... | collective-permute-start | bytes 1179656 | tf_op jit(solution)/shard_map/ppermute | solution.py:290
  10.0 6.7 %collective-permute-start.4 = (f32[32,512]{1,0:T(8,128)S(1)}, f32[32,512]{1,0:T(8,128)S(1)}, u32[]{:S(2)}, u32[]{:S(2)}) collective-permute-start(f32[32,512]{1,0:T(8,128)S(1)} %dynamic-slice_add_fusion), channel_id=1, source_target_pairs={{0,12},{1,13},{2,14},{3,15},{4,8},{5,9},{6,10},{7,11},{8,4},{9,5},... | collective-permute-start | bytes 196616 | tf_op jit(solution)/shard_map/ppermute | solution.py:290
  14.0 5.4 %collective-permute-start.3 = (f32[32,512]{1,0:T(8,128)S(1)}, f32[32,512]{1,0:T(8,128)S(1)}, u32[]{:S(2)}, u32[]{:S(2)}) collective-permute-start(f32[32,512]{1,0:T(8,128)S(1)} %dynamic-slice_add_fusion), channel_id=1, source_target_pairs={{0,8},{1,9},{2,10},{3,11},{4,12},{5,13},{6,14},{7,15},{8,0},{9,1},... | collective-permute-start | bytes 196616 | tf_op jit(solution)/shard_map/ppermute | solution.py:290
  14.0 5.4 %collective-permute-start.2 = (f32[32,512]{1,0:T(8,128)S(1)}, f32[32,512]{1,0:T(8,128)S(1)}, u32[]{:S(2)}, u32[]{:S(2)}) collective-permute-start(f32[32,512]{1,0:T(8,128)S(1)} %dynamic-slice_add_fusion), channel_id=1, source_target_pairs={{0,4},{1,5},{2,6},{3,7},{4,0},{5,1},{6,2},{7,3},{8,12},{9,13},{10,... | collective-permute-start | bytes 196616 | tf_op jit(solution)/shard_map/ppermute | solution.py:290
  19.4 5.2 %collective-permute-start.8 = (f32[32,512]{1,0:T(8,128)S(1)}, f32[32,512]{1,0:T(8,128)S(1)}, u32[]{:S(2)}, u32[]{:S(2)}) collective-permute-start(f32[32,512]{1,0:T(8,128)S(1)} %add_add_fusion.refs_0_), channel_id=1, source_target_pairs={{0,18},{1,19},{2,16},{3,17},{4,22},{5,23},{6,20},{7,21},{8,26},{9,... | collective-permute-start | bytes 196616 | tf_op jit(solution)/shard_map/ppermute | solution.py:290
  22.0 4.3 %collective-permute-start.7 = (f32[32,512]{1,0:T(8,128)S(1)}, f32[32,512]{1,0:T(8,128)S(1)}, u32[]{:S(2)}, u32[]{:S(2)}) collective-permute-start(f32[32,512]{1,0:T(8,128)S(1)} %add_add_fusion.refs_0_), channel_id=1, source_target_pairs={{0,16},{1,17},{2,18},{3,19},{4,20},{5,21},{6,22},{7,23},{8,24},{9,... | collective-permute-start | bytes 196616 | tf_op jit(solution)/shard_map/ppermute | solution.py:290
  22.5 4.3 %collective-permute-start.6 = (f32[32,512]{1,0:T(8,128)S(1)}, f32[32,512]{1,0:T(8,128)S(1)}, u32[]{:S(2)}, u32[]{:S(2)}) collective-permute-start(f32[32,512]{1,0:T(8,128)S(1)} %add_add_fusion.refs_0_), channel_id=1, source_target_pairs={{0,2},{1,3},{2,0},{3,1},{4,6},{5,7},{6,4},{7,5},{8,10},{9,11},{10,... | collective-permute-start | bytes 196616 | tf_op jit(solution)/shard_map/ppermute | solution.py:290
  26.8 18.7 %collective-permute-start.13 = (f32[128,1280]{1,0:T(8,128)S(1)}, f32[128,1280]{1,0:T(8,128)S(1)}, u32[]{:S(2)}, u32[]{:S(2)}) collective-permute-start(f32[128,1280]{1,0:T(8,128)S(1)} %slice.6), channel_id=1, source_target_pairs={{0,16},{1,17},{2,18},{3,19},{4,20},{5,21},{6,22},{7,23},{8,24},{9,... | collective-permute-start | bytes 1966088 | tf_op jit(solution)/shard_map/ppermute | solution.py:290
  28.2 1.3 %collective-permute-start.9 = (f32[32,512]{1,0:T(8,128)S(1)}, f32[32,512]{1,0:T(8,128)S(1)}, u32[]{:S(2)}, u32[]{:S(2)}) collective-permute-start(f32[32,512]{1,0:T(8,128)S(1)} %add_add_fusion.refs_0_), channel_id=1, source_target_pairs={{0,1},{1,0},{2,3},{3,2},{4,5},{5,4},{6,7},{7,6},{8,9},{9,8},{10,11... | collective-permute-start | bytes 196616 | tf_op jit(solution)/shard_map/ppermute | solution.py:290
  28.3 1.4 %collective-permute-start.10 = (f32[32,512]{1,0:T(8,128)S(1)}, f32[32,512]{1,0:T(8,128)S(1)}, u32[]{:S(2)}, u32[]{:S(2)}) collective-permute-start(f32[32,512]{1,0:T(8,128)S(1)} %collective-permute-done.6.refs_1_), channel_id=1, source_target_pairs={{0,1},{1,0},{2,3},{3,2},{4,5},{5,4},{6,7},{7,6},{8,9},{9,8},{10,11... | collective-permute-start | bytes 196616 | tf_op jit(solution)/shard_map/ppermute | solution.py:290
  28.8 1.3 %collective-permute-start.11 = (f32[32,512]{1,0:T(8,128)S(1)}, f32[32,512]{1,0:T(8,128)S(1)}, u32[]{:S(2)}, u32[]{:S(2)}) collective-permute-start(f32[32,512]{1,0:T(8,128)S(1)} %collective-permute-done.7.refs_2_), channel_id=1, source_target_pairs={{0,1},{1,0},{2,3},{3,2},{4,5},{5,4},{6,7},{7,6},{8,9},{9,8},{10,11... | collective-permute-start | bytes 196616 | tf_op jit(solution)/shard_map/ppermute | solution.py:290
  28.8 1.4 %collective-permute-start.12 = (f32[32,512]{1,0:T(8,128)S(1)}, f32[32,512]{1,0:T(8,128)S(1)}, u32[]{:S(2)}, u32[]{:S(2)}) collective-permute-start(f32[32,512]{1,0:T(8,128)S(1)} %collective-permute-done.8.refs_3_), channel_id=1, source_target_pairs={{0,1},{1,0},{2,3},{3,2},{4,5},{5,4},{6,7},{7,6},{8,9},{9,8},{10,11... | collective-permute-start | bytes 196616 | tf_op jit(solution)/shard_map/ppermute | solution.py:290

commit v4 on v3

--- a/solution.py
+++ b/solution.py
@@ -186,12 +186,10 @@
 
 
 def solve_kernel(places, own, *refs):
-    own_core, own_side = own_bits()
     count = len(places)
     pieces = refs[:count]
-    target, inverse_var = refs[count : count + 2]
-    weights = refs[count + 2]
-    fwd = refs[count + 3]
+    target, inverse_var, weights, fwd, gram, cross, inverse = refs[count:]
+    own_core, own_side = own_bits()
     rows = pieces[0].shape[0]
     for piece, (far, dy, dc) in zip(pieces, places):
         core = own_core if dc == 0 else 1 - own_core
@@ -200,29 +198,37 @@
     members = fwd.shape[0]
     spread = fwd[...] - jnp.mean(fwd[...], axis=0, keepdims=True)
     weighted = spread * inverse_var[0:1, :]
-    gram = dot(weighted, spread, ((1,), (1,)))
-    cross = dot(weighted, target[...] - fwd[0:own, :], ((1,), (1,)))
+    row = lax.broadcasted_iota(jnp.int32, gram.shape, 0)
+    col = lax.broadcasted_iota(jnp.int32, gram.shape, 1)
+    gram[...] = dot3(weighted, spread, ((1,), (1,))) + jnp.where(row == col, float(members - 1), 0.0)
+    cross[...] = dot3(weighted, target[...] - fwd[0:own, :], ((1,), (1,)))
     blocks = members // LANE
-    eye = (
-        lax.broadcasted_iota(jnp.int32, (LANE, LANE), 0) == lax.broadcasted_iota(jnp.int32, (LANE, LANE), 1)
-    ).astype(f32) * (members - 1)
     cut = lambda i: slice(i * LANE, (i + 1) * LANE)
-    g = [[gram[cut(i), cut(k)] + (eye if i == k else 0.0) for k in range(blocks)] for i in range(blocks)]
-    c = [cross[cut(i), :] for i in range(blocks)]
-    t = [[None] * blocks for _ in range(blocks)]
-    for j in range(blocks):
-        inv = block_inverse(g[j][j])
-        c[j] = dot(inv, c[j], ((1,), (0,)))
-        for k in range(j + 1, blocks):
-            t[j][k] = dot(inv, g[j][k], ((1,), (0,)))
-        for i in range(j + 1, blocks):
-            c[i] = c[i] - dot(g[i][j], c[j], ((1,), (0,)))
-            for k in range(j + 1, blocks):
-                g[i][k] = g[i][k] - dot(g[i][j], t[j][k], ((1,), (0,)))
-    for j in reversed(range(blocks)):
-        for k in range(j + 1, blocks):
-            c[j] = c[j] - dot(t[j][k], c[k], ((1,), (0,)))
-    w = jnp.concatenate(c, axis=0)
+
+    def eliminate(j, carry):
+        at = pl.ds(pl.multiple_of(j * LANE, LANE), LANE)
+        inverse[...] = block_inverse(gram[at, at])
+        for i in range(blocks):
+
+            @pl.when(j == i)
+            def _():
+                top = dot3(inverse[...], cross[cut(i), :], ((1,), (0,)))
+                cross[cut(i), :] = top
+                if i + 1 < blocks:
+                    rest = slice((i + 1) * LANE, members)
+                    low = gram[rest, cut(i)]
+                    side = dot3(inverse[...], gram[cut(i), rest], ((1,), (0,)))
+                    gram[rest, rest] = gram[rest, rest] - dot3(low, side, ((1,), (0,)))
+                    cross[rest, :] = cross[rest, :] - dot3(low, top, ((1,), (0,)))
+                    gram[cut(i), rest] = side
+
+        return carry
+
+    lax.fori_loop(0, blocks, eliminate, 0)
+    for i in reversed(range(blocks - 1)):
+        rest = slice((i + 1) * LANE, members)
+        cross[cut(i), :] = cross[cut(i), :] - dot3(gram[cut(i), rest], cross[rest, :], ((1,), (0,)))
+    w = cross[...]
     weights[...] = (w - jnp.mean(w, axis=0, keepdims=True)).T
 
 
@@ -233,8 +239,13 @@
         out_shape=jax.ShapeDtypeStruct((own, members), f32),
         in_specs=[VMEM] * (len(pieces) + 2),
         out_specs=VMEM,
-        scratch_shapes=[pltpu.VMEM((members, rows), f32)],
-        cost_estimate=pl.CostEstimate(flops=1, bytes_accessed=1, transcendentals=0),
+        scratch_shapes=[
+            pltpu.VMEM((members, rows), f32),
+            pltpu.VMEM((members, members), f32),
+            pltpu.VMEM((members, own), f32),
+            pltpu.VMEM((LANE, LANE), f32),
+        ],
+        cost_estimate=pl.CostEstimate(flops=6_000_000_000, bytes_accessed=1, transcendentals=0),
         compiler_params=pltpu.CompilerParams(vmem_limit_bytes=VMEM_LIMIT),
         name="solve",
     )(*pieces, target, inverse_var)
@@ -308,7 +319,7 @@
         stride *= ways
     places = [(far, dy, 0) for far in range(n_mem) for dy in range(2)]
     pieces = [total if (far, dy) == (0, 0) else swap(total, far, 2 * dy) for far, dy, _ in places]
-    rest, pieces = lax.optimization_barrier((ensemble[:, mid:], pieces))
+    rest, _ = lax.optimization_barrier((ensemble[:, mid:], total))
     late = [swap(rest, far, 0) for far in range(1, n_mem)]
     pieces += [swap(piece, 0, 1) for piece in pieces]
     places += [(far, dy, 1) for far, dy, _ in places]

time: 47.5 us -> 40.9 us (0.86)
  Pallas kernels: 20.8 us -> 15.8 us
  waiting for transfers between devices: 10.4 us -> 9.42 us
    pallas_call x1, Pallas kernels: 15.3 us -> 10.2 us  [solve(): pl.pallas_call(functools.partial(solve_kernel, places, own), out_shape=ja...]
    ppermute x14, waiting for transfers between devices: 10.4 us -> 9.42 us  [swap(): return lax.ppermute(x, ('mem', 'par'), pairs)]
  transfers between devices with their start and end apart: 14 -> 14, of which waited for: 11 -> 9; matrix products, arithmetic and copies ran while one was open for 0% -> 0% of each run, Pallas kernels for 34% -> 27%
where the time goes in v4:
time: 40.9 us; the launch traced here: 40.8 us
  Pallas kernels  15.8 us (39%)
  starting transfers between devices  15.4 us (38%)
  waiting for transfers between devices  9.42 us (23%)
    ppermute x14, starting transfers between devices, swap(): return lax.ppermute(x, ('mem', 'par'), pairs)  15.4 us
    pallas_call x1, Pallas kernels, solve(): pl.pallas_call(functools.partial(solve_kernel, places, own), out_shape=ja...  10.2 us
    ppermute x14, waiting for transfers between devices, swap(): return lax.ppermute(x, ('mem', 'par'), pairs)  9.42 us
    pallas_call x1, Pallas kernels, forward(): pl.pallas_call(functools.partial(forward_kernel, steps), out_shape=(half,...  3.1 us
    pallas_call x1, Pallas kernels, update(): pl.pallas_call(functools.partial(update_kernel, len(halves) // 2), out_sh...  1.78 us
  transfers between devices with their start and end apart: 14, of which 9 were waited for; matrix products, arithmetic and copies ran while one was open for 0% of the time, Pallas kernels for 27%

profile of v4, /device:TPU:0, one launch (start us, length us, event | category | flops | bytes accessed | tf_op | source)
XLA Modules:
  0.0 40.8 jit_solution(2808243276770695541)
XLA Ops:
  0.0 3.1 %forward.1 = (f32[64,512]{1,0:T(8,128)S(1)}, f32[64,512]{1,0:T(8,128)S(1)}) custom-call(f32[128,2048]{1,0:T(8,128)} %own_ens.1, f32[2048,512]{1,0:T(8,128)} %op.1), custom_call_target="tpu_custom_call" | custom-call | flops 268435456 | bytes 5242880 | tf_op jit(solution)/shard_map/forward/pallas_call | solution.py:139
  3.1 0.5 %collective-permute-start = (f32[64,512]{1,0:T(8,128)S(1)}, f32[64,512]{1,0:T(8,128)S(1)}, u32[]{:S(2)}, u32[]{:S(2)}) collective-permute-start(f32[64,512]{1,0:T(8,128)S(1)} %get-tuple-element.18), channel_id=1, source_target_pairs={{0,1},{1,0},{2,3},{3,2},{4,5},{5,4},{6,7},{7,6},{8,9},{9,8},{10,11... | collective-permute-start | bytes 393224 | tf_op jit(solution)/shard_map/ppermute | solution.py:301
  3.7 1.0 %collective-permute-done = f32[64,512]{1,0:T(8,128)S(1)} collective-permute-done((f32[64,512]{1,0:T(8,128)S(1)}, f32[64,512]{1,0:T(8,128)S(1)}, u32[]{:S(2)}, u32[]{:S(2)}) %collective-permute-start) | collective-permute-done | bytes 131104 | tf_op jit(solution)/shard_map/ppermute | solution.py:301
  4.7 2.9 %collective-permute-start.1 = (f32[32,512]{1,0:T(8,128)S(1)}, f32[32,512]{1,0:T(8,128)S(1)}, u32[]{:S(2)}, u32[]{:S(2)}) collective-permute-start(f32[32,512]{1,0:T(8,128)S(1)} %constant_dynamic-slice_fusion), channel_id=1, source_target_pairs={{0,2},{1,3},{2,0},{3,1},{4,6},{5,7},{6,4},{7,5},{8,10},{9,11},{10,... | collective-permute-start | bytes 196616 | tf_op jit(solution)/shard_map/ppermute | solution.py:301
  7.6 1.6 %collective-permute-start.5 = (f32[128,768]{1,0:T(8,128)S(1)}, f32[128,768]{1,0:T(8,128)S(1)}, u32[]{:S(2)}, u32[]{:S(2)}) collective-permute-start(f32[128,768]{1,0:T(8,128)S(1)} %slice.6), channel_id=1, source_target_pairs={{0,16},{1,17},{2,18},{3,19},{4,20},{5,21},{6,22},{7,23},{8,24},{9,... | collective-permute-start | bytes 1179656 | tf_op jit(solution)/shard_map/ppermute | solution.py:301
  9.2 0.8 %collective-permute-done.1 = f32[32,512]{1,0:T(8,128)S(1)} collective-permute-done((f32[32,512]{1,0:T(8,128)S(1)}, f32[32,512]{1,0:T(8,128)S(1)}, u32[]{:S(2)}, u32[]{:S(2)}) %collective-permute-start.1) | collective-permute-done | bytes 65568 | tf_op jit(solution)/shard_map/ppermute | solution.py:301
  10.0 4.0 %collective-permute-start.4 = (f32[32,512]{1,0:T(8,128)S(1)}, f32[32,512]{1,0:T(8,128)S(1)}, u32[]{:S(2)}, u32[]{:S(2)}) collective-permute-start(f32[32,512]{1,0:T(8,128)S(1)} %dynamic-slice_add_fusion), channel_id=1, source_target_pairs={{0,12},{1,13},{2,14},{3,15},{4,8},{5,9},{6,10},{7,11},{8,4},{9,5},... | collective-permute-start | bytes 196616 | tf_op jit(solution)/shard_map/ppermute | solution.py:301
  14.1 0.6 %collective-permute-start.2 = (f32[32,512]{1,0:T(8,128)S(1)}, f32[32,512]{1,0:T(8,128)S(1)}, u32[]{:S(2)}, u32[]{:S(2)}) collective-permute-start(f32[32,512]{1,0:T(8,128)S(1)} %dynamic-slice_add_fusion), channel_id=1, source_target_pairs={{0,4},{1,5},{2,6},{3,7},{4,0},{5,1},{6,2},{7,3},{8,12},{9,13},{10,... | collective-permute-start | bytes 196616 | tf_op jit(solution)/shard_map/ppermute | solution.py:301
  14.7 0.7 %lookup.1 = (f32[128,512]{1,0:T(8,128)S(1)}, f32[8,512]{1,0:T(8,128)S(1)}) custom-call(s32[1,512]{1,0:T(1,128)S(1)} %bitcast.5, f32[128,128]{1,0:T(8,128)S(1)} %bitcast.3, f32[128,128]{1,0:T(8,128)S(1)} %bitcast.4, f32[128,512]{1,0:T(8,128)S(1)} %copy-done.1), custom_call_target="tpu_custom_call" | custom-call | flops 25769803776 | bytes 1048576 | tf_op jit(solution)/shard_map/lookup/pallas_call | solution.py:174
  15.4 1.4 %collective-permute-done.4 = f32[32,512]{1,0:T(8,128)S(1)} collective-permute-done((f32[32,512]{1,0:T(8,128)S(1)}, f32[32,512]{1,0:T(8,128)S(1)}, u32[]{:S(2)}, u32[]{:S(2)}) %collective-permute-start.4) | collective-permute-done | bytes 65568 | tf_op jit(solution)/shard_map/ppermute | solution.py:301
  16.8 2.6 %collective-permute-done.3 = f32[32,512]{1,0:T(8,128)S(1)} collective-permute-done((f32[32,512]{1,0:T(8,128)S(1)}, f32[32,512]{1,0:T(8,128)S(1)}, u32[]{:S(2)}, u32[]{:S(2)}) %collective-permute-start.3) | collective-permute-done | bytes 65568 | tf_op jit(solution)/shard_map/ppermute | solution.py:301
  19.5 2.5 %collective-permute-start.8 = (f32[32,512]{1,0:T(8,128)S(1)}, f32[32,512]{1,0:T(8,128)S(1)}, u32[]{:S(2)}, u32[]{:S(2)}) collective-permute-start(f32[32,512]{1,0:T(8,128)S(1)} %add_add_fusion.refs_0_), channel_id=1, source_target_pairs={{0,18},{1,19},{2,16},{3,17},{4,22},{5,23},{6,20},{7,21},{8,26},{9,... | collective-permute-start | bytes 196616 | tf_op jit(solution)/shard_map/ppermute | solution.py:301
  22.0 0.5 %collective-permute-start.7 = (f32[32,512]{1,0:T(8,128)S(1)}, f32[32,512]{1,0:T(8,128)S(1)}, u32[]{:S(2)}, u32[]{:S(2)}) collective-permute-start(f32[32,512]{1,0:T(8,128)S(1)} %add_add_fusion.refs_0_), channel_id=1, source_target_pairs={{0,16},{1,17},{2,18},{3,19},{4,20},{5,21},{6,22},{7,23},{8,24},{9,... | collective-permute-start | bytes 196616 | tf_op jit(solution)/shard_map/ppermute | solution.py:301
  22.5 0.5 %collective-permute-start.6 = (f32[32,512]{1,0:T(8,128)S(1)}, f32[32,512]{1,0:T(8,128)S(1)}, u32[]{:S(2)}, u32[]{:S(2)}) collective-permute-start(f32[32,512]{1,0:T(8,128)S(1)} %add_add_fusion.refs_0_), channel_id=1, source_target_pairs={{0,2},{1,3},{2,0},{3,1},{4,6},{5,7},{6,4},{7,5},{8,10},{9,11},{10,... | collective-permute-start | bytes 196616 | tf_op jit(solution)/shard_map/ppermute | solution.py:301
  23.1 1.5 %collective-permute-start.13 = (f32[128,1280]{1,0:T(8,128)S(1)}, f32[128,1280]{1,0:T(8,128)S(1)}, u32[]{:S(2)}, u32[]{:S(2)}) collective-permute-start(f32[128,1280]{1,0:T(8,128)S(1)} %slice.7), channel_id=1, source_target_pairs={{0,16},{1,17},{2,18},{3,19},{4,20},{5,21},{6,22},{7,23},{8,24},{9,... | collective-permute-start | bytes 1966088 | tf_op jit(solution)/shard_map/ppermute | solution.py:301
  24.6 0.5 %collective-permute-done.8.refs_3_ = f32[32,512]{1,0:T(8,128)S(1)} collective-permute-done((f32[32,512]{1,0:T(8,128)S(1)}, f32[32,512]{1,0:T(8,128)S(1)}, u32[]{:S(2)}, u32[]{:S(2)}) %collective-permute-start.8) | collective-permute-done | bytes 65568 | tf_op jit(solution)/shard_map/ppermute | solution.py:301
  25.1 0.1 collective-permute-start.12
  25.1 1.9 %collective-permute-done.7.refs_2_ = f32[32,512]{1,0:T(8,128)S(1)} collective-permute-done((f32[32,512]{1,0:T(8,128)S(1)}, f32[32,512]{1,0:T(8,128)S(1)}, u32[]{:S(2)}, u32[]{:S(2)}) %collective-permute-start.7) | collective-permute-done | bytes 65568 | tf_op jit(solution)/shard_map/ppermute | solution.py:301
  27.0 0.5 %collective-permute-start.10 = (f32[32,512]{1,0:T(8,128)S(1)}, f32[32,512]{1,0:T(8,128)S(1)}, u32[]{:S(2)}, u32[]{:S(2)}) collective-permute-start(f32[32,512]{1,0:T(8,128)S(1)} %collective-permute-done.6.refs_1_), channel_id=1, source_target_pairs={{0,1},{1,0},{2,3},{3,2},{4,5},{5,4},{6,7},{7,6},{8,9},{9,8},{10,11... | collective-permute-start | bytes 196616 | tf_op jit(solution)/shard_map/ppermute | solution.py:301
  27.5 0.7 %collective-permute-done.11.refs_6_ = f32[32,512]{1,0:T(8,128)S(1)} collective-permute-done((f32[32,512]{1,0:T(8,128)S(1)}, f32[32,512]{1,0:T(8,128)S(1)}, u32[]{:S(2)}, u32[]{:S(2)}) %collective-permute-start.11) | collective-permute-done | bytes 65568 | tf_op jit(solution)/shard_map/ppermute | solution.py:301
  28.2 0.2 collective-permute-done.10.refs_5_
  28.4 10.2 %solve.1.weights = f32[128,256]{1,0:T(8,128)S(1)} custom-call(f32[32,512]{1,0:T(8,128)S(1)} %add_add_fusion.refs_0_, f32[32,512]{1,0:T(8,128)S(1)} %collective-permute-done.6.refs_1_, f32[32,512]{1,0:T(8,128)S(1)} %collective-permute-done.7.refs_2_, f32[32,512]{1,0:T(8,128)S(1)} %collective-permute-done.8.refs_3_, ...), custom_call_target="tpu_custom_call" | custom-call | flops 6000000000 | bytes 1 | tf_op jit(solution)/shard_map/solve/pallas_call | solution.py:237
  38.6 0.4 collective-permute-done.13.refs_1_
  39.0 1.8 %update.1 = f32[128,2048]{1,0:T(8,128)} custom-call(f32[128,256]{1,0:T(8,128)S(1)} %solve.1.weights, f32[128,2048]{1,0:T(8,128)S(1)} %copy-done, f32[128,768]{1,0:T(8,128)S(1)} %collective-permute-done.5.refs_0_, f32[128,1280]{1,0:T(8,128)S(1)} %collective-permute-done.13.refs_1_), custom_call_target="tpu_custom_call" | custom-call | flops 134217728 | bytes 3145728 | tf_op jit(solution)/shard_map/update/pallas_call | solution.py:279
  (24 shorter events, 0.2 us)
Async XLA Ops:
  0.0 7.6 %copy-start = (f32[128,2048]{1,0:T(8,128)S(1)}, f32[128,2048]{1,0:T(8,128)}, u32[]{:S(2)}) copy-start(f32[128,2048]{1,0:T(8,128)} %own_ens.1) | copy-start | bytes 3145732
  0.0 14.7 %copy-start.4 = (s32[512]{0:T(512)S(1)}, s32[512]{0:T(512)}, u32[]{:S(2)}) copy-start(s32[512]{0:T(512)} %param.11) | copy-start | bytes 6148
  0.0 14.7 %copy-start.3 = (f32[16384]{0:T(1024)S(1)}, f32[16384]{0:T(1024)}, u32[]{:S(2)}) copy-start(f32[16384]{0:T(1024)} %param.10) | copy-start | bytes 196612
  0.0 14.7 %copy-start.2 = (f32[16384]{0:T(1024)S(1)}, f32[16384]{0:T(1024)}, u32[]{:S(2)}) copy-start(f32[16384]{0:T(1024)} %param.9) | copy-start | bytes 196612
  0.0 14.7 %copy-start.1 = (f32[128,512]{1,0:T(8,128)S(1)}, f32[128,512]{1,0:T(8,128)}, u32[]{:S(2)}) copy-start(f32[128,512]{1,0:T(8,128)} %noise.1) | copy-start | bytes 786436
  3.1 1.5 %collective-permute-start = (f32[64,512]{1,0:T(8,128)S(1)}, f32[64,512]{1,0:T(8,128)S(1)}, u32[]{:S(2)}, u32[]{:S(2)}) collective-permute-start(f32[64,512]{1,0:T(8,128)S(1)} %get-tuple-element.18), channel_id=1, source_target_pairs={{0,1},{1,0},{2,3},{3,2},{4,5},{5,4},{6,7},{7,6},{8,9},{9,8},{10,11... | collective-permute-start | bytes 393224 | tf_op jit(solution)/shard_map/ppermute | solution.py:301
  4.7 5.3 %collective-permute-start.1 = (f32[32,512]{1,0:T(8,128)S(1)}, f32[32,512]{1,0:T(8,128)S(1)}, u32[]{:S(2)}, u32[]{:S(2)}) collective-permute-start(f32[32,512]{1,0:T(8,128)S(1)} %constant_dynamic-slice_fusion), channel_id=1, source_target_pairs={{0,2},{1,3},{2,0},{3,1},{4,6},{5,7},{6,4},{7,5},{8,10},{9,11},{10,... | collective-permute-start | bytes 196616 | tf_op jit(solution)/shard_map/ppermute | solution.py:301
  7.6 11.8 %collective-permute-start.5 = (f32[128,768]{1,0:T(8,128)S(1)}, f32[128,768]{1,0:T(8,128)S(1)}, u32[]{:S(2)}, u32[]{:S(2)}) collective-permute-start(f32[128,768]{1,0:T(8,128)S(1)} %slice.6), channel_id=1, source_target_pairs={{0,16},{1,17},{2,18},{3,19},{4,20},{5,21},{6,22},{7,23},{8,24},{9,... | collective-permute-start | bytes 1179656 | tf_op jit(solution)/shard_map/ppermute | solution.py:301
  10.0 6.7 %collective-permute-start.4 = (f32[32,512]{1,0:T(8,128)S(1)}, f32[32,512]{1,0:T(8,128)S(1)}, u32[]{:S(2)}, u32[]{:S(2)}) collective-permute-start(f32[32,512]{1,0:T(8,128)S(1)} %dynamic-slice_add_fusion), channel_id=1, source_target_pairs={{0,12},{1,13},{2,14},{3,15},{4,8},{5,9},{6,10},{7,11},{8,4},{9,5},... | collective-permute-start | bytes 196616 | tf_op jit(solution)/shard_map/ppermute | solution.py:301
  14.1 5.4 %collective-permute-start.3 = (f32[32,512]{1,0:T(8,128)S(1)}, f32[32,512]{1,0:T(8,128)S(1)}, u32[]{:S(2)}, u32[]{:S(2)}) collective-permute-start(f32[32,512]{1,0:T(8,128)S(1)} %dynamic-slice_add_fusion), channel_id=1, source_target_pairs={{0,8},{1,9},{2,10},{3,11},{4,12},{5,13},{6,14},{7,15},{8,0},{9,1},... | collective-permute-start | bytes 196616 | tf_op jit(solution)/shard_map/ppermute | solution.py:301
  14.1 5.4 %collective-permute-start.2 = (f32[32,512]{1,0:T(8,128)S(1)}, f32[32,512]{1,0:T(8,128)S(1)}, u32[]{:S(2)}, u32[]{:S(2)}) collective-permute-start(f32[32,512]{1,0:T(8,128)S(1)} %dynamic-slice_add_fusion), channel_id=1, source_target_pairs={{0,4},{1,5},{2,6},{3,7},{4,0},{5,1},{6,2},{7,3},{8,12},{9,13},{10,... | collective-permute-start | bytes 196616 | tf_op jit(solution)/shard_map/ppermute | solution.py:301
  19.5 5.6 %collective-permute-start.8 = (f32[32,512]{1,0:T(8,128)S(1)}, f32[32,512]{1,0:T(8,128)S(1)}, u32[]{:S(2)}, u32[]{:S(2)}) collective-permute-start(f32[32,512]{1,0:T(8,128)S(1)} %add_add_fusion.refs_0_), channel_id=1, source_target_pairs={{0,18},{1,19},{2,16},{3,17},{4,22},{5,23},{6,20},{7,21},{8,26},{9,... | collective-permute-start | bytes 196616 | tf_op jit(solution)/shard_map/ppermute | solution.py:301
  22.0 5.0 %collective-permute-start.7 = (f32[32,512]{1,0:T(8,128)S(1)}, f32[32,512]{1,0:T(8,128)S(1)}, u32[]{:S(2)}, u32[]{:S(2)}) collective-permute-start(f32[32,512]{1,0:T(8,128)S(1)} %add_add_fusion.refs_0_), channel_id=1, source_target_pairs={{0,16},{1,17},{2,18},{3,19},{4,20},{5,21},{6,22},{7,23},{8,24},{9,... | collective-permute-start | bytes 196616 | tf_op jit(solution)/shard_map/ppermute | solution.py:301
  22.5 4.5 %collective-permute-start.6 = (f32[32,512]{1,0:T(8,128)S(1)}, f32[32,512]{1,0:T(8,128)S(1)}, u32[]{:S(2)}, u32[]{:S(2)}) collective-permute-start(f32[32,512]{1,0:T(8,128)S(1)} %add_add_fusion.refs_0_), channel_id=1, source_target_pairs={{0,2},{1,3},{2,0},{3,1},{4,6},{5,7},{6,4},{7,5},{8,10},{9,11},{10,... | collective-permute-start | bytes 196616 | tf_op jit(solution)/shard_map/ppermute | solution.py:301
  23.1 15.9 %collective-permute-start.13 = (f32[128,1280]{1,0:T(8,128)S(1)}, f32[128,1280]{1,0:T(8,128)S(1)}, u32[]{:S(2)}, u32[]{:S(2)}) collective-permute-start(f32[128,1280]{1,0:T(8,128)S(1)} %slice.7), channel_id=1, source_target_pairs={{0,16},{1,17},{2,18},{3,19},{4,20},{5,21},{6,22},{7,23},{8,24},{9,... | collective-permute-start | bytes 1966088 | tf_op jit(solution)/shard_map/ppermute | solution.py:301
  24.6 2.9 %collective-permute-start.9 = (f32[32,512]{1,0:T(8,128)S(1)}, f32[32,512]{1,0:T(8,128)S(1)}, u32[]{:S(2)}, u32[]{:S(2)}) collective-permute-start(f32[32,512]{1,0:T(8,128)S(1)} %add_add_fusion.refs_0_), channel_id=1, source_target_pairs={{0,1},{1,0},{2,3},{3,2},{4,5},{5,4},{6,7},{7,6},{8,9},{9,8},{10,11... | collective-permute-start | bytes 196616 | tf_op jit(solution)/shard_map/ppermute | solution.py:301
  25.1 2.4 %collective-permute-start.12 = (f32[32,512]{1,0:T(8,128)S(1)}, f32[32,512]{1,0:T(8,128)S(1)}, u32[]{:S(2)}, u32[]{:S(2)}) collective-permute-start(f32[32,512]{1,0:T(8,128)S(1)} %collective-permute-done.8.refs_3_), channel_id=1, source_target_pairs={{0,1},{1,0},{2,3},{3,2},{4,5},{5,4},{6,7},{7,6},{8,9},{9,8},{10,11... | collective-permute-start | bytes 196616 | tf_op jit(solution)/shard_map/ppermute | solution.py:301
  27.0 1.3 %collective-permute-start.11 = (f32[32,512]{1,0:T(8,128)S(1)}, f32[32,512]{1,0:T(8,128)S(1)}, u32[]{:S(2)}, u32[]{:S(2)}) collective-permute-start(f32[32,512]{1,0:T(8,128)S(1)} %collective-permute-done.7.refs_2_), channel_id=1, source_target_pairs={{0,1},{1,0},{2,3},{3,2},{4,5},{5,4},{6,7},{7,6},{8,9},{9,8},{10,11... | collective-permute-start | bytes 196616 | tf_op jit(solution)/shard_map/ppermute | solution.py:301
  27.0 1.4 %collective-permute-start.10 = (f32[32,512]{1,0:T(8,128)S(1)}, f32[32,512]{1,0:T(8,128)S(1)}, u32[]{:S(2)}, u32[]{:S(2)}) collective-permute-start(f32[32,512]{1,0:T(8,128)S(1)} %collective-permute-done.6.refs_1_), channel_id=1, source_target_pairs={{0,1},{1,0},{2,3},{3,2},{4,5},{5,4},{6,7},{7,6},{8,9},{9,8},{10,11... | collective-permute-start | bytes 196616 | tf_op jit(solution)/shard_map/ppermute | solution.py:301

commit v5 on v3

--- a/solution.py
+++ b/solution.py
@@ -28,34 +28,28 @@
     return terms[0]
 
 
-def small_inverse(e):
-    n = len(e)
-
-    def at(m, i, k):
-        return m[min(i, k)][max(i, k)]
-
-    if n == 2:
-        a, b, c = e[0][0], e[0][1], e[1][1]
-        d = 1.0 / (a * c - b * b)
-        return [[c * d, -(b * d)], [None, a * d]]
-    m = n // 2
-    span = range(m)
-    top = small_inverse([[at(e, i, k) for k in span] for i in span])
-    side = [[at(e, i, m + k) for k in span] for i in span]
-    t = [[add_all(at(top, i, l) * side[l][k] for l in span) for k in span] for i in span]
-    rest = [
-        [at(e, m + i, m + k) - add_all(side[l][i] * t[l][k] for l in span) if i <= k else None for k in span]
-        for i in span
-    ]
-    low = small_inverse(rest)
-    u = [[add_all(t[i][l] * at(low, l, k) for l in span) for k in span] for i in span]
-    out = [[None] * n for _ in range(n)]
-    for i in span:
-        for k in span:
-            if i <= k:
-                out[i][k] = top[i][k] + add_all(u[i][l] * t[k][l] for l in span)
-                out[m + i][m + k] = low[i][k]
-            out[i][m + k] = -u[i][k]
+def pivot_rows(e, rows):
+    n = len(rows)
+    e = [list(line) for line in e]
+    rows = list(rows)
+    low = [[None] * n for _ in range(n)]
+    out = [None] * n
+    for a in range(0, n, 2):
+        b = a + 1
+        scale = 1.0 / (e[a][a] * e[b][b] - e[a][b] * e[a][b])
+        aa, bb, ab = e[b][b] * scale, e[a][a] * scale, -(e[a][b] * scale)
+        out[a] = aa * rows[a] + ab * rows[b]
+        out[b] = ab * rows[a] + bb * rows[b]
+        for i in range(b + 1, n):
+            la = e[a][i] * aa + e[b][i] * ab
+            lb = e[a][i] * ab + e[b][i] * bb
+            low[i][a], low[i][b] = la, lb
+            for m in range(i, n):
+                e[i][m] = e[i][m] - (la * e[a][m] + lb * e[b][m])
+            rows[i] = rows[i] - (la * rows[a] + lb * rows[b])
+    for a in range(n - 4, -1, -2):
+        for k in (a, a + 1):
+            out[k] = out[k] - add_all(low[i][k] * out[i] for i in range(a + 2, n))
     return out
 
 
@@ -63,32 +57,33 @@
     return jnp.broadcast_to(v[:, k : k + 1], v.shape)
 
 
-def down(v, i):
-    return jnp.broadcast_to(v[i : i + 1, :], v.shape)
-
-
-def block_inverse(matrix):
-    lane = lax.broadcasted_iota(jnp.int32, (SUB, LANE), 1)
-    sub = lax.broadcasted_iota(jnp.int32, (SUB, LANE), 0)
-    n = LANE // SUB
+def block_inverse(matrix, buf):
+    size = matrix.shape[0]
+    lane = lax.broadcasted_iota(jnp.int32, (SUB, size), 1)
+    sub = lax.broadcasted_iota(jnp.int32, (SUB, size), 0)
+    n = size // SUB
     m = [matrix[SUB * i : SUB * (i + 1), :] for i in range(n)]
+    low, scaled = [], []
     for j in range(n):
         at = SUB * j
         here = (lane >= at) & (lane < at + SUB)
-        cols = [across(m[j], at + k) for k in range(SUB)]
-        inv = small_inverse([[down(cols[k], i) if i <= k else None for k in range(SUB)] for i in range(SUB)])
+        base = (j % 2) * SUB * (SUB + 1)
+        for k in range(SUB):
+            buf[base + SUB * k : base + SUB * (k + 1), :] = across(m[j], at + k)
         row = jnp.where(here, (lane - at == sub).astype(f32), m[j])
-        rows = [down(row, k) for k in range(SUB)]
-        new = [add_all(inv[min(i, k)][max(i, k)] * rows[k] for k in range(SUB)) for i in range(SUB)]
-        for d in range(1, n):
-            i = (j + d) % n
-            drop = add_all(across(m[i], at + k) * new[k] for k in range(SUB))
-            m[i] = jnp.where(here, 0.0, m[i]) - drop
+        buf[base + SUB * SUB : base + SUB * (SUB + 1), :] = row
+        spread = lambda i: jnp.broadcast_to(buf[base + i : base + i + 1, :], (SUB, size))
+        e = [[spread(SUB * k + i) if i <= k else None for k in range(SUB)] for i in range(SUB)]
+        new = pivot_rows(e, [spread(SUB * SUB + k) for k in range(SUB)])
+        for i in range(j + 1, n):
+            m[i] = jnp.where(here, 0.0, m[i]) - add_all(across(m[i], at + k) * new[k] for k in range(SUB))
         done = new[0]
         for i in range(1, SUB):
             done = jnp.where(sub == i, new[i], done)
-        m[j] = done
-    return jnp.concatenate(m, axis=0)
+        keep = lane < at + SUB
+        low.append(jnp.where(keep, row, 0.0))
+        scaled.append(jnp.where(keep, done, 0.0))
+    return jnp.concatenate(low, axis=0), jnp.concatenate(scaled, axis=0)
 
 
 def own_bits():
@@ -155,7 +150,7 @@
     )(pltpu.with_memory_space_constraint(ens, pltpu.HBM), pltpu.with_memory_space_constraint(op, pltpu.HBM))
 
 
-def lookup_kernel(rows, obs, var, noise, target, inverse_var):
+def lookup_kernel(rows, obs, var, noise, target, root):
     index = rows[...]
     high = lax.shift_right_logical(index, 7)
     low = lax.bitwise_and(index, LANE - 1)
@@ -166,7 +161,7 @@
     obs_rows = jnp.sum(dot(obs[...], pick_high, ((0,), (0,))) * pick_low, axis=0, keepdims=True)
     var_rows = jnp.sum(dot(var[...], pick_high, ((0,), (0,))) * pick_low, axis=0, keepdims=True)
     target[...] = obs_rows + jnp.sqrt(var_rows) * noise[...]
-    inverse_var[...] = jnp.broadcast_to(1.0 / var_rows, inverse_var.shape)
+    root[...] = jnp.broadcast_to(lax.rsqrt(var_rows), root.shape)
 
 
 def lookup(rows, obs, var, noise):
@@ -185,59 +180,130 @@
     )(rows.reshape(1, count), obs.reshape(-1, LANE), var.reshape(-1, LANE), noise)
 
 
-def solve_kernel(places, own, *refs):
-    own_core, own_side = own_bits()
+def fenced(body):
+    pl.when(lax.axis_index("par") >= 0)(body)
+
+
+def set_inverse(out, matrix, buf, low, scaled):
+    @fenced
+    def _():
+        low[...], scaled[...] = block_inverse(matrix[...], buf)
+
+    out[...] = dot3(low[...], scaled[...], ((0,), (0,)))
+
+
+def add_diagonal(matrix, value):
+    row = lax.broadcasted_iota(jnp.int32, matrix.shape, 0)
+    col = lax.broadcasted_iota(jnp.int32, matrix.shape, 1)
+    return matrix + jnp.where(row == col, value, 0.0)
+
+
+def near_kernel(members, count, *refs):
+    pieces = refs[:count]
+    root, inverse, near, shift, gram, buf, low, scaled = refs[count:]
+    rows = pieces[0].shape[0]
+    for i, piece in enumerate(pieces):
+        near[i * rows : (i + 1) * rows, :] = piece[...]
+    mean = jnp.mean(near[...], axis=0, keepdims=True)
+    shift[...] = jnp.broadcast_to(mean, shift.shape)
+    z = (near[...] - mean) * root[0:1, :]
+    near[...] = z
+    gram[...] = add_diagonal(dot3(z, z, ((1,), (1,))), float(members - 1))
+    set_inverse(inverse, gram, buf, low, scaled)
+
+
+def solve_near(pieces, root, members):
+    rows, cols = pieces[0].shape
+    size = rows * len(pieces)
+    square = jax.ShapeDtypeStruct((size, size), f32)
+    return pl.pallas_call(
+        functools.partial(near_kernel, members, len(pieces)),
+        out_shape=(square, jax.ShapeDtypeStruct((size, cols), f32), jax.ShapeDtypeStruct((SUB, cols), f32)),
+        in_specs=[VMEM] * (len(pieces) + 1),
+        out_specs=(VMEM, VMEM, VMEM),
+        scratch_shapes=solve_scratch(size),
+        cost_estimate=pl.CostEstimate(flops=3_000_000_000, bytes_accessed=1, transcendentals=0),
+        compiler_params=pltpu.CompilerParams(vmem_limit_bytes=VMEM_LIMIT),
+        name="solve_near",
+    )(*pieces, root)
+
+
+def solve_scratch(size):
+    return [
+        pltpu.VMEM((size, size), f32),
+        pltpu.VMEM((2 * SUB * (SUB + 1), size), f32),
+        pltpu.VMEM((size, size), f32),
+        pltpu.VMEM((size, size), f32),
+    ]
+
+
+def solve_kernel(places, *refs):
     count = len(places)
     pieces = refs[:count]
-    target, inverse_var = refs[count : count + 2]
-    weights = refs[count + 2]
-    fwd = refs[count + 3]
+    inverse, near, shift, target, root, weights = refs[count : count + 6]
+    fwd, gram, buf, low, scaled, second, far_z, right, out = refs[count + 6 :]
     rows = pieces[0].shape[0]
-    for piece, (far, dy, dc) in zip(pieces, places):
+    own, size = target.shape[0], near.shape[0]
+    members = 2 * size
+    own_core, own_side = own_bits()
+
+    def start(place):
+        far, dy, dc = place
         core = own_core if dc == 0 else 1 - own_core
         side = own_side if dy == 0 else 1 - own_side
-        fwd[pl.ds(pl.multiple_of(far * own + (core * 2 + side) * rows, SUB), rows), :] = piece[...]
-    members = fwd.shape[0]
-    spread = fwd[...] - jnp.mean(fwd[...], axis=0, keepdims=True)
-    weighted = spread * inverse_var[0:1, :]
-    gram = dot(weighted, spread, ((1,), (1,)))
-    cross = dot(weighted, target[...] - fwd[0:own, :], ((1,), (1,)))
-    blocks = members // LANE
-    eye = (
-        lax.broadcasted_iota(jnp.int32, (LANE, LANE), 0) == lax.broadcasted_iota(jnp.int32, (LANE, LANE), 1)
-    ).astype(f32) * (members - 1)
-    cut = lambda i: slice(i * LANE, (i + 1) * LANE)
-    g = [[gram[cut(i), cut(k)] + (eye if i == k else 0.0) for k in range(blocks)] for i in range(blocks)]
-    c = [cross[cut(i), :] for i in range(blocks)]
-    t = [[None] * blocks for _ in range(blocks)]
-    for j in range(blocks):
-        inv = block_inverse(g[j][j])
-        c[j] = dot(inv, c[j], ((1,), (0,)))
-        for k in range(j + 1, blocks):
-            t[j][k] = dot(inv, g[j][k], ((1,), (0,)))
-        for i in range(j + 1, blocks):
-            c[i] = c[i] - dot(g[i][j], c[j], ((1,), (0,)))
-            for k in range(j + 1, blocks):
-                g[i][k] = g[i][k] - dot(g[i][j], t[j][k], ((1,), (0,)))
-    for j in reversed(range(blocks)):
-        for k in range(j + 1, blocks):
-            c[j] = c[j] - dot(t[j][k], c[k], ((1,), (0,)))
-    w = jnp.concatenate(c, axis=0)
-    weights[...] = (w - jnp.mean(w, axis=0, keepdims=True)).T
-
-
-def solve(pieces, places, target, inverse_var, members):
-    own, rows = target.shape
-    return pl.pallas_call(
-        functools.partial(solve_kernel, places, own),
-        out_shape=jax.ShapeDtypeStruct((own, members), f32),
-        in_specs=[VMEM] * (len(pieces) + 2),
+        return pl.multiple_of(far * own + (core * 2 + side) * rows, SUB)
+
+    for piece, place in zip(pieces, places):
+        if place[0] == 0:
+            fwd[pl.ds(start(place), rows), :] = piece[...]
+    scale = root[0:1, :]
+    for i, piece in enumerate(pieces[count // 2 :]):
+        far_z[i * rows : (i + 1) * rows, :] = (piece[...] - shift[0:1, :]) * scale
+    residual = (target[...] - fwd[...]) * scale
+    za, zb = near[...], far_z[...]
+    side = dot3(zb, za, ((1,), (1,)))
+    ca, cb = dot3(za, residual, ((1,), (1,))), dot3(zb, residual, ((1,), (1,)))
+    mean = (jnp.sum(ca, axis=0, keepdims=True) + jnp.sum(cb, axis=0, keepdims=True)) / members
+    ones = jnp.ones((size, own), f32)
+    ra = jnp.concatenate([ca - mean, ones], axis=1)
+    rb = jnp.concatenate([cb - mean, ones], axis=1)
+    top = dot3(inverse[...], jnp.concatenate([side.T, ra], axis=1), ((1,), (0,)))
+    drop = dot3(side, top, ((1,), (0,)))
+    gram[...] = add_diagonal(dot3(zb, zb, ((1,), (1,))), float(members - 1)) - drop[:, :size]
+    right[0:size, :] = top
+    right[size:, size:] = rb - drop[:, size:]
+    set_inverse(second, gram, buf, low, scaled)
+    xb = dot3(second[...], right[size:, size:], ((1,), (0,)))
+    xa = right[0:size, size:] - dot3(right[0:size, 0:size], xb, ((1,), (0,)))
+    x = jnp.concatenate([xa, xb], axis=0)
+    w, unit = x[:, :own], x[:, own:]
+    w = w - unit * (jnp.sum(w, axis=0, keepdims=True) / jnp.sum(unit, axis=0, keepdims=True))
+    w = w - jnp.mean(w, axis=0, keepdims=True)
+    for i, place in enumerate(places):
+        out[pl.ds(start(place), rows), :] = w[i * rows : (i + 1) * rows, :]
+    weights[...] = out[...].T
+
+
+def solve(pieces, places, inverse, near, shift, target, root):
+    own, cols = target.shape
+    size = near.shape[0]
+    return pl.pallas_call(
+        functools.partial(solve_kernel, places),
+        out_shape=jax.ShapeDtypeStruct((own, 2 * size), f32),
+        in_specs=[VMEM] * (len(pieces) + 5),
         out_specs=VMEM,
-        scratch_shapes=[pltpu.VMEM((members, rows), f32)],
-        cost_estimate=pl.CostEstimate(flops=1, bytes_accessed=1, transcendentals=0),
+        scratch_shapes=[pltpu.VMEM((own, cols), f32)]
+        + solve_scratch(size)
+        + [
+            pltpu.VMEM((size, size), f32),
+            pltpu.VMEM((size, cols), f32),
+            pltpu.VMEM((2 * size, size + 2 * own), f32),
+            pltpu.VMEM((2 * size, own), f32),
+        ],
+        cost_estimate=pl.CostEstimate(flops=3_000_000_000, bytes_accessed=1, transcendentals=0),
         compiler_params=pltpu.CompilerParams(vmem_limit_bytes=VMEM_LIMIT),
         name="solve",
-    )(*pieces, target, inverse_var)
+    )(*pieces, inverse, near, shift, target, root)
 
 
 def update_kernel(fars, weights, own_ens, *refs):
@@ -297,23 +363,23 @@
     total = lax.dynamic_slice_in_dim(part, side * size, size, 0) + swap(
         lax.dynamic_slice_in_dim(part, (1 - side) * size, size, 0), 0, 2
     )
-    target, inverse_var = lookup(rows, observations, variances, noise)
+    target, root = lookup(rows, observations, variances, noise)
     stride = 4
     while stride < n_par:
         ways = min(4, n_par // stride)
         terms = [total] + [swap(total, 0, d * stride) for d in range(1, ways)]
         if stride == 4:
-            terms, target, inverse_var, early = lax.optimization_barrier((terms, target, inverse_var, early))
+            terms, target, root, early = lax.optimization_barrier((terms, target, root, early))
         total = add_all(terms)
         stride *= ways
     places = [(far, dy, 0) for far in range(n_mem) for dy in range(2)]
     pieces = [total if (far, dy) == (0, 0) else swap(total, far, 2 * dy) for far, dy, _ in places]
-    rest, pieces = lax.optimization_barrier((ensemble[:, mid:], pieces))
+    rest, _ = lax.optimization_barrier((ensemble[:, mid:], total))
     late = [swap(rest, far, 0) for far in range(1, n_mem)]
+    inverse, near, shift = solve_near(pieces, root, ensemble.shape[0] * n_mem)
     pieces += [swap(piece, 0, 1) for piece in pieces]
     places += [(far, dy, 1) for far, dy, _ in places]
-    members = ensemble.shape[0] * n_mem
-    weights = solve(pieces, places, target, inverse_var, members)
+    weights = solve(pieces, places, inverse, near, shift, target, root)
     return update(weights, ensemble, [half for pair in zip(early, late) for half in pair])
 
 

time: 47.5 us -> 49.6 us (1.044)
  waiting for transfers between devices: 10.4 us -> 19.1 us
  Pallas kernels: 20.8 us -> 14.8 us
    ppermute x14, waiting for transfers between devices: 10.4 us -> 19.1 us  [swap(): return lax.ppermute(x, ('mem', 'par'), pairs)]
    pallas_call x1 -> x2, Pallas kernels: 15.3 us -> 9.22 us  [the longest x1 5.36 us: solve(): pl.pallas_call(functools.partial(solve_kernel, places), out_shape=jax.Sha...]
  transfers between devices with their start and end apart: 14 -> 14, of which waited for: 11 -> 5; matrix products, arithmetic and copies ran while one was open for 0% -> 0% of each run, Pallas kernels for 34% -> 20%
where the time goes in v5:
time: 49.6 us; the launch traced here: 49.4 us
  waiting for transfers between devices  19.1 us (39%)
  starting transfers between devices  15.3 us (31%)
  Pallas kernels  14.8 us (30%)
    ppermute x14, waiting for transfers between devices, swap(): return lax.ppermute(x, ('mem', 'par'), pairs)  19.1 us
    ppermute x14, starting transfers between devices, swap(): return lax.ppermute(x, ('mem', 'par'), pairs)  15.3 us
    pallas_call x1, Pallas kernels, solve(): pl.pallas_call(functools.partial(solve_kernel, places), out_shape=jax.Sha...  5.36 us
    pallas_call x1, Pallas kernels, solve_near(): pl.pallas_call(functools.partial(near_kernel, members, len(pieces)), out_...  3.86 us
    pallas_call x1, Pallas kernels, forward(): pl.pallas_call(functools.partial(forward_kernel, steps), out_shape=(half,...  3.1 us
    pallas_call x1, Pallas kernels, update(): pl.pallas_call(functools.partial(update_kernel, len(halves) // 2), out_sh...  1.78 us
  transfers between devices with their start and end apart: 14, of which 5 were waited for; matrix products, arithmetic and copies ran while one was open for 0% of the time, Pallas kernels for 20%

profile of v5, /device:TPU:0, one launch (start us, length us, event | category | flops | bytes accessed | tf_op | source)
XLA Modules:
  0.0 49.4 jit_solution(3456171978954660417)
XLA Ops:
  0.0 3.1 %forward.1 = (f32[64,512]{1,0:T(8,128)S(1)}, f32[64,512]{1,0:T(8,128)S(1)}) custom-call(f32[128,2048]{1,0:T(8,128)} %own_ens.1, f32[2048,512]{1,0:T(8,128)} %op.1), custom_call_target="tpu_custom_call" | custom-call | flops 268435456 | bytes 5242880 | tf_op jit(solution)/shard_map/forward/pallas_call | solution.py:134
  3.1 0.5 %collective-permute-start = (f32[64,512]{1,0:T(8,128)S(1)}, f32[64,512]{1,0:T(8,128)S(1)}, u32[]{:S(2)}, u32[]{:S(2)}) collective-permute-start(f32[64,512]{1,0:T(8,128)S(1)} %get-tuple-element.21), channel_id=1, source_target_pairs={{0,1},{1,0},{2,3},{3,2},{4,5},{5,4},{6,7},{7,6},{8,9},{9,8},{10,11... | collective-permute-start | bytes 393224 | tf_op jit(solution)/shard_map/ppermute | solution.py:356
  3.7 1.0 %collective-permute-done = f32[64,512]{1,0:T(8,128)S(1)} collective-permute-done((f32[64,512]{1,0:T(8,128)S(1)}, f32[64,512]{1,0:T(8,128)S(1)}, u32[]{:S(2)}, u32[]{:S(2)}) %collective-permute-start) | collective-permute-done | bytes 131104 | tf_op jit(solution)/shard_map/ppermute | solution.py:356
  4.7 2.9 %collective-permute-start.1 = (f32[32,512]{1,0:T(8,128)S(1)}, f32[32,512]{1,0:T(8,128)S(1)}, u32[]{:S(2)}, u32[]{:S(2)}) collective-permute-start(f32[32,512]{1,0:T(8,128)S(1)} %constant_dynamic-slice_fusion), channel_id=1, source_target_pairs={{0,2},{1,3},{2,0},{3,1},{4,6},{5,7},{6,4},{7,5},{8,10},{9,11},{10,... | collective-permute-start | bytes 196616 | tf_op jit(solution)/shard_map/ppermute | solution.py:356
  7.6 1.6 %collective-permute-start.5 = (f32[128,768]{1,0:T(8,128)S(1)}, f32[128,768]{1,0:T(8,128)S(1)}, u32[]{:S(2)}, u32[]{:S(2)}) collective-permute-start(f32[128,768]{1,0:T(8,128)S(1)} %slice.6), channel_id=1, source_target_pairs={{0,16},{1,17},{2,18},{3,19},{4,20},{5,21},{6,22},{7,23},{8,24},{9,... | collective-permute-start | bytes 1179656 | tf_op jit(solution)/shard_map/ppermute | solution.py:356
  9.2 0.8 %collective-permute-done.1 = f32[32,512]{1,0:T(8,128)S(1)} collective-permute-done((f32[32,512]{1,0:T(8,128)S(1)}, f32[32,512]{1,0:T(8,128)S(1)}, u32[]{:S(2)}, u32[]{:S(2)}) %collective-permute-start.1) | collective-permute-done | bytes 65568 | tf_op jit(solution)/shard_map/ppermute | solution.py:356
  10.0 4.0 %collective-permute-start.4 = (f32[32,512]{1,0:T(8,128)S(1)}, f32[32,512]{1,0:T(8,128)S(1)}, u32[]{:S(2)}, u32[]{:S(2)}) collective-permute-start(f32[32,512]{1,0:T(8,128)S(1)} %dynamic-slice_add_fusion), channel_id=1, source_target_pairs={{0,12},{1,13},{2,14},{3,15},{4,8},{5,9},{6,10},{7,11},{8,4},{9,5},... | collective-permute-start | bytes 196616 | tf_op jit(solution)/shard_map/ppermute | solution.py:356
  14.1 0.0 collective-permute-start.3
  14.1 0.6 %collective-permute-start.2 = (f32[32,512]{1,0:T(8,128)S(1)}, f32[32,512]{1,0:T(8,128)S(1)}, u32[]{:S(2)}, u32[]{:S(2)}) collective-permute-start(f32[32,512]{1,0:T(8,128)S(1)} %dynamic-slice_add_fusion), channel_id=1, source_target_pairs={{0,4},{1,5},{2,6},{3,7},{4,0},{5,1},{6,2},{7,3},{8,12},{9,13},{10,... | collective-permute-start | bytes 196616 | tf_op jit(solution)/shard_map/ppermute | solution.py:356
  14.7 0.7 %lookup.1 = (f32[128,512]{1,0:T(8,128)S(1)}, f32[8,512]{1,0:T(8,128)S(1)}) custom-call(s32[1,512]{1,0:T(1,128)S(1)} %bitcast.5, f32[128,128]{1,0:T(8,128)S(1)} %bitcast.3, f32[128,128]{1,0:T(8,128)S(1)} %bitcast.4, f32[128,512]{1,0:T(8,128)S(1)} %copy-done.1), custom_call_target="tpu_custom_call" | custom-call | flops 25769803776 | bytes 1048576 | tf_op jit(solution)/shard_map/lookup/pallas_call | solution.py:169
  15.5 1.3 %collective-permute-done.4 = f32[32,512]{1,0:T(8,128)S(1)} collective-permute-done((f32[32,512]{1,0:T(8,128)S(1)}, f32[32,512]{1,0:T(8,128)S(1)}, u32[]{:S(2)}, u32[]{:S(2)}) %collective-permute-start.4) | collective-permute-done | bytes 65568 | tf_op jit(solution)/shard_map/ppermute | solution.py:356
  16.8 2.6 %collective-permute-done.3 = f32[32,512]{1,0:T(8,128)S(1)} collective-permute-done((f32[32,512]{1,0:T(8,128)S(1)}, f32[32,512]{1,0:T(8,128)S(1)}, u32[]{:S(2)}, u32[]{:S(2)}) %collective-permute-start.3) | collective-permute-done | bytes 65568 | tf_op jit(solution)/shard_map/ppermute | solution.py:356
  19.5 1.5 %collective-permute-start.13 = (f32[128,1280]{1,0:T(8,128)S(1)}, f32[128,1280]{1,0:T(8,128)S(1)}, u32[]{:S(2)}, u32[]{:S(2)}) collective-permute-start(f32[128,1280]{1,0:T(8,128)S(1)} %slice.7), channel_id=1, source_target_pairs={{0,16},{1,17},{2,18},{3,19},{4,20},{5,21},{6,22},{7,23},{8,24},{9,... | collective-permute-start | bytes 1966088 | tf_op jit(solution)/shard_map/ppermute | solution.py:356
  21.0 1.5 %collective-permute-start.8 = (f32[32,512]{1,0:T(8,128)S(1)}, f32[32,512]{1,0:T(8,128)S(1)}, u32[]{:S(2)}, u32[]{:S(2)}) collective-permute-start(f32[32,512]{1,0:T(8,128)S(1)} %add_add_fusion.refs_0_), channel_id=1, source_target_pairs={{0,18},{1,19},{2,16},{3,17},{4,22},{5,23},{6,20},{7,21},{8,26},{9,... | collective-permute-start | bytes 196616 | tf_op jit(solution)/shard_map/ppermute | solution.py:356
  22.5 1.5 %collective-permute-start.7 = (f32[32,512]{1,0:T(8,128)S(1)}, f32[32,512]{1,0:T(8,128)S(1)}, u32[]{:S(2)}, u32[]{:S(2)}) collective-permute-start(f32[32,512]{1,0:T(8,128)S(1)} %add_add_fusion.refs_0_), channel_id=1, source_target_pairs={{0,16},{1,17},{2,18},{3,19},{4,20},{5,21},{6,22},{7,23},{8,24},{9,... | collective-permute-start | bytes 196616 | tf_op jit(solution)/shard_map/ppermute | solution.py:356
  24.0 0.5 %collective-permute-start.6 = (f32[32,512]{1,0:T(8,128)S(1)}, f32[32,512]{1,0:T(8,128)S(1)}, u32[]{:S(2)}, u32[]{:S(2)}) collective-permute-start(f32[32,512]{1,0:T(8,128)S(1)} %add_add_fusion.refs_0_), channel_id=1, source_target_pairs={{0,2},{1,3},{2,0},{3,1},{4,6},{5,7},{6,4},{7,5},{8,10},{9,11},{10,... | collective-permute-start | bytes 196616 | tf_op jit(solution)/shard_map/ppermute | solution.py:356
  24.5 0.0 collective-permute-start.9
  24.5 13.3 %collective-permute-done.8.refs_3_ = f32[32,512]{1,0:T(8,128)S(1)} collective-permute-done((f32[32,512]{1,0:T(8,128)S(1)}, f32[32,512]{1,0:T(8,128)S(1)}, u32[]{:S(2)}, u32[]{:S(2)}) %collective-permute-start.8) | collective-permute-done | bytes 65568 | tf_op jit(solution)/shard_map/ppermute | solution.py:356
  37.8 0.0 collective-permute-start.12
  37.8 0.5 %collective-permute-start.11 = (f32[32,512]{1,0:T(8,128)S(1)}, f32[32,512]{1,0:T(8,128)S(1)}, u32[]{:S(2)}, u32[]{:S(2)}) collective-permute-start(f32[32,512]{1,0:T(8,128)S(1)} %collective-permute-done.7.refs_2_), channel_id=1, source_target_pairs={{0,1},{1,0},{2,3},{3,2},{4,5},{5,4},{6,7},{7,6},{8,9},{9,8},{10,11... | collective-permute-start | bytes 196616 | tf_op jit(solution)/shard_map/ppermute | solution.py:356
  38.3 0.1 collective-permute-start.10
  38.4 3.9 %solve_near.1 = (f32[128,128]{1,0:T(8,128)S(1)}, f32[128,512]{1,0:T(8,128)S(1)}, f32[8,512]{1,0:T(8,128)S(1)}) custom-call(f32[32,512]{1,0:T(8,128)S(1)} %add_add_fusion.refs_0_, f32[32,512]{1,0:T(8,128)S(1)} %collective-permute-done.6.refs_1_, f32[32,512]{1,0:T(8,128)S(1)} %collective-permute-done.7.refs_2_, f32[32,512]{1,0:T(8,128)S(1)} %collective-permute-done.8.refs_3_, ...), custom_call_target="tpu_custom_call" | custom-call | flops 3000000000 | bytes 1 | tf_op jit(solution)/shard_map/solve_near/pallas_call | solution.py:219
  42.3 5.4 %solve.1.weights = f32[128,256]{1,0:T(8,128)S(1)} custom-call(f32[32,512]{1,0:T(8,128)S(1)} %add_add_fusion.refs_0_, f32[32,512]{1,0:T(8,128)S(1)} %collective-permute-done.6.refs_1_, f32[32,512]{1,0:T(8,128)S(1)} %collective-permute-done.7.refs_2_, f32[32,512]{1,0:T(8,128)S(1)} %collective-permute-done.8.refs_3_, ...), custom_call_target="tpu_custom_call" | custom-call | flops 3000000000 | bytes 1 | tf_op jit(solution)/shard_map/solve/pallas_call | solution.py:290
  47.7 1.8 %update.1 = f32[128,2048]{1,0:T(8,128)} custom-call(f32[128,256]{1,0:T(8,128)S(1)} %solve.1.weights, f32[128,2048]{1,0:T(8,128)S(1)} %copy-done, f32[128,768]{1,0:T(8,128)S(1)} %collective-permute-done.5.refs_0_, f32[128,1280]{1,0:T(8,128)S(1)} %collective-permute-done.13.refs_1_), custom_call_target="tpu_custom_call" | custom-call | flops 134217728 | bytes 3145728 | tf_op jit(solution)/shard_map/update/pallas_call | solution.py:334
  (25 shorter events, 0.2 us)
Async XLA Ops:
  0.0 7.6 %copy-start = (f32[128,2048]{1,0:T(8,128)S(1)}, f32[128,2048]{1,0:T(8,128)}, u32[]{:S(2)}) copy-start(f32[128,2048]{1,0:T(8,128)} %own_ens.1) | copy-start | bytes 3145732
  0.0 14.7 %copy-start.4 = (s32[512]{0:T(512)S(1)}, s32[512]{0:T(512)}, u32[]{:S(2)}) copy-start(s32[512]{0:T(512)} %param.11) | copy-start | bytes 6148
  0.0 14.7 %copy-start.3 = (f32[16384]{0:T(1024)S(1)}, f32[16384]{0:T(1024)}, u32[]{:S(2)}) copy-start(f32[16384]{0:T(1024)} %param.10) | copy-start | bytes 196612
  0.0 14.7 %copy-start.2 = (f32[16384]{0:T(1024)S(1)}, f32[16384]{0:T(1024)}, u32[]{:S(2)}) copy-start(f32[16384]{0:T(1024)} %param.9) | copy-start | bytes 196612
  0.0 14.7 %copy-start.1 = (f32[128,512]{1,0:T(8,128)S(1)}, f32[128,512]{1,0:T(8,128)}, u32[]{:S(2)}) copy-start(f32[128,512]{1,0:T(8,128)} %noise.1) | copy-start | bytes 786436
  3.1 1.5 %collective-permute-start = (f32[64,512]{1,0:T(8,128)S(1)}, f32[64,512]{1,0:T(8,128)S(1)}, u32[]{:S(2)}, u32[]{:S(2)}) collective-permute-start(f32[64,512]{1,0:T(8,128)S(1)} %get-tuple-element.21), channel_id=1, source_target_pairs={{0,1},{1,0},{2,3},{3,2},{4,5},{5,4},{6,7},{7,6},{8,9},{9,8},{10,11... | collective-permute-start | bytes 393224 | tf_op jit(solution)/shard_map/ppermute | solution.py:356
  4.7 5.3 %collective-permute-start.1 = (f32[32,512]{1,0:T(8,128)S(1)}, f32[32,512]{1,0:T(8,128)S(1)}, u32[]{:S(2)}, u32[]{:S(2)}) collective-permute-start(f32[32,512]{1,0:T(8,128)S(1)} %constant_dynamic-slice_fusion), channel_id=1, source_target_pairs={{0,2},{1,3},{2,0},{3,1},{4,6},{5,7},{6,4},{7,5},{8,10},{9,11},{10,... | collective-permute-start | bytes 196616 | tf_op jit(solution)/shard_map/ppermute | solution.py:356
  7.6 11.8 %collective-permute-start.5 = (f32[128,768]{1,0:T(8,128)S(1)}, f32[128,768]{1,0:T(8,128)S(1)}, u32[]{:S(2)}, u32[]{:S(2)}) collective-permute-start(f32[128,768]{1,0:T(8,128)S(1)} %slice.6), channel_id=1, source_target_pairs={{0,16},{1,17},{2,18},{3,19},{4,20},{5,21},{6,22},{7,23},{8,24},{9,... | collective-permute-start | bytes 1179656 | tf_op jit(solution)/shard_map/ppermute | solution.py:356
  10.0 6.7 %collective-permute-start.4 = (f32[32,512]{1,0:T(8,128)S(1)}, f32[32,512]{1,0:T(8,128)S(1)}, u32[]{:S(2)}, u32[]{:S(2)}) collective-permute-start(f32[32,512]{1,0:T(8,128)S(1)} %dynamic-slice_add_fusion), channel_id=1, source_target_pairs={{0,12},{1,13},{2,14},{3,15},{4,8},{5,9},{6,10},{7,11},{8,4},{9,5},... | collective-permute-start | bytes 196616 | tf_op jit(solution)/shard_map/ppermute | solution.py:356
  14.1 5.4 %collective-permute-start.3 = (f32[32,512]{1,0:T(8,128)S(1)}, f32[32,512]{1,0:T(8,128)S(1)}, u32[]{:S(2)}, u32[]{:S(2)}) collective-permute-start(f32[32,512]{1,0:T(8,128)S(1)} %dynamic-slice_add_fusion), channel_id=1, source_target_pairs={{0,8},{1,9},{2,10},{3,11},{4,12},{5,13},{6,14},{7,15},{8,0},{9,1},... | collective-permute-start | bytes 196616 | tf_op jit(solution)/shard_map/ppermute | solution.py:356
  14.1 5.4 %collective-permute-start.2 = (f32[32,512]{1,0:T(8,128)S(1)}, f32[32,512]{1,0:T(8,128)S(1)}, u32[]{:S(2)}, u32[]{:S(2)}) collective-permute-start(f32[32,512]{1,0:T(8,128)S(1)} %dynamic-slice_add_fusion), channel_id=1, source_target_pairs={{0,4},{1,5},{2,6},{3,7},{4,0},{5,1},{6,2},{7,3},{8,12},{9,13},{10,... | collective-permute-start | bytes 196616 | tf_op jit(solution)/shard_map/ppermute | solution.py:356
  19.5 28.2 %collective-permute-start.13 = (f32[128,1280]{1,0:T(8,128)S(1)}, f32[128,1280]{1,0:T(8,128)S(1)}, u32[]{:S(2)}, u32[]{:S(2)}) collective-permute-start(f32[128,1280]{1,0:T(8,128)S(1)} %slice.7), channel_id=1, source_target_pairs={{0,16},{1,17},{2,18},{3,19},{4,20},{5,21},{6,22},{7,23},{8,24},{9,... | collective-permute-start | bytes 1966088 | tf_op jit(solution)/shard_map/ppermute | solution.py:356
  21.0 16.8 %collective-permute-start.8 = (f32[32,512]{1,0:T(8,128)S(1)}, f32[32,512]{1,0:T(8,128)S(1)}, u32[]{:S(2)}, u32[]{:S(2)}) collective-permute-start(f32[32,512]{1,0:T(8,128)S(1)} %add_add_fusion.refs_0_), channel_id=1, source_target_pairs={{0,18},{1,19},{2,16},{3,17},{4,22},{5,23},{6,20},{7,21},{8,26},{9,... | collective-permute-start | bytes 196616 | tf_op jit(solution)/shard_map/ppermute | solution.py:356
  22.5 15.3 %collective-permute-start.7 = (f32[32,512]{1,0:T(8,128)S(1)}, f32[32,512]{1,0:T(8,128)S(1)}, u32[]{:S(2)}, u32[]{:S(2)}) collective-permute-start(f32[32,512]{1,0:T(8,128)S(1)} %add_add_fusion.refs_0_), channel_id=1, source_target_pairs={{0,16},{1,17},{2,18},{3,19},{4,20},{5,21},{6,22},{7,23},{8,24},{9,... | collective-permute-start | bytes 196616 | tf_op jit(solution)/shard_map/ppermute | solution.py:356
  24.0 14.3 %collective-permute-start.6 = (f32[32,512]{1,0:T(8,128)S(1)}, f32[32,512]{1,0:T(8,128)S(1)}, u32[]{:S(2)}, u32[]{:S(2)}) collective-permute-start(f32[32,512]{1,0:T(8,128)S(1)} %add_add_fusion.refs_0_), channel_id=1, source_target_pairs={{0,2},{1,3},{2,0},{3,1},{4,6},{5,7},{6,4},{7,5},{8,10},{9,11},{10,... | collective-permute-start | bytes 196616 | tf_op jit(solution)/shard_map/ppermute | solution.py:356
  24.5 17.8 %collective-permute-start.9 = (f32[32,512]{1,0:T(8,128)S(1)}, f32[32,512]{1,0:T(8,128)S(1)}, u32[]{:S(2)}, u32[]{:S(2)}) collective-permute-start(f32[32,512]{1,0:T(8,128)S(1)} %add_add_fusion.refs_0_), channel_id=1, source_target_pairs={{0,1},{1,0},{2,3},{3,2},{4,5},{5,4},{6,7},{7,6},{8,9},{9,8},{10,11... | collective-permute-start | bytes 196616 | tf_op jit(solution)/shard_map/ppermute | solution.py:356
  37.8 4.5 %collective-permute-start.12 = (f32[32,512]{1,0:T(8,128)S(1)}, f32[32,512]{1,0:T(8,128)S(1)}, u32[]{:S(2)}, u32[]{:S(2)}) collective-permute-start(f32[32,512]{1,0:T(8,128)S(1)} %collective-permute-done.8.refs_3_), channel_id=1, source_target_pairs={{0,1},{1,0},{2,3},{3,2},{4,5},{5,4},{6,7},{7,6},{8,9},{9,8},{10,11... | collective-permute-start | bytes 196616 | tf_op jit(solution)/shard_map/ppermute | solution.py:356
  37.8 4.5 %collective-permute-start.11 = (f32[32,512]{1,0:T(8,128)S(1)}, f32[32,512]{1,0:T(8,128)S(1)}, u32[]{:S(2)}, u32[]{:S(2)}) collective-permute-start(f32[32,512]{1,0:T(8,128)S(1)} %collective-permute-done.7.refs_2_), channel_id=1, source_target_pairs={{0,1},{1,0},{2,3},{3,2},{4,5},{5,4},{6,7},{7,6},{8,9},{9,8},{10,11... | collective-permute-start | bytes 196616 | tf_op jit(solution)/shard_map/ppermute | solution.py:356
  38.3 4.0 %collective-permute-start.10 = (f32[32,512]{1,0:T(8,128)S(1)}, f32[32,512]{1,0:T(8,128)S(1)}, u32[]{:S(2)}, u32[]{:S(2)}) collective-permute-start(f32[32,512]{1,0:T(8,128)S(1)} %collective-permute-done.6.refs_1_), channel_id=1, source_target_pairs={{0,1},{1,0},{2,3},{3,2},{4,5},{5,4},{6,7},{7,6},{8,9},{9,8},{10,11... | collective-permute-start | bytes 196616 | tf_op jit(solution)/shard_map/ppermute | solution.py:356

commit v6 on v5

--- a/solution.py
+++ b/solution.py
@@ -13,7 +13,8 @@
 VMEM = pl.BlockSpec(memory_space=pltpu.VMEM)
 HBM = pl.BlockSpec(memory_space=pltpu.HBM)
 VMEM_LIMIT = 20 << 20
-PARTS, EARLY = 8, 3
+PARTS = 8
+CUTS = (0, 1, 4, 8)
 
 
 def dot(a, b, dims, precision=HIGHEST):
@@ -222,7 +223,7 @@
         in_specs=[VMEM] * (len(pieces) + 1),
         out_specs=(VMEM, VMEM, VMEM),
         scratch_shapes=solve_scratch(size),
-        cost_estimate=pl.CostEstimate(flops=3_000_000_000, bytes_accessed=1, transcendentals=0),
+        cost_estimate=pl.CostEstimate(flops=5_000_000_000, bytes_accessed=1, transcendentals=0),
         compiler_params=pltpu.CompilerParams(vmem_limit_bytes=VMEM_LIMIT),
         name="solve_near",
     )(*pieces, root)
@@ -300,49 +301,48 @@
             pltpu.VMEM((2 * size, size + 2 * own), f32),
             pltpu.VMEM((2 * size, own), f32),
         ],
-        cost_estimate=pl.CostEstimate(flops=3_000_000_000, bytes_accessed=1, transcendentals=0),
+        cost_estimate=pl.CostEstimate(flops=5_000_000_000, bytes_accessed=1, transcendentals=0),
         compiler_params=pltpu.CompilerParams(vmem_limit_bytes=VMEM_LIMIT),
         name="solve",
     )(*pieces, inverse, near, shift, target, root)
 
 
-def update_kernel(fars, weights, own_ens, *refs):
-    halves = refs[: 2 * fars]
-    out, buf, sems = refs[2 * fars :]
+def update_kernel(weights, own_ens, *refs):
+    parts = len(CUTS) - 1
+    others, (out, buf, sems) = refs[:-3], refs[-3:]
     own, params = own_ens.shape
-    steps = sems.shape[0]
-    width = params // steps
+    width = params // PARTS
     copies = []
-    for i in range(steps):
-        cols = slice(i * width, (i + 1) * width)
-        half, at = (0, i) if i * width < halves[0].shape[1] else (1, i - halves[0].shape[1] // width)
-        part = own_ens[:, cols]
-        total = part + dot3(weights[:, :own], part, ((1,), (0,)))
-        for far in range(fars):
-            w = weights[:, (far + 1) * own : (far + 2) * own]
-            total = total + dot3(w, halves[2 * far + half][:, at * width : (at + 1) * width], ((1,), (0,)))
-        buf[:, cols] = total
-        copies.append(pltpu.make_async_copy(buf.at[:, cols], out.at[:, cols], sems.at[i]))
-        copies[-1].start()
+    for part in range(parts):
+        for i in range(CUTS[part], CUTS[part + 1]):
+            cols = slice(i * width, (i + 1) * width)
+            at = slice((i - CUTS[part]) * width, (i - CUTS[part] + 1) * width)
+            total = own_ens[:, cols]
+            total = total + dot3(weights[:, :own], total, ((1,), (0,)))
+            for far in range(1, len(others) // parts + 1):
+                w = weights[:, far * own : (far + 1) * own]
+                total = total + dot3(w, others[(far - 1) * parts + part][:, at], ((1,), (0,)))
+            buf[:, cols] = total
+            copies.append(pltpu.make_async_copy(buf.at[:, cols], out.at[:, cols], sems.at[i]))
+            copies[-1].start()
     for copy in copies:
         copy.wait()
 
 
-def update(weights, own_ens, halves):
+def update(weights, own_ens, others):
     own, params = own_ens.shape
-    steps = PARTS
-    return pl.pallas_call(
-        functools.partial(update_kernel, len(halves) // 2),
+    return pl.pallas_call(
+        update_kernel,
         out_shape=jax.ShapeDtypeStruct((own, params), f32),
-        in_specs=[VMEM] * (2 + len(halves)),
+        in_specs=[VMEM] * (2 + len(others)),
         out_specs=HBM,
-        scratch_shapes=[pltpu.VMEM((own, params), f32), pltpu.SemaphoreType.DMA((steps,))],
+        scratch_shapes=[pltpu.VMEM((own, params), f32), pltpu.SemaphoreType.DMA((PARTS,))],
         cost_estimate=pl.CostEstimate(
             flops=2 * own * weights.shape[1] * params, bytes_accessed=4 * params * (own + weights.shape[1]), transcendentals=0
         ),
         compiler_params=pltpu.CompilerParams(vmem_limit_bytes=VMEM_LIMIT),
         name="update",
-    )(weights, own_ens, *halves)
+    )(weights, own_ens, *others)
 
 
 def per_device(n_mem, n_par, operator, ensemble, noise, observations, variances, rows):
@@ -355,32 +355,34 @@
         ]
         return lax.ppermute(x, ("mem", "par"), pairs)
 
-    mid = ensemble.shape[1] // PARTS * EARLY
-    early = [swap(ensemble[:, :mid], far, 0) for far in range(1, n_mem)]
+    width = ensemble.shape[1] // PARTS
+    first, second, third = (ensemble[:, width * i : width * k] for i, k in zip(CUTS, CUTS[1:]))
+    first = [swap(first, far, 0) for far in range(1, n_mem)]
+    second = [swap(second, far, 0) for far in range(1, n_mem)]
     keep, send = forward(ensemble, operator)
     part = keep + swap(send, 0, 1)
     size = part.shape[0] // 2
-    total = lax.dynamic_slice_in_dim(part, side * size, size, 0) + swap(
-        lax.dynamic_slice_in_dim(part, (1 - side) * size, size, 0), 0, 2
-    )
+    other = swap(lax.dynamic_slice_in_dim(part, (1 - side) * size, size, 0), 0, 2)
+    other, first = lax.optimization_barrier((other, first))
+    total = lax.dynamic_slice_in_dim(part, side * size, size, 0) + other
     target, root = lookup(rows, observations, variances, noise)
     stride = 4
     while stride < n_par:
         ways = min(4, n_par // stride)
         terms = [total] + [swap(total, 0, d * stride) for d in range(1, ways)]
         if stride == 4:
-            terms, target, root, early = lax.optimization_barrier((terms, target, root, early))
+            terms, target, root, second = lax.optimization_barrier((terms, target, root, second))
         total = add_all(terms)
         stride *= ways
     places = [(far, dy, 0) for far in range(n_mem) for dy in range(2)]
     pieces = [total if (far, dy) == (0, 0) else swap(total, far, 2 * dy) for far, dy, _ in places]
-    rest, _ = lax.optimization_barrier((ensemble[:, mid:], total))
-    late = [swap(rest, far, 0) for far in range(1, n_mem)]
+    third, _ = lax.optimization_barrier((third, total))
+    third = [swap(third, far, 0) for far in range(1, n_mem)]
     inverse, near, shift = solve_near(pieces, root, ensemble.shape[0] * n_mem)
     pieces += [swap(piece, 0, 1) for piece in pieces]
     places += [(far, dy, 1) for far, dy, _ in places]
     weights = solve(pieces, places, inverse, near, shift, target, root)
-    return update(weights, ensemble, [half for pair in zip(early, late) for half in pair])
+    return update(weights, ensemble, [part for far in zip(first, second, third) for part in far])
 
 
 def solution(mesh):

time: 49.6 us -> 39.9 us (0.80)
  waiting for transfers between devices: 19.1 us -> 8.85 us
  starting transfers between devices: 15.3 us -> 15.9 us
    ppermute x14 -> x15, waiting for transfers between devices: 19.1 us -> 8.85 us  [swap(): return lax.ppermute(x, ('mem', 'par'), pairs)]
    ppermute x14 -> x15, starting transfers between devices: 15.3 us -> 15.9 us  [swap(): return lax.ppermute(x, ('mem', 'par'), pairs)]
  transfers between devices with their start and end apart: 14 -> 15, of which waited for: 5 -> 9; matrix products, arithmetic and copies ran while one was open for 0% -> 0% of each run, Pallas kernels for 20% -> 25%
where the time goes in v6:
time: 39.9 us; the launch traced here: 39.8 us
  starting transfers between devices  15.9 us (40%)
  Pallas kernels  14.8 us (37%)
  waiting for transfers between devices  8.85 us (22%)
    ppermute x15, starting transfers between devices, swap(): return lax.ppermute(x, ('mem', 'par'), pairs)  15.9 us
    ppermute x15, waiting for transfers between devices, swap(): return lax.ppermute(x, ('mem', 'par'), pairs)  8.85 us
    pallas_call x1, Pallas kernels, solve(): pl.pallas_call(functools.partial(solve_kernel, places), out_shape=jax.Sha...  5.35 us
    pallas_call x1, Pallas kernels, solve_near(): pl.pallas_call(functools.partial(near_kernel, members, len(pieces)), out_...  3.87 us
    pallas_call x1, Pallas kernels, forward(): pl.pallas_call(functools.partial(forward_kernel, steps), out_shape=(half,...  3.1 us
    pallas_call x1, Pallas kernels, update(): pl.pallas_call(update_kernel, out_shape=jax.ShapeDtypeStruct((own, params...  1.78 us
  transfers between devices with their start and end apart: 15, of which 9 were waited for; matrix products, arithmetic and copies ran while one was open for 0% of the time, Pallas kernels for 25%

profile of v6, /device:TPU:0, one launch (start us, length us, event | category | flops | bytes accessed | tf_op | source)
XLA Modules:
  0.0 39.8 jit_solution(1234261220439784680)
XLA Ops:
  0.0 3.1 %forward.1 = (f32[64,512]{1,0:T(8,128)S(1)}, f32[64,512]{1,0:T(8,128)S(1)}) custom-call(f32[128,2048]{1,0:T(8,128)} %own_ens.1, f32[2048,512]{1,0:T(8,128)} %op.1), custom_call_target="tpu_custom_call" | custom-call | flops 268435456 | bytes 5242880 | tf_op jit(solution)/shard_map/forward/pallas_call | solution.py:135
  3.1 0.5 %collective-permute-start = (f32[64,512]{1,0:T(8,128)S(1)}, f32[64,512]{1,0:T(8,128)S(1)}, u32[]{:S(2)}, u32[]{:S(2)}) collective-permute-start(f32[64,512]{1,0:T(8,128)S(1)} %get-tuple-element.23), channel_id=1, source_target_pairs={{0,1},{1,0},{2,3},{3,2},{4,5},{5,4},{6,7},{7,6},{8,9},{9,8},{10,11... | collective-permute-start | bytes 393224 | tf_op jit(solution)/shard_map/ppermute | solution.py:356
  3.7 2.6 %collective-permute-start.2 = (f32[128,256]{1,0:T(8,128)S(1)}, f32[128,256]{1,0:T(8,128)S(1)}, u32[]{:S(2)}, u32[]{:S(2)}) collective-permute-start(f32[128,256]{1,0:T(8,128)S(1)} %slice.9), channel_id=1, source_target_pairs={{0,16},{1,17},{2,18},{3,19},{4,20},{5,21},{6,22},{7,23},{8,24},{9,... | collective-permute-start | bytes 393224 | tf_op jit(solution)/shard_map/ppermute | solution.py:356
  6.3 1.6 %collective-permute-start.1 = (f32[32,512]{1,0:T(8,128)S(1)}, f32[32,512]{1,0:T(8,128)S(1)}, u32[]{:S(2)}, u32[]{:S(2)}) collective-permute-start(f32[32,512]{1,0:T(8,128)S(1)} %constant_dynamic-slice_fusion), channel_id=1, source_target_pairs={{0,2},{1,3},{2,0},{3,1},{4,6},{5,7},{6,4},{7,5},{8,10},{9,11},{10,... | collective-permute-start | bytes 196616 | tf_op jit(solution)/shard_map/ppermute | solution.py:356
  7.9 1.3 %collective-permute-start.6 = (f32[128,768]{1,0:T(8,128)S(1)}, f32[128,768]{1,0:T(8,128)S(1)}, u32[]{:S(2)}, u32[]{:S(2)}) collective-permute-start(f32[128,768]{1,0:T(8,128)S(1)} %slice.10), channel_id=1, source_target_pairs={{0,16},{1,17},{2,18},{3,19},{4,20},{5,21},{6,22},{7,23},{8,24},{9,... | collective-permute-start | bytes 1179656 | tf_op jit(solution)/shard_map/ppermute | solution.py:356
  9.2 1.2 %collective-permute-done.2.refs_0_ = f32[128,256]{1,0:T(8,128)S(1)} collective-permute-done((f32[128,256]{1,0:T(8,128)S(1)}, f32[128,256]{1,0:T(8,128)S(1)}, u32[]{:S(2)}, u32[]{:S(2)}) %collective-permute-start.2) | collective-permute-done | bytes 131104 | tf_op jit(solution)/shard_map/ppermute | solution.py:356
  10.4 0.2 collective-permute-done.1
  10.6 3.8 %collective-permute-start.5 = (f32[32,512]{1,0:T(8,128)S(1)}, f32[32,512]{1,0:T(8,128)S(1)}, u32[]{:S(2)}, u32[]{:S(2)}) collective-permute-start(f32[32,512]{1,0:T(8,128)S(1)} %dynamic-slice_add_fusion), channel_id=1, source_target_pairs={{0,12},{1,13},{2,14},{3,15},{4,8},{5,9},{6,10},{7,11},{8,4},{9,5},... | collective-permute-start | bytes 196616 | tf_op jit(solution)/shard_map/ppermute | solution.py:356
  14.4 0.7 %collective-permute-start.3 = (f32[32,512]{1,0:T(8,128)S(1)}, f32[32,512]{1,0:T(8,128)S(1)}, u32[]{:S(2)}, u32[]{:S(2)}) collective-permute-start(f32[32,512]{1,0:T(8,128)S(1)} %dynamic-slice_add_fusion), channel_id=1, source_target_pairs={{0,4},{1,5},{2,6},{3,7},{4,0},{5,1},{6,2},{7,3},{8,12},{9,13},{10,... | collective-permute-start | bytes 196616 | tf_op jit(solution)/shard_map/ppermute | solution.py:356
  15.1 0.7 %lookup.1 = (f32[128,512]{1,0:T(8,128)S(1)}, f32[8,512]{1,0:T(8,128)S(1)}) custom-call(s32[1,512]{1,0:T(1,128)S(1)} %bitcast.5, f32[128,128]{1,0:T(8,128)S(1)} %bitcast.3, f32[128,128]{1,0:T(8,128)S(1)} %bitcast.4, f32[128,512]{1,0:T(8,128)S(1)} %copy-done.1), custom_call_target="tpu_custom_call" | custom-call | flops 25769803776 | bytes 1048576 | tf_op jit(solution)/shard_map/lookup/pallas_call | solution.py:170
  15.8 1.6 %collective-permute-done.5 = f32[32,512]{1,0:T(8,128)S(1)} collective-permute-done((f32[32,512]{1,0:T(8,128)S(1)}, f32[32,512]{1,0:T(8,128)S(1)}, u32[]{:S(2)}, u32[]{:S(2)}) %collective-permute-start.5) | collective-permute-done | bytes 65568 | tf_op jit(solution)/shard_map/ppermute | solution.py:356
  17.4 2.5 %collective-permute-done.4 = f32[32,512]{1,0:T(8,128)S(1)} collective-permute-done((f32[32,512]{1,0:T(8,128)S(1)}, f32[32,512]{1,0:T(8,128)S(1)}, u32[]{:S(2)}, u32[]{:S(2)}) %collective-permute-start.4) | collective-permute-done | bytes 65568 | tf_op jit(solution)/shard_map/ppermute | solution.py:356
  19.9 2.6 %collective-permute-start.9 = (f32[32,512]{1,0:T(8,128)S(1)}, f32[32,512]{1,0:T(8,128)S(1)}, u32[]{:S(2)}, u32[]{:S(2)}) collective-permute-start(f32[32,512]{1,0:T(8,128)S(1)} %add_add_fusion.refs_0_), channel_id=1, source_target_pairs={{0,18},{1,19},{2,16},{3,17},{4,22},{5,23},{6,20},{7,21},{8,26},{9,... | collective-permute-start | bytes 196616 | tf_op jit(solution)/shard_map/ppermute | solution.py:356
  22.5 0.5 %collective-permute-start.8 = (f32[32,512]{1,0:T(8,128)S(1)}, f32[32,512]{1,0:T(8,128)S(1)}, u32[]{:S(2)}, u32[]{:S(2)}) collective-permute-start(f32[32,512]{1,0:T(8,128)S(1)} %add_add_fusion.refs_0_), channel_id=1, source_target_pairs={{0,16},{1,17},{2,18},{3,19},{4,20},{5,21},{6,22},{7,23},{8,24},{9,... | collective-permute-start | bytes 196616 | tf_op jit(solution)/shard_map/ppermute | solution.py:356
  23.0 0.5 %collective-permute-start.7 = (f32[32,512]{1,0:T(8,128)S(1)}, f32[32,512]{1,0:T(8,128)S(1)}, u32[]{:S(2)}, u32[]{:S(2)}) collective-permute-start(f32[32,512]{1,0:T(8,128)S(1)} %add_add_fusion.refs_0_), channel_id=1, source_target_pairs={{0,2},{1,3},{2,0},{3,1},{4,6},{5,7},{6,4},{7,5},{8,10},{9,11},{10,... | collective-permute-start | bytes 196616 | tf_op jit(solution)/shard_map/ppermute | solution.py:356
  23.6 1.6 %collective-permute-start.14 = (f32[128,1024]{1,0:T(8,128)S(1)}, f32[128,1024]{1,0:T(8,128)S(1)}, u32[]{:S(2)}, u32[]{:S(2)}) collective-permute-start(f32[128,1024]{1,0:T(8,128)S(1)} %slice.11), channel_id=1, source_target_pairs={{0,16},{1,17},{2,18},{3,19},{4,20},{5,21},{6,22},{7,23},{8,24},{9,... | collective-permute-start | bytes 1572872 | tf_op jit(solution)/shard_map/ppermute | solution.py:356
  25.3 0.1 collective-permute-start.13
  25.4 1.5 %collective-permute-done.8.refs_2_ = f32[32,512]{1,0:T(8,128)S(1)} collective-permute-done((f32[32,512]{1,0:T(8,128)S(1)}, f32[32,512]{1,0:T(8,128)S(1)}, u32[]{:S(2)}, u32[]{:S(2)}) %collective-permute-start.8) | collective-permute-done | bytes 65568 | tf_op jit(solution)/shard_map/ppermute | solution.py:356
  26.9 0.4 %collective-permute-done.7.refs_1_ = f32[32,512]{1,0:T(8,128)S(1)} collective-permute-done((f32[32,512]{1,0:T(8,128)S(1)}, f32[32,512]{1,0:T(8,128)S(1)}, u32[]{:S(2)}, u32[]{:S(2)}) %collective-permute-start.7) | collective-permute-done | bytes 65568 | tf_op jit(solution)/shard_map/ppermute | solution.py:356
  27.3 0.1 collective-permute-start.11
  27.4 3.9 %solve_near.1 = (f32[128,128]{1,0:T(8,128)S(1)}, f32[128,512]{1,0:T(8,128)S(1)}, f32[8,512]{1,0:T(8,128)S(1)}) custom-call(f32[32,512]{1,0:T(8,128)S(1)} %add_add_fusion.refs_0_, f32[32,512]{1,0:T(8,128)S(1)} %collective-permute-done.7.refs_1_, f32[32,512]{1,0:T(8,128)S(1)} %collective-permute-done.8.refs_2_, f32[32,512]{1,0:T(8,128)S(1)} %collective-permute-done.9.refs_3_, ...), custom_call_target="tpu_custom_call" | custom-call | flops 5000000000 | bytes 1 | tf_op jit(solution)/shard_map/solve_near/pallas_call | solution.py:220
  31.3 5.4 %solve.1.weights = f32[128,256]{1,0:T(8,128)S(1)} custom-call(f32[32,512]{1,0:T(8,128)S(1)} %add_add_fusion.refs_0_, f32[32,512]{1,0:T(8,128)S(1)} %collective-permute-done.7.refs_1_, f32[32,512]{1,0:T(8,128)S(1)} %collective-permute-done.8.refs_2_, f32[32,512]{1,0:T(8,128)S(1)} %collective-permute-done.9.refs_3_, ...), custom_call_target="tpu_custom_call" | custom-call | flops 5000000000 | bytes 1 | tf_op jit(solution)/shard_map/solve/pallas_call | solution.py:291
  36.7 1.3 %collective-permute-done.14.refs_2_ = f32[128,1024]{1,0:T(8,128)S(1)} collective-permute-done((f32[128,1024]{1,0:T(8,128)S(1)}, f32[128,1024]{1,0:T(8,128)S(1)}, u32[]{:S(2)}, u32[]{:S(2)}) %collective-permute-start.14) | collective-permute-done | bytes 524320 | tf_op jit(solution)/shard_map/ppermute | solution.py:356
  38.0 1.8 %update.1 = f32[128,2048]{1,0:T(8,128)} custom-call(f32[128,256]{1,0:T(8,128)S(1)} %solve.1.weights, f32[128,2048]{1,0:T(8,128)S(1)} %copy-done, f32[128,256]{1,0:T(8,128)S(1)} %collective-permute-done.2.refs_0_, f32[128,768]{1,0:T(8,128)S(1)} %collective-permute-done.6.refs_1_, f32[128,1024]{1,0:T(8,128)S(1)} %collective-permute-done.14.refs_2_), custom_call_target="tpu_custom_call" | custom-call | flops 134217728 | bytes 3145728 | tf_op jit(solution)/shard_map/update/pallas_call | solution.py:334
  (28 shorter events, 0.4 us)
Async XLA Ops:
  0.0 3.7 %copy-start = (f32[128,2048]{1,0:T(8,128)S(1)}, f32[128,2048]{1,0:T(8,128)}, u32[]{:S(2)}) copy-start(f32[128,2048]{1,0:T(8,128)} %own_ens.1) | copy-start | bytes 3145732
  0.0 15.1 %copy-start.4 = (s32[512]{0:T(512)S(1)}, s32[512]{0:T(512)}, u32[]{:S(2)}) copy-start(s32[512]{0:T(512)} %param.11) | copy-start | bytes 6148
  0.0 15.1 %copy-start.3 = (f32[16384]{0:T(1024)S(1)}, f32[16384]{0:T(1024)}, u32[]{:S(2)}) copy-start(f32[16384]{0:T(1024)} %param.10) | copy-start | bytes 196612
  0.0 15.1 %copy-start.2 = (f32[16384]{0:T(1024)S(1)}, f32[16384]{0:T(1024)}, u32[]{:S(2)}) copy-start(f32[16384]{0:T(1024)} %param.9) | copy-start | bytes 196612
  0.0 15.1 %copy-start.1 = (f32[128,512]{1,0:T(8,128)S(1)}, f32[128,512]{1,0:T(8,128)}, u32[]{:S(2)}) copy-start(f32[128,512]{1,0:T(8,128)} %noise.1) | copy-start | bytes 786436
  3.1 3.1 %collective-permute-start = (f32[64,512]{1,0:T(8,128)S(1)}, f32[64,512]{1,0:T(8,128)S(1)}, u32[]{:S(2)}, u32[]{:S(2)}) collective-permute-start(f32[64,512]{1,0:T(8,128)S(1)} %get-tuple-element.23), channel_id=1, source_target_pairs={{0,1},{1,0},{2,3},{3,2},{4,5},{5,4},{6,7},{7,6},{8,9},{9,8},{10,11... | collective-permute-start | bytes 393224 | tf_op jit(solution)/shard_map/ppermute | solution.py:356
  3.7 6.7 %collective-permute-start.2 = (f32[128,256]{1,0:T(8,128)S(1)}, f32[128,256]{1,0:T(8,128)S(1)}, u32[]{:S(2)}, u32[]{:S(2)}) collective-permute-start(f32[128,256]{1,0:T(8,128)S(1)} %slice.9), channel_id=1, source_target_pairs={{0,16},{1,17},{2,18},{3,19},{4,20},{5,21},{6,22},{7,23},{8,24},{9,... | collective-permute-start | bytes 393224 | tf_op jit(solution)/shard_map/ppermute | solution.py:356
  6.3 4.3 %collective-permute-start.1 = (f32[32,512]{1,0:T(8,128)S(1)}, f32[32,512]{1,0:T(8,128)S(1)}, u32[]{:S(2)}, u32[]{:S(2)}) collective-permute-start(f32[32,512]{1,0:T(8,128)S(1)} %constant_dynamic-slice_fusion), channel_id=1, source_target_pairs={{0,2},{1,3},{2,0},{3,1},{4,6},{5,7},{6,4},{7,5},{8,10},{9,11},{10,... | collective-permute-start | bytes 196616 | tf_op jit(solution)/shard_map/ppermute | solution.py:356
  7.9 12.0 %collective-permute-start.6 = (f32[128,768]{1,0:T(8,128)S(1)}, f32[128,768]{1,0:T(8,128)S(1)}, u32[]{:S(2)}, u32[]{:S(2)}) collective-permute-start(f32[128,768]{1,0:T(8,128)S(1)} %slice.10), channel_id=1, source_target_pairs={{0,16},{1,17},{2,18},{3,19},{4,20},{5,21},{6,22},{7,23},{8,24},{9,... | collective-permute-start | bytes 1179656 | tf_op jit(solution)/shard_map/ppermute | solution.py:356
  10.6 6.8 %collective-permute-start.5 = (f32[32,512]{1,0:T(8,128)S(1)}, f32[32,512]{1,0:T(8,128)S(1)}, u32[]{:S(2)}, u32[]{:S(2)}) collective-permute-start(f32[32,512]{1,0:T(8,128)S(1)} %dynamic-slice_add_fusion), channel_id=1, source_target_pairs={{0,12},{1,13},{2,14},{3,15},{4,8},{5,9},{6,10},{7,11},{8,4},{9,5},... | collective-permute-start | bytes 196616 | tf_op jit(solution)/shard_map/ppermute | solution.py:356
  14.4 5.4 %collective-permute-start.4 = (f32[32,512]{1,0:T(8,128)S(1)}, f32[32,512]{1,0:T(8,128)S(1)}, u32[]{:S(2)}, u32[]{:S(2)}) collective-permute-start(f32[32,512]{1,0:T(8,128)S(1)} %dynamic-slice_add_fusion), channel_id=1, source_target_pairs={{0,8},{1,9},{2,10},{3,11},{4,12},{5,13},{6,14},{7,15},{8,0},{9,1},... | collective-permute-start | bytes 196616 | tf_op jit(solution)/shard_map/ppermute | solution.py:356
  14.4 5.5 %collective-permute-start.3 = (f32[32,512]{1,0:T(8,128)S(1)}, f32[32,512]{1,0:T(8,128)S(1)}, u32[]{:S(2)}, u32[]{:S(2)}) collective-permute-start(f32[32,512]{1,0:T(8,128)S(1)} %dynamic-slice_add_fusion), channel_id=1, source_target_pairs={{0,4},{1,5},{2,6},{3,7},{4,0},{5,1},{6,2},{7,3},{8,12},{9,13},{10,... | collective-permute-start | bytes 196616 | tf_op jit(solution)/shard_map/ppermute | solution.py:356
  19.9 5.3 %collective-permute-start.9 = (f32[32,512]{1,0:T(8,128)S(1)}, f32[32,512]{1,0:T(8,128)S(1)}, u32[]{:S(2)}, u32[]{:S(2)}) collective-permute-start(f32[32,512]{1,0:T(8,128)S(1)} %add_add_fusion.refs_0_), channel_id=1, source_target_pairs={{0,18},{1,19},{2,16},{3,17},{4,22},{5,23},{6,20},{7,21},{8,26},{9,... | collective-permute-start | bytes 196616 | tf_op jit(solution)/shard_map/ppermute | solution.py:356
  22.5 4.4 %collective-permute-start.8 = (f32[32,512]{1,0:T(8,128)S(1)}, f32[32,512]{1,0:T(8,128)S(1)}, u32[]{:S(2)}, u32[]{:S(2)}) collective-permute-start(f32[32,512]{1,0:T(8,128)S(1)} %add_add_fusion.refs_0_), channel_id=1, source_target_pairs={{0,16},{1,17},{2,18},{3,19},{4,20},{5,21},{6,22},{7,23},{8,24},{9,... | collective-permute-start | bytes 196616 | tf_op jit(solution)/shard_map/ppermute | solution.py:356
  23.0 4.3 %collective-permute-start.7 = (f32[32,512]{1,0:T(8,128)S(1)}, f32[32,512]{1,0:T(8,128)S(1)}, u32[]{:S(2)}, u32[]{:S(2)}) collective-permute-start(f32[32,512]{1,0:T(8,128)S(1)} %add_add_fusion.refs_0_), channel_id=1, source_target_pairs={{0,2},{1,3},{2,0},{3,1},{4,6},{5,7},{6,4},{7,5},{8,10},{9,11},{10,... | collective-permute-start | bytes 196616 | tf_op jit(solution)/shard_map/ppermute | solution.py:356
  23.5 7.7 %collective-permute-start.10 = (f32[32,512]{1,0:T(8,128)S(1)}, f32[32,512]{1,0:T(8,128)S(1)}, u32[]{:S(2)}, u32[]{:S(2)}) collective-permute-start(f32[32,512]{1,0:T(8,128)S(1)} %add_add_fusion.refs_0_), channel_id=1, source_target_pairs={{0,1},{1,0},{2,3},{3,2},{4,5},{5,4},{6,7},{7,6},{8,9},{9,8},{10,11... | collective-permute-start | bytes 196616 | tf_op jit(solution)/shard_map/ppermute | solution.py:356
  23.6 14.4 %collective-permute-start.14 = (f32[128,1024]{1,0:T(8,128)S(1)}, f32[128,1024]{1,0:T(8,128)S(1)}, u32[]{:S(2)}, u32[]{:S(2)}) collective-permute-start(f32[128,1024]{1,0:T(8,128)S(1)} %slice.11), channel_id=1, source_target_pairs={{0,16},{1,17},{2,18},{3,19},{4,20},{5,21},{6,22},{7,23},{8,24},{9,... | collective-permute-start | bytes 1572872 | tf_op jit(solution)/shard_map/ppermute | solution.py:356
  25.3 6.0 %collective-permute-start.13 = (f32[32,512]{1,0:T(8,128)S(1)}, f32[32,512]{1,0:T(8,128)S(1)}, u32[]{:S(2)}, u32[]{:S(2)}) collective-permute-start(f32[32,512]{1,0:T(8,128)S(1)} %collective-permute-done.9.refs_3_), channel_id=1, source_target_pairs={{0,1},{1,0},{2,3},{3,2},{4,5},{5,4},{6,7},{7,6},{8,9},{9,8},{10,11... | collective-permute-start | bytes 196616 | tf_op jit(solution)/shard_map/ppermute | solution.py:356
  26.9 4.4 %collective-permute-start.12 = (f32[32,512]{1,0:T(8,128)S(1)}, f32[32,512]{1,0:T(8,128)S(1)}, u32[]{:S(2)}, u32[]{:S(2)}) collective-permute-start(f32[32,512]{1,0:T(8,128)S(1)} %collective-permute-done.8.refs_2_), channel_id=1, source_target_pairs={{0,1},{1,0},{2,3},{3,2},{4,5},{5,4},{6,7},{7,6},{8,9},{9,8},{10,11... | collective-permute-start | bytes 196616 | tf_op jit(solution)/shard_map/ppermute | solution.py:356
  27.3 4.0 %collective-permute-start.11 = (f32[32,512]{1,0:T(8,128)S(1)}, f32[32,512]{1,0:T(8,128)S(1)}, u32[]{:S(2)}, u32[]{:S(2)}) collective-permute-start(f32[32,512]{1,0:T(8,128)S(1)} %collective-permute-done.7.refs_1_), channel_id=1, source_target_pairs={{0,1},{1,0},{2,3},{3,2},{4,5},{5,4},{6,7},{7,6},{8,9},{9,8},{10,11... | collective-permute-start | bytes 196616 | tf_op jit(solution)/shard_map/ppermute | solution.py:356

commit v7 on v6

--- a/solution.py
+++ b/solution.py
@@ -10,11 +10,12 @@
 f32 = jnp.float32
 HIGHEST = lax.Precision.HIGHEST
 SUB, LANE = 8, 128
+BUF_ROWS = 2 * SUB * SUB + SUB
 VMEM = pl.BlockSpec(memory_space=pltpu.VMEM)
 HBM = pl.BlockSpec(memory_space=pltpu.HBM)
 VMEM_LIMIT = 20 << 20
 PARTS = 8
-CUTS = (0, 1, 4, 8)
+CUTS = (0, 1, 4, 5, 8)
 
 
 def dot(a, b, dims, precision=HIGHEST):
@@ -29,29 +30,32 @@
     return terms[0]
 
 
-def pivot_rows(e, rows):
-    n = len(rows)
+def pivot_rows(e, sets):
+    n = len(e)
     e = [list(line) for line in e]
-    rows = list(rows)
+    sets = [list(rows) for rows in sets]
     low = [[None] * n for _ in range(n)]
-    out = [None] * n
+    outs = [[None] * n for _ in sets]
     for a in range(0, n, 2):
         b = a + 1
         scale = 1.0 / (e[a][a] * e[b][b] - e[a][b] * e[a][b])
         aa, bb, ab = e[b][b] * scale, e[a][a] * scale, -(e[a][b] * scale)
-        out[a] = aa * rows[a] + ab * rows[b]
-        out[b] = ab * rows[a] + bb * rows[b]
+        for rows, out in zip(sets, outs):
+            out[a] = aa * rows[a] + ab * rows[b]
+            out[b] = ab * rows[a] + bb * rows[b]
         for i in range(b + 1, n):
             la = e[a][i] * aa + e[b][i] * ab
             lb = e[a][i] * ab + e[b][i] * bb
             low[i][a], low[i][b] = la, lb
             for m in range(i, n):
                 e[i][m] = e[i][m] - (la * e[a][m] + lb * e[b][m])
-            rows[i] = rows[i] - (la * rows[a] + lb * rows[b])
+            for rows in sets:
+                rows[i] = rows[i] - (la * rows[a] + lb * rows[b])
     for a in range(n - 4, -1, -2):
         for k in (a, a + 1):
-            out[k] = out[k] - add_all(low[i][k] * out[i] for i in range(a + 2, n))
-    return out
+            for out in outs:
+                out[k] = out[k] - add_all(low[i][k] * out[i] for i in range(a + 2, n))
+    return outs
 
 
 def across(v, k):
@@ -63,20 +67,40 @@
     lane = lax.broadcasted_iota(jnp.int32, (SUB, size), 1)
     sub = lax.broadcasted_iota(jnp.int32, (SUB, size), 0)
     n = size // SUB
+    square = SUB * SUB
     m = [matrix[SUB * i : SUB * (i + 1), :] for i in range(n)]
     low, scaled = [], []
+    cols = [across(m[0], k) for k in range(SUB)]
     for j in range(n):
         at = SUB * j
         here = (lane >= at) & (lane < at + SUB)
-        base = (j % 2) * SUB * (SUB + 1)
-        for k in range(SUB):
-            buf[base + SUB * k : base + SUB * (k + 1), :] = across(m[j], at + k)
+        base = (j % 2) * BUF_ROWS
+
+        def put(start, values):
+            for k, value in enumerate(values):
+                buf[base + start + SUB * k : base + start + SUB * (k + 1), :] = value
+
+        def get(i):
+            return jnp.broadcast_to(buf[base + i : base + i + 1, :], (SUB, size))
+
+        put(0, cols)
         row = jnp.where(here, (lane - at == sub).astype(f32), m[j])
-        buf[base + SUB * SUB : base + SUB * (SUB + 1), :] = row
-        spread = lambda i: jnp.broadcast_to(buf[base + i : base + i + 1, :], (SUB, size))
-        e = [[spread(SUB * k + i) if i <= k else None for k in range(SUB)] for i in range(SUB)]
-        new = pivot_rows(e, [spread(SUB * SUB + k) for k in range(SUB)])
-        for i in range(j + 1, n):
+        put(2 * square, [row])
+        e = [[get(SUB * k + i) if i <= k else None for k in range(SUB)] for i in range(SUB)]
+        sets = [[get(2 * square + k) for k in range(SUB)]]
+        if j + 1 < n:
+            side = [across(m[j + 1], at + k) for k in range(SUB)]
+            old = [across(m[j + 1], at + SUB + k) for k in range(SUB)]
+            put(square, side)
+            sets.append(side)
+        outs = pivot_rows(e, sets)
+        new = outs[0]
+        if j + 1 < n:
+            cols = [
+                old[i] - add_all(get(square + SUB * k + i) * outs[1][k] for k in range(SUB)) for i in range(SUB)
+            ]
+            m[j + 1] = jnp.where(here, 0.0, m[j + 1]) - add_all(side[k] * new[k] for k in range(SUB))
+        for i in range(j + 2, n):
             m[i] = jnp.where(here, 0.0, m[i]) - add_all(across(m[i], at + k) * new[k] for k in range(SUB))
         done = new[0]
         for i in range(1, SUB):
@@ -232,7 +256,7 @@
 def solve_scratch(size):
     return [
         pltpu.VMEM((size, size), f32),
-        pltpu.VMEM((2 * SUB * (SUB + 1), size), f32),
+        pltpu.VMEM((2 * BUF_ROWS, size), f32),
         pltpu.VMEM((size, size), f32),
         pltpu.VMEM((size, size), f32),
     ]
@@ -356,7 +380,7 @@
         return lax.ppermute(x, ("mem", "par"), pairs)
 
     width = ensemble.shape[1] // PARTS
-    first, second, third = (ensemble[:, width * i : width * k] for i, k in zip(CUTS, CUTS[1:]))
+    first, second, third, last = (ensemble[:, width * i : width * k] for i, k in zip(CUTS, CUTS[1:]))
     first = [swap(first, far, 0) for far in range(1, n_mem)]
     second = [swap(second, far, 0) for far in range(1, n_mem)]
     keep, send = forward(ensemble, operator)
@@ -371,18 +395,21 @@
         ways = min(4, n_par // stride)
         terms = [total] + [swap(total, 0, d * stride) for d in range(1, ways)]
         if stride == 4:
+            third, total = lax.optimization_barrier((third, total))
+            third = [swap(third, far, 0) for far in range(1, n_mem)]
             terms, target, root, second = lax.optimization_barrier((terms, target, root, second))
         total = add_all(terms)
         stride *= ways
     places = [(far, dy, 0) for far in range(n_mem) for dy in range(2)]
     pieces = [total if (far, dy) == (0, 0) else swap(total, far, 2 * dy) for far, dy, _ in places]
-    third, _ = lax.optimization_barrier((third, total))
-    third = [swap(third, far, 0) for far in range(1, n_mem)]
+    last, _ = lax.optimization_barrier((last, total))
+    last = [swap(last, far, 0) for far in range(1, n_mem)]
     inverse, near, shift = solve_near(pieces, root, ensemble.shape[0] * n_mem)
-    pieces += [swap(piece, 0, 1) for piece in pieces]
+    held, pieces[1], third = lax.optimization_barrier((pieces[0], pieces[1], third))
+    pieces += [swap(piece, 0, 1) for piece in [held] + pieces[1:]]
     places += [(far, dy, 1) for far, dy, _ in places]
     weights = solve(pieces, places, inverse, near, shift, target, root)
-    return update(weights, ensemble, [part for far in zip(first, second, third) for part in far])
+    return update(weights, ensemble, [part for far in zip(first, second, third, last) for part in far])
 
 
 def solution(mesh):

time: 39.9 us -> 38.2 us (0.957)
  waiting for transfers between devices: 8.85 us -> 6.11 us
  starting transfers between devices: 15.9 us -> 18 us
  Pallas kernels: 14.8 us -> 13.7 us
    ppermute x15 -> x16, waiting for transfers between devices: 8.85 us -> 6.11 us  [swap(): return lax.ppermute(x, ('mem', 'par'), pairs)]
    ppermute x15 -> x16, starting transfers between devices: 15.9 us -> 18 us  [swap(): return lax.ppermute(x, ('mem', 'par'), pairs)]
    pallas_call x1, Pallas kernels: 5.35 us -> 4.78 us  [solve(): pl.pallas_call(functools.partial(solve_kernel, places), out_shape=jax.Sha...]
    pallas_call x1, Pallas kernels: 3.87 us -> 3.3 us  [solve_near(): pl.pallas_call(functools.partial(near_kernel, members, len(pieces)), out_...]
  transfers between devices with their start and end apart: 15 -> 16, of which waited for: 9 -> 7; matrix products, arithmetic and copies ran while one was open for 0% -> 0% of each run, Pallas kernels for 25% -> 23%
where the time goes in v7:
time: 38.2 us; the launch traced here: 38 us
  starting transfers between devices  18 us (47%)
  Pallas kernels  13.7 us (36%)
  waiting for transfers between devices  6.11 us (16%)
    ppermute x16, starting transfers between devices, swap(): return lax.ppermute(x, ('mem', 'par'), pairs)  18 us
    ppermute x16, waiting for transfers between devices, swap(): return lax.ppermute(x, ('mem', 'par'), pairs)  6.11 us
    pallas_call x1, Pallas kernels, solve(): pl.pallas_call(functools.partial(solve_kernel, places), out_shape=jax.Sha...  4.78 us
    pallas_call x1, Pallas kernels, solve_near(): pl.pallas_call(functools.partial(near_kernel, members, len(pieces)), out_...  3.3 us
    pallas_call x1, Pallas kernels, forward(): pl.pallas_call(functools.partial(forward_kernel, steps), out_shape=(half,...  3.1 us
    pallas_call x1, Pallas kernels, update(): pl.pallas_call(update_kernel, out_shape=jax.ShapeDtypeStruct((own, params...  1.78 us
  transfers between devices with their start and end apart: 16, of which 7 were waited for; matrix products, arithmetic and copies ran while one was open for 0% of the time, Pallas kernels for 23%

profile of v7, /device:TPU:0, one launch (start us, length us, event | category | flops | bytes accessed | tf_op | source)
XLA Modules:
  0.0 38.0 jit_solution(9344461850171415627)
XLA Ops:
  0.0 3.1 %forward.1 = (f32[64,512]{1,0:T(8,128)S(1)}, f32[64,512]{1,0:T(8,128)S(1)}) custom-call(f32[128,2048]{1,0:T(8,128)} %own_ens.1, f32[2048,512]{1,0:T(8,128)} %op.1), custom_call_target="tpu_custom_call" | custom-call | flops 268435456 | bytes 5242880 | tf_op jit(solution)/shard_map/forward/pallas_call | solution.py:159
  3.1 0.5 %collective-permute-start = (f32[64,512]{1,0:T(8,128)S(1)}, f32[64,512]{1,0:T(8,128)S(1)}, u32[]{:S(2)}, u32[]{:S(2)}) collective-permute-start(f32[64,512]{1,0:T(8,128)S(1)} %get-tuple-element.27), channel_id=1, source_target_pairs={{0,1},{1,0},{2,3},{3,2},{4,5},{5,4},{6,7},{7,6},{8,9},{9,8},{10,11... | collective-permute-start | bytes 393224 | tf_op jit(solution)/shard_map/ppermute | solution.py:380
  3.7 2.6 %collective-permute-start.2 = (f32[128,256]{1,0:T(8,128)S(1)}, f32[128,256]{1,0:T(8,128)S(1)}, u32[]{:S(2)}, u32[]{:S(2)}) collective-permute-start(f32[128,256]{1,0:T(8,128)S(1)} %get-tuple-element.50), channel_id=1, source_target_pairs={{0,16},{1,17},{2,18},{3,19},{4,20},{5,21},{6,22},{7,23},{8,24},{9,... | collective-permute-start | bytes 393224 | tf_op jit(solution)/shard_map/ppermute | solution.py:380
  6.3 1.6 %collective-permute-start.1 = (f32[32,512]{1,0:T(8,128)S(1)}, f32[32,512]{1,0:T(8,128)S(1)}, u32[]{:S(2)}, u32[]{:S(2)}) collective-permute-start(f32[32,512]{1,0:T(8,128)S(1)} %constant_dynamic-slice_fusion), channel_id=1, source_target_pairs={{0,2},{1,3},{2,0},{3,1},{4,6},{5,7},{6,4},{7,5},{8,10},{9,11},{10,... | collective-permute-start | bytes 196616 | tf_op jit(solution)/shard_map/ppermute | solution.py:380
  8.0 1.3 %collective-permute-start.6 = (f32[128,768]{1,0:T(8,128)S(1)}, f32[128,768]{1,0:T(8,128)S(1)}, u32[]{:S(2)}, u32[]{:S(2)}) collective-permute-start(f32[128,768]{1,0:T(8,128)S(1)} %get-tuple-element.48), channel_id=1, source_target_pairs={{0,16},{1,17},{2,18},{3,19},{4,20},{5,21},{6,22},{7,23},{8,24},{9,... | collective-permute-start | bytes 1179656 | tf_op jit(solution)/shard_map/ppermute | solution.py:380
  9.2 1.1 %collective-permute-done.2.refs_0_ = f32[128,256]{1,0:T(8,128)S(1)} collective-permute-done((f32[128,256]{1,0:T(8,128)S(1)}, f32[128,256]{1,0:T(8,128)S(1)}, u32[]{:S(2)}, u32[]{:S(2)}) %collective-permute-start.2) | collective-permute-done | bytes 131104 | tf_op jit(solution)/shard_map/ppermute | solution.py:380
  10.4 0.2 collective-permute-done.1
  10.6 3.8 %collective-permute-start.5 = (f32[32,512]{1,0:T(8,128)S(1)}, f32[32,512]{1,0:T(8,128)S(1)}, u32[]{:S(2)}, u32[]{:S(2)}) collective-permute-start(f32[32,512]{1,0:T(8,128)S(1)} %dynamic-slice_add_fusion), channel_id=1, source_target_pairs={{0,12},{1,13},{2,14},{3,15},{4,8},{5,9},{6,10},{7,11},{8,4},{9,5},... | collective-permute-start | bytes 196616 | tf_op jit(solution)/shard_map/ppermute | solution.py:380
  14.4 0.7 %collective-permute-start.3 = (f32[32,512]{1,0:T(8,128)S(1)}, f32[32,512]{1,0:T(8,128)S(1)}, u32[]{:S(2)}, u32[]{:S(2)}) collective-permute-start(f32[32,512]{1,0:T(8,128)S(1)} %dynamic-slice_add_fusion), channel_id=1, source_target_pairs={{0,4},{1,5},{2,6},{3,7},{4,0},{5,1},{6,2},{7,3},{8,12},{9,13},{10,... | collective-permute-start | bytes 196616 | tf_op jit(solution)/shard_map/ppermute | solution.py:380
  15.1 0.7 %lookup.1 = (f32[128,512]{1,0:T(8,128)S(1)}, f32[8,512]{1,0:T(8,128)S(1)}) custom-call(s32[1,512]{1,0:T(1,128)S(1)} %bitcast.5, f32[128,128]{1,0:T(8,128)S(1)} %bitcast.3, f32[128,128]{1,0:T(8,128)S(1)} %bitcast.4, f32[128,512]{1,0:T(8,128)S(1)} %copy-done.1), custom_call_target="tpu_custom_call" | custom-call | flops 25769803776 | bytes 1048576 | tf_op jit(solution)/shard_map/lookup/pallas_call | solution.py:194
  15.8 2.0 %collective-permute-start.8 = (f32[128,256]{1,0:T(8,128)S(1)}, f32[128,256]{1,0:T(8,128)S(1)}, u32[]{:S(2)}, u32[]{:S(2)}) collective-permute-start(f32[128,256]{1,0:T(8,128)S(1)} %get-tuple-element.35), channel_id=1, source_target_pairs={{0,16},{1,17},{2,18},{3,19},{4,20},{5,21},{6,22},{7,23},{8,24},{9,... | collective-permute-start | bytes 393224 | tf_op jit(solution)/shard_map/ppermute | solution.py:380
  17.8 2.1 %collective-permute-done.4 = f32[32,512]{1,0:T(8,128)S(1)} collective-permute-done((f32[32,512]{1,0:T(8,128)S(1)}, f32[32,512]{1,0:T(8,128)S(1)}, u32[]{:S(2)}, u32[]{:S(2)}) %collective-permute-start.4) | collective-permute-done | bytes 65568 | tf_op jit(solution)/shard_map/ppermute | solution.py:380
  19.9 0.1 collective-permute-done.3
  19.9 0.1 collective-permute-done.6.refs_1_
  20.0 1.6 %collective-permute-start.7 = (f32[32,512]{1,0:T(8,128)S(1)}, f32[32,512]{1,0:T(8,128)S(1)}, u32[]{:S(2)}, u32[]{:S(2)}) collective-permute-start(f32[32,512]{1,0:T(8,128)S(1)} %add_add_fusion.refs_0_), channel_id=1, source_target_pairs={{0,2},{1,3},{2,0},{3,1},{4,6},{5,7},{6,4},{7,5},{8,10},{9,11},{10,... | collective-permute-start | bytes 196616 | tf_op jit(solution)/shard_map/ppermute | solution.py:380
  21.6 1.4 %collective-permute-start.10 = (f32[32,512]{1,0:T(8,128)S(1)}, f32[32,512]{1,0:T(8,128)S(1)}, u32[]{:S(2)}, u32[]{:S(2)}) collective-permute-start(f32[32,512]{1,0:T(8,128)S(1)} %add_add_fusion.refs_0_), channel_id=1, source_target_pairs={{0,18},{1,19},{2,16},{3,17},{4,22},{5,23},{6,20},{7,21},{8,26},{9,... | collective-permute-start | bytes 196616 | tf_op jit(solution)/shard_map/ppermute | solution.py:380
  23.0 0.6 %collective-permute-start.9 = (f32[32,512]{1,0:T(8,128)S(1)}, f32[32,512]{1,0:T(8,128)S(1)}, u32[]{:S(2)}, u32[]{:S(2)}) collective-permute-start(f32[32,512]{1,0:T(8,128)S(1)} %add_add_fusion.refs_0_), channel_id=1, source_target_pairs={{0,16},{1,17},{2,18},{3,19},{4,20},{5,21},{6,22},{7,23},{8,24},{9,... | collective-permute-start | bytes 196616 | tf_op jit(solution)/shard_map/ppermute | solution.py:380
  23.6 1.5 %collective-permute-start.15 = (f32[128,768]{1,0:T(8,128)S(1)}, f32[128,768]{1,0:T(8,128)S(1)}, u32[]{:S(2)}, u32[]{:S(2)}) collective-permute-start(f32[128,768]{1,0:T(8,128)S(1)} %get-tuple-element.46), channel_id=1, source_target_pairs={{0,16},{1,17},{2,18},{3,19},{4,20},{5,21},{6,22},{7,23},{8,24},{9,... | collective-permute-start | bytes 1179656 | tf_op jit(solution)/shard_map/ppermute | solution.py:380
  25.1 0.5 %collective-permute-start.12 = (f32[32,512]{1,0:T(8,128)S(1)}, f32[32,512]{1,0:T(8,128)S(1)}, u32[]{:S(2)}, u32[]{:S(2)}) collective-permute-start(f32[32,512]{1,0:T(8,128)S(1)} %collective-permute-done.7.refs_1_), channel_id=1, source_target_pairs={{0,1},{1,0},{2,3},{3,2},{4,5},{5,4},{6,7},{7,6},{8,9},{9,8},{10,11... | collective-permute-start | bytes 196616 | tf_op jit(solution)/shard_map/ppermute | solution.py:380
  25.6 1.9 %collective-permute-done.10.refs_3_ = f32[32,512]{1,0:T(8,128)S(1)} collective-permute-done((f32[32,512]{1,0:T(8,128)S(1)}, f32[32,512]{1,0:T(8,128)S(1)}, u32[]{:S(2)}, u32[]{:S(2)}) %collective-permute-start.10) | collective-permute-done | bytes 65568 | tf_op jit(solution)/shard_map/ppermute | solution.py:380
  27.5 0.6 %collective-permute-done.9.refs_2_ = f32[32,512]{1,0:T(8,128)S(1)} collective-permute-done((f32[32,512]{1,0:T(8,128)S(1)}, f32[32,512]{1,0:T(8,128)S(1)}, u32[]{:S(2)}, u32[]{:S(2)}) %collective-permute-start.9) | collective-permute-done | bytes 65568 | tf_op jit(solution)/shard_map/ppermute | solution.py:380
  28.1 3.3 %solve_near.1 = (f32[128,128]{1,0:T(8,128)S(1)}, f32[128,512]{1,0:T(8,128)S(1)}, f32[8,512]{1,0:T(8,128)S(1)}) custom-call(f32[32,512]{1,0:T(8,128)S(1)} %add_add_fusion.refs_0_, f32[32,512]{1,0:T(8,128)S(1)} %collective-permute-done.7.refs_1_, f32[32,512]{1,0:T(8,128)S(1)} %collective-permute-done.9.refs_2_, f32[32,512]{1,0:T(8,128)S(1)} %collective-permute-done.10.refs_3_, ...), custom_call_target="tpu_custom_call" | custom-call | flops 5000000000 | bytes 1 | tf_op jit(solution)/shard_map/solve_near/pallas_call | solution.py:244
  31.4 4.8 %solve.1.weights = f32[128,256]{1,0:T(8,128)S(1)} custom-call(f32[32,512]{1,0:T(8,128)S(1)} %add_add_fusion.refs_0_, f32[32,512]{1,0:T(8,128)S(1)} %collective-permute-done.7.refs_1_, f32[32,512]{1,0:T(8,128)S(1)} %collective-permute-done.9.refs_2_, f32[32,512]{1,0:T(8,128)S(1)} %collective-permute-done.10.refs_3_, ...), custom_call_target="tpu_custom_call" | custom-call | flops 5000000000 | bytes 1 | tf_op jit(solution)/shard_map/solve/pallas_call | solution.py:315
  36.2 1.8 %update.1 = f32[128,2048]{1,0:T(8,128)} custom-call(f32[128,256]{1,0:T(8,128)S(1)} %solve.1.weights, f32[128,2048]{1,0:T(8,128)S(1)} %copy-done, f32[128,256]{1,0:T(8,128)S(1)} %collective-permute-done.2.refs_0_, f32[128,768]{1,0:T(8,128)S(1)} %collective-permute-done.6.refs_1_, f32[128,256]{1,0:T(8,128)S(1)} %collective-permute-done.8.refs_2_, ...), custom_call_target="tpu_custom_call" | custom-call | flops 134217728 | bytes 3145728 | tf_op jit(solution)/shard_map/update/pallas_call | solution.py:358
  (29 shorter events, 0.2 us)
Async XLA Ops:
  0.0 3.7 %copy-start = (f32[128,2048]{1,0:T(8,128)S(1)}, f32[128,2048]{1,0:T(8,128)}, u32[]{:S(2)}) copy-start(f32[128,2048]{1,0:T(8,128)} %own_ens.1) | copy-start | bytes 3145732
  0.0 15.1 %copy-start.4 = (s32[512]{0:T(512)S(1)}, s32[512]{0:T(512)}, u32[]{:S(2)}) copy-start(s32[512]{0:T(512)} %param.11) | copy-start | bytes 6148
  0.0 15.1 %copy-start.3 = (f32[16384]{0:T(1024)S(1)}, f32[16384]{0:T(1024)}, u32[]{:S(2)}) copy-start(f32[16384]{0:T(1024)} %param.10) | copy-start | bytes 196612
  0.0 15.1 %copy-start.2 = (f32[16384]{0:T(1024)S(1)}, f32[16384]{0:T(1024)}, u32[]{:S(2)}) copy-start(f32[16384]{0:T(1024)} %param.9) | copy-start | bytes 196612
  0.0 15.1 %copy-start.1 = (f32[128,512]{1,0:T(8,128)S(1)}, f32[128,512]{1,0:T(8,128)}, u32[]{:S(2)}) copy-start(f32[128,512]{1,0:T(8,128)} %noise.1) | copy-start | bytes 786436
  3.1 3.1 %collective-permute-start = (f32[64,512]{1,0:T(8,128)S(1)}, f32[64,512]{1,0:T(8,128)S(1)}, u32[]{:S(2)}, u32[]{:S(2)}) collective-permute-start(f32[64,512]{1,0:T(8,128)S(1)} %get-tuple-element.27), channel_id=1, source_target_pairs={{0,1},{1,0},{2,3},{3,2},{4,5},{5,4},{6,7},{7,6},{8,9},{9,8},{10,11... | collective-permute-start | bytes 393224 | tf_op jit(solution)/shard_map/ppermute | solution.py:380
  3.7 6.7 %collective-permute-start.2 = (f32[128,256]{1,0:T(8,128)S(1)}, f32[128,256]{1,0:T(8,128)S(1)}, u32[]{:S(2)}, u32[]{:S(2)}) collective-permute-start(f32[128,256]{1,0:T(8,128)S(1)} %get-tuple-element.50), channel_id=1, source_target_pairs={{0,16},{1,17},{2,18},{3,19},{4,20},{5,21},{6,22},{7,23},{8,24},{9,... | collective-permute-start | bytes 393224 | tf_op jit(solution)/shard_map/ppermute | solution.py:380
  6.3 4.3 %collective-permute-start.1 = (f32[32,512]{1,0:T(8,128)S(1)}, f32[32,512]{1,0:T(8,128)S(1)}, u32[]{:S(2)}, u32[]{:S(2)}) collective-permute-start(f32[32,512]{1,0:T(8,128)S(1)} %constant_dynamic-slice_fusion), channel_id=1, source_target_pairs={{0,2},{1,3},{2,0},{3,1},{4,6},{5,7},{6,4},{7,5},{8,10},{9,11},{10,... | collective-permute-start | bytes 196616 | tf_op jit(solution)/shard_map/ppermute | solution.py:380
  8.0 12.1 %collective-permute-start.6 = (f32[128,768]{1,0:T(8,128)S(1)}, f32[128,768]{1,0:T(8,128)S(1)}, u32[]{:S(2)}, u32[]{:S(2)}) collective-permute-start(f32[128,768]{1,0:T(8,128)S(1)} %get-tuple-element.48), channel_id=1, source_target_pairs={{0,16},{1,17},{2,18},{3,19},{4,20},{5,21},{6,22},{7,23},{8,24},{9,... | collective-permute-start | bytes 1179656 | tf_op jit(solution)/shard_map/ppermute | solution.py:380
  10.6 7.1 %collective-permute-start.5 = (f32[32,512]{1,0:T(8,128)S(1)}, f32[32,512]{1,0:T(8,128)S(1)}, u32[]{:S(2)}, u32[]{:S(2)}) collective-permute-start(f32[32,512]{1,0:T(8,128)S(1)} %dynamic-slice_add_fusion), channel_id=1, source_target_pairs={{0,12},{1,13},{2,14},{3,15},{4,8},{5,9},{6,10},{7,11},{8,4},{9,5},... | collective-permute-start | bytes 196616 | tf_op jit(solution)/shard_map/ppermute | solution.py:380
  14.4 5.5 %collective-permute-start.4 = (f32[32,512]{1,0:T(8,128)S(1)}, f32[32,512]{1,0:T(8,128)S(1)}, u32[]{:S(2)}, u32[]{:S(2)}) collective-permute-start(f32[32,512]{1,0:T(8,128)S(1)} %dynamic-slice_add_fusion), channel_id=1, source_target_pairs={{0,8},{1,9},{2,10},{3,11},{4,12},{5,13},{6,14},{7,15},{8,0},{9,1},... | collective-permute-start | bytes 196616 | tf_op jit(solution)/shard_map/ppermute | solution.py:380
  14.4 5.5 %collective-permute-start.3 = (f32[32,512]{1,0:T(8,128)S(1)}, f32[32,512]{1,0:T(8,128)S(1)}, u32[]{:S(2)}, u32[]{:S(2)}) collective-permute-start(f32[32,512]{1,0:T(8,128)S(1)} %dynamic-slice_add_fusion), channel_id=1, source_target_pairs={{0,4},{1,5},{2,6},{3,7},{4,0},{5,1},{6,2},{7,3},{8,12},{9,13},{10,... | collective-permute-start | bytes 196616 | tf_op jit(solution)/shard_map/ppermute | solution.py:380
  15.8 9.2 %collective-permute-start.8 = (f32[128,256]{1,0:T(8,128)S(1)}, f32[128,256]{1,0:T(8,128)S(1)}, u32[]{:S(2)}, u32[]{:S(2)}) collective-permute-start(f32[128,256]{1,0:T(8,128)S(1)} %get-tuple-element.35), channel_id=1, source_target_pairs={{0,16},{1,17},{2,18},{3,19},{4,20},{5,21},{6,22},{7,23},{8,24},{9,... | collective-permute-start | bytes 393224 | tf_op jit(solution)/shard_map/ppermute | solution.py:380
  20.0 5.0 %collective-permute-start.7 = (f32[32,512]{1,0:T(8,128)S(1)}, f32[32,512]{1,0:T(8,128)S(1)}, u32[]{:S(2)}, u32[]{:S(2)}) collective-permute-start(f32[32,512]{1,0:T(8,128)S(1)} %add_add_fusion.refs_0_), channel_id=1, source_target_pairs={{0,2},{1,3},{2,0},{3,1},{4,6},{5,7},{6,4},{7,5},{8,10},{9,11},{10,... | collective-permute-start | bytes 196616 | tf_op jit(solution)/shard_map/ppermute | solution.py:380
  21.6 5.9 %collective-permute-start.10 = (f32[32,512]{1,0:T(8,128)S(1)}, f32[32,512]{1,0:T(8,128)S(1)}, u32[]{:S(2)}, u32[]{:S(2)}) collective-permute-start(f32[32,512]{1,0:T(8,128)S(1)} %add_add_fusion.refs_0_), channel_id=1, source_target_pairs={{0,18},{1,19},{2,16},{3,17},{4,22},{5,23},{6,20},{7,21},{8,26},{9,... | collective-permute-start | bytes 196616 | tf_op jit(solution)/shard_map/ppermute | solution.py:380
  23.0 5.0 %collective-permute-start.9 = (f32[32,512]{1,0:T(8,128)S(1)}, f32[32,512]{1,0:T(8,128)S(1)}, u32[]{:S(2)}, u32[]{:S(2)}) collective-permute-start(f32[32,512]{1,0:T(8,128)S(1)} %add_add_fusion.refs_0_), channel_id=1, source_target_pairs={{0,16},{1,17},{2,18},{3,19},{4,20},{5,21},{6,22},{7,23},{8,24},{9,... | collective-permute-start | bytes 196616 | tf_op jit(solution)/shard_map/ppermute | solution.py:380
  23.6 12.6 %collective-permute-start.15 = (f32[128,768]{1,0:T(8,128)S(1)}, f32[128,768]{1,0:T(8,128)S(1)}, u32[]{:S(2)}, u32[]{:S(2)}) collective-permute-start(f32[128,768]{1,0:T(8,128)S(1)} %get-tuple-element.46), channel_id=1, source_target_pairs={{0,16},{1,17},{2,18},{3,19},{4,20},{5,21},{6,22},{7,23},{8,24},{9,... | collective-permute-start | bytes 1179656 | tf_op jit(solution)/shard_map/ppermute | solution.py:380
  25.1 6.3 %collective-permute-start.11 = (f32[32,512]{1,0:T(8,128)S(1)}, f32[32,512]{1,0:T(8,128)S(1)}, u32[]{:S(2)}, u32[]{:S(2)}) collective-permute-start(f32[32,512]{1,0:T(8,128)S(1)} %add_add_fusion.refs_0_), channel_id=1, source_target_pairs={{0,1},{1,0},{2,3},{3,2},{4,5},{5,4},{6,7},{7,6},{8,9},{9,8},{10,11... | collective-permute-start | bytes 196616 | tf_op jit(solution)/shard_map/ppermute | solution.py:380
  25.1 6.3 %collective-permute-start.12 = (f32[32,512]{1,0:T(8,128)S(1)}, f32[32,512]{1,0:T(8,128)S(1)}, u32[]{:S(2)}, u32[]{:S(2)}) collective-permute-start(f32[32,512]{1,0:T(8,128)S(1)} %collective-permute-done.7.refs_1_), channel_id=1, source_target_pairs={{0,1},{1,0},{2,3},{3,2},{4,5},{5,4},{6,7},{7,6},{8,9},{9,8},{10,11... | collective-permute-start | bytes 196616 | tf_op jit(solution)/shard_map/ppermute | solution.py:380
  27.5 3.9 %collective-permute-start.14 = (f32[32,512]{1,0:T(8,128)S(1)}, f32[32,512]{1,0:T(8,128)S(1)}, u32[]{:S(2)}, u32[]{:S(2)}) collective-permute-start(f32[32,512]{1,0:T(8,128)S(1)} %collective-permute-done.10.refs_3_), channel_id=1, source_target_pairs={{0,1},{1,0},{2,3},{3,2},{4,5},{5,4},{6,7},{7,6},{8,9},{9,8},{10,11... | collective-permute-start | bytes 196616 | tf_op jit(solution)/shard_map/ppermute | solution.py:380
  28.1 3.3 %collective-permute-start.13 = (f32[32,512]{1,0:T(8,128)S(1)}, f32[32,512]{1,0:T(8,128)S(1)}, u32[]{:S(2)}, u32[]{:S(2)}) collective-permute-start(f32[32,512]{1,0:T(8,128)S(1)} %collective-permute-done.9.refs_2_), channel_id=1, source_target_pairs={{0,1},{1,0},{2,3},{3,2},{4,5},{5,4},{6,7},{7,6},{8,9},{9,8},{10,11... | collective-permute-start | bytes 196616 | tf_op jit(solution)/shard_map/ppermute | solution.py:380

commit v8 on v7

--- a/solution.py
+++ b/solution.py
@@ -109,6 +109,25 @@
         low.append(jnp.where(keep, row, 0.0))
         scaled.append(jnp.where(keep, done, 0.0))
     return jnp.concatenate(low, axis=0), jnp.concatenate(scaled, axis=0)
+
+
+def own_bits():
+    index = lax.axis_index("par")
+    return lax.bitwise_and(index, 1), lax.bitwise_and(lax.shift_right_logical(index, 1), 1)
+
+
+def halves(x):
+    high = x.astype(jnp.bfloat16)
+    return high, (x - high.astype(f32)).astype(jnp.bfloat16)
+
+
+def matmul(a, b, dims=((1,), (0,))):
+    return lax.dot_general(a, b, (dims, ((), ())), preferred_element_type=f32)
+
+
+def dot3(a, b, dims):
+    (ah, al), (bh, bl) = halves(a), halves(b)
+    return matmul(ah, bh, dims) + (matmul(ah, bl, dims) + matmul(al, bh, dims))
 
 
 def own_bits():
@@ -334,19 +353,17 @@
 def update_kernel(weights, own_ens, *refs):
     parts = len(CUTS) - 1
     others, (out, buf, sems) = refs[:-3], refs[-3:]
-    own, params = own_ens.shape
-    width = params // PARTS
+    width = out.shape[1] // PARTS
+    w_high, w_low = halves(weights[...])
     copies = []
     for part in range(parts):
         for i in range(CUTS[part], CUTS[part + 1]):
             cols = slice(i * width, (i + 1) * width)
             at = slice((i - CUTS[part]) * width, (i - CUTS[part] + 1) * width)
-            total = own_ens[:, cols]
-            total = total + dot3(weights[:, :own], total, ((1,), (0,)))
-            for far in range(1, len(others) // parts + 1):
-                w = weights[:, far * own : (far + 1) * own]
-                total = total + dot3(w, others[(far - 1) * parts + part][:, at], ((1,), (0,)))
-            buf[:, cols] = total
+            held = [own_ens[:, cols]] + [ref[:, at] for ref in others[part::parts]]
+            high, low = halves(jnp.concatenate(held, axis=0))
+            change = matmul(w_high, high) + (matmul(w_high, low) + matmul(w_low, high))
+            buf[:, cols] = held[0] + change
             copies.append(pltpu.make_async_copy(buf.at[:, cols], out.at[:, cols], sems.at[i]))
             copies[-1].start()
     for copy in copies:
@@ -405,8 +422,8 @@
     last, _ = lax.optimization_barrier((last, total))
     last = [swap(last, far, 0) for far in range(1, n_mem)]
     inverse, near, shift = solve_near(pieces, root, ensemble.shape[0] * n_mem)
-    held, pieces[1], third = lax.optimization_barrier((pieces[0], pieces[1], third))
-    pieces += [swap(piece, 0, 1) for piece in [held] + pieces[1:]]
+    mine, pieces[1], third = lax.optimization_barrier((pieces[0], pieces[1], third))
+    pieces += [swap(piece, 0, 1) for piece in [mine] + pieces[1:]]
     places += [(far, dy, 1) for far, dy, _ in places]
     weights = solve(pieces, places, inverse, near, shift, target, root)
     return update(weights, ensemble, [part for far in zip(first, second, third, last) for part in far])

time: 38.2 us -> 37.9 us (level)
  no operation moved by 1% of the time
where the time goes in v8:
time: 37.9 us; the launch traced here: 37.7 us
  starting transfers between devices  18 us (47%)
  Pallas kernels  13.4 us (35%)
  waiting for transfers between devices  6.11 us (16%)
    ppermute x16, starting transfers between devices, swap(): return lax.ppermute(x, ('mem', 'par'), pairs)  18 us
    ppermute x16, waiting for transfers between devices, swap(): return lax.ppermute(x, ('mem', 'par'), pairs)  6.11 us
    pallas_call x1, Pallas kernels, solve(): pl.pallas_call(functools.partial(solve_kernel, places), out_shape=jax.Sha...  4.78 us
    pallas_call x1, Pallas kernels, solve_near(): pl.pallas_call(functools.partial(near_kernel, members, len(pieces)), out_...  3.3 us
    pallas_call x1, Pallas kernels, forward(): pl.pallas_call(functools.partial(forward_kernel, steps), out_shape=(half,...  3.1 us
    pallas_call x1, Pallas kernels, update(): pl.pallas_call(update_kernel, out_shape=jax.ShapeDtypeStruct((own, params...  1.49 us
  transfers between devices with their start and end apart: 16, of which 7 were waited for; matrix products, arithmetic and copies ran while one was open for 0% of the time, Pallas kernels for 23%

profile of v8, /device:TPU:0, one launch (start us, length us, event | category | flops | bytes accessed | tf_op | source)
XLA Modules:
  0.0 37.7 jit_solution(14386373714789295430)
XLA Ops:
  0.0 3.1 %forward.1 = (f32[64,512]{1,0:T(8,128)S(1)}, f32[64,512]{1,0:T(8,128)S(1)}) custom-call(f32[128,2048]{1,0:T(8,128)} %own_ens.1, f32[2048,512]{1,0:T(8,128)} %op.1), custom_call_target="tpu_custom_call" | custom-call | flops 268435456 | bytes 5242880 | tf_op jit(solution)/shard_map/forward/pallas_call | solution.py:178
  3.1 0.5 %collective-permute-start = (f32[64,512]{1,0:T(8,128)S(1)}, f32[64,512]{1,0:T(8,128)S(1)}, u32[]{:S(2)}, u32[]{:S(2)}) collective-permute-start(f32[64,512]{1,0:T(8,128)S(1)} %get-tuple-element.27), channel_id=1, source_target_pairs={{0,1},{1,0},{2,3},{3,2},{4,5},{5,4},{6,7},{7,6},{8,9},{9,8},{10,11... | collective-permute-start | bytes 393224 | tf_op jit(solution)/shard_map/ppermute | solution.py:397
  3.7 2.6 %collective-permute-start.2 = (f32[128,256]{1,0:T(8,128)S(1)}, f32[128,256]{1,0:T(8,128)S(1)}, u32[]{:S(2)}, u32[]{:S(2)}) collective-permute-start(f32[128,256]{1,0:T(8,128)S(1)} %get-tuple-element.50), channel_id=1, source_target_pairs={{0,16},{1,17},{2,18},{3,19},{4,20},{5,21},{6,22},{7,23},{8,24},{9,... | collective-permute-start | bytes 393224 | tf_op jit(solution)/shard_map/ppermute | solution.py:397
  6.3 1.6 %collective-permute-start.1 = (f32[32,512]{1,0:T(8,128)S(1)}, f32[32,512]{1,0:T(8,128)S(1)}, u32[]{:S(2)}, u32[]{:S(2)}) collective-permute-start(f32[32,512]{1,0:T(8,128)S(1)} %constant_dynamic-slice_fusion), channel_id=1, source_target_pairs={{0,2},{1,3},{2,0},{3,1},{4,6},{5,7},{6,4},{7,5},{8,10},{9,11},{10,... | collective-permute-start | bytes 196616 | tf_op jit(solution)/shard_map/ppermute | solution.py:397
  8.0 1.3 %collective-permute-start.6 = (f32[128,768]{1,0:T(8,128)S(1)}, f32[128,768]{1,0:T(8,128)S(1)}, u32[]{:S(2)}, u32[]{:S(2)}) collective-permute-start(f32[128,768]{1,0:T(8,128)S(1)} %get-tuple-element.48), channel_id=1, source_target_pairs={{0,16},{1,17},{2,18},{3,19},{4,20},{5,21},{6,22},{7,23},{8,24},{9,... | collective-permute-start | bytes 1179656 | tf_op jit(solution)/shard_map/ppermute | solution.py:397
  9.2 1.1 %collective-permute-done.2.refs_0_ = f32[128,256]{1,0:T(8,128)S(1)} collective-permute-done((f32[128,256]{1,0:T(8,128)S(1)}, f32[128,256]{1,0:T(8,128)S(1)}, u32[]{:S(2)}, u32[]{:S(2)}) %collective-permute-start.2) | collective-permute-done | bytes 131104 | tf_op jit(solution)/shard_map/ppermute | solution.py:397
  10.4 0.2 collective-permute-done.1
  10.6 3.8 %collective-permute-start.5 = (f32[32,512]{1,0:T(8,128)S(1)}, f32[32,512]{1,0:T(8,128)S(1)}, u32[]{:S(2)}, u32[]{:S(2)}) collective-permute-start(f32[32,512]{1,0:T(8,128)S(1)} %dynamic-slice_add_fusion), channel_id=1, source_target_pairs={{0,12},{1,13},{2,14},{3,15},{4,8},{5,9},{6,10},{7,11},{8,4},{9,5},... | collective-permute-start | bytes 196616 | tf_op jit(solution)/shard_map/ppermute | solution.py:397
  14.4 0.7 %collective-permute-start.3 = (f32[32,512]{1,0:T(8,128)S(1)}, f32[32,512]{1,0:T(8,128)S(1)}, u32[]{:S(2)}, u32[]{:S(2)}) collective-permute-start(f32[32,512]{1,0:T(8,128)S(1)} %dynamic-slice_add_fusion), channel_id=1, source_target_pairs={{0,4},{1,5},{2,6},{3,7},{4,0},{5,1},{6,2},{7,3},{8,12},{9,13},{10,... | collective-permute-start | bytes 196616 | tf_op jit(solution)/shard_map/ppermute | solution.py:397
  15.1 0.7 %lookup.1 = (f32[128,512]{1,0:T(8,128)S(1)}, f32[8,512]{1,0:T(8,128)S(1)}) custom-call(s32[1,512]{1,0:T(1,128)S(1)} %bitcast.5, f32[128,128]{1,0:T(8,128)S(1)} %bitcast.3, f32[128,128]{1,0:T(8,128)S(1)} %bitcast.4, f32[128,512]{1,0:T(8,128)S(1)} %copy-done.1), custom_call_target="tpu_custom_call" | custom-call | flops 25769803776 | bytes 1048576 | tf_op jit(solution)/shard_map/lookup/pallas_call | solution.py:213
  15.8 2.0 %collective-permute-start.8 = (f32[128,256]{1,0:T(8,128)S(1)}, f32[128,256]{1,0:T(8,128)S(1)}, u32[]{:S(2)}, u32[]{:S(2)}) collective-permute-start(f32[128,256]{1,0:T(8,128)S(1)} %get-tuple-element.35), channel_id=1, source_target_pairs={{0,16},{1,17},{2,18},{3,19},{4,20},{5,21},{6,22},{7,23},{8,24},{9,... | collective-permute-start | bytes 393224 | tf_op jit(solution)/shard_map/ppermute | solution.py:397
  17.8 2.1 %collective-permute-done.4 = f32[32,512]{1,0:T(8,128)S(1)} collective-permute-done((f32[32,512]{1,0:T(8,128)S(1)}, f32[32,512]{1,0:T(8,128)S(1)}, u32[]{:S(2)}, u32[]{:S(2)}) %collective-permute-start.4) | collective-permute-done | bytes 65568 | tf_op jit(solution)/shard_map/ppermute | solution.py:397
  19.9 0.1 collective-permute-done.3
  19.9 0.1 collective-permute-done.6.refs_1_
  20.0 1.6 %collective-permute-start.7 = (f32[32,512]{1,0:T(8,128)S(1)}, f32[32,512]{1,0:T(8,128)S(1)}, u32[]{:S(2)}, u32[]{:S(2)}) collective-permute-start(f32[32,512]{1,0:T(8,128)S(1)} %add_add_fusion.refs_0_), channel_id=1, source_target_pairs={{0,2},{1,3},{2,0},{3,1},{4,6},{5,7},{6,4},{7,5},{8,10},{9,11},{10,... | collective-permute-start | bytes 196616 | tf_op jit(solution)/shard_map/ppermute | solution.py:397
  21.6 1.4 %collective-permute-start.10 = (f32[32,512]{1,0:T(8,128)S(1)}, f32[32,512]{1,0:T(8,128)S(1)}, u32[]{:S(2)}, u32[]{:S(2)}) collective-permute-start(f32[32,512]{1,0:T(8,128)S(1)} %add_add_fusion.refs_0_), channel_id=1, source_target_pairs={{0,18},{1,19},{2,16},{3,17},{4,22},{5,23},{6,20},{7,21},{8,26},{9,... | collective-permute-start | bytes 196616 | tf_op jit(solution)/shard_map/ppermute | solution.py:397
  23.0 0.6 %collective-permute-start.9 = (f32[32,512]{1,0:T(8,128)S(1)}, f32[32,512]{1,0:T(8,128)S(1)}, u32[]{:S(2)}, u32[]{:S(2)}) collective-permute-start(f32[32,512]{1,0:T(8,128)S(1)} %add_add_fusion.refs_0_), channel_id=1, source_target_pairs={{0,16},{1,17},{2,18},{3,19},{4,20},{5,21},{6,22},{7,23},{8,24},{9,... | collective-permute-start | bytes 196616 | tf_op jit(solution)/shard_map/ppermute | solution.py:397
  23.6 1.5 %collective-permute-start.15 = (f32[128,768]{1,0:T(8,128)S(1)}, f32[128,768]{1,0:T(8,128)S(1)}, u32[]{:S(2)}, u32[]{:S(2)}) collective-permute-start(f32[128,768]{1,0:T(8,128)S(1)} %get-tuple-element.46), channel_id=1, source_target_pairs={{0,16},{1,17},{2,18},{3,19},{4,20},{5,21},{6,22},{7,23},{8,24},{9,... | collective-permute-start | bytes 1179656 | tf_op jit(solution)/shard_map/ppermute | solution.py:397
  25.1 0.5 %collective-permute-start.12 = (f32[32,512]{1,0:T(8,128)S(1)}, f32[32,512]{1,0:T(8,128)S(1)}, u32[]{:S(2)}, u32[]{:S(2)}) collective-permute-start(f32[32,512]{1,0:T(8,128)S(1)} %collective-permute-done.7.refs_1_), channel_id=1, source_target_pairs={{0,1},{1,0},{2,3},{3,2},{4,5},{5,4},{6,7},{7,6},{8,9},{9,8},{10,11... | collective-permute-start | bytes 196616 | tf_op jit(solution)/shard_map/ppermute | solution.py:397
  25.6 1.9 %collective-permute-done.10.refs_3_ = f32[32,512]{1,0:T(8,128)S(1)} collective-permute-done((f32[32,512]{1,0:T(8,128)S(1)}, f32[32,512]{1,0:T(8,128)S(1)}, u32[]{:S(2)}, u32[]{:S(2)}) %collective-permute-start.10) | collective-permute-done | bytes 65568 | tf_op jit(solution)/shard_map/ppermute | solution.py:397
  27.5 0.6 %collective-permute-done.9.refs_2_ = f32[32,512]{1,0:T(8,128)S(1)} collective-permute-done((f32[32,512]{1,0:T(8,128)S(1)}, f32[32,512]{1,0:T(8,128)S(1)}, u32[]{:S(2)}, u32[]{:S(2)}) %collective-permute-start.9) | collective-permute-done | bytes 65568 | tf_op jit(solution)/shard_map/ppermute | solution.py:397
  28.1 3.3 %solve_near.1 = (f32[128,128]{1,0:T(8,128)S(1)}, f32[128,512]{1,0:T(8,128)S(1)}, f32[8,512]{1,0:T(8,128)S(1)}) custom-call(f32[32,512]{1,0:T(8,128)S(1)} %add_add_fusion.refs_0_, f32[32,512]{1,0:T(8,128)S(1)} %collective-permute-done.7.refs_1_, f32[32,512]{1,0:T(8,128)S(1)} %collective-permute-done.9.refs_2_, f32[32,512]{1,0:T(8,128)S(1)} %collective-permute-done.10.refs_3_, ...), custom_call_target="tpu_custom_call" | custom-call | flops 5000000000 | bytes 1 | tf_op jit(solution)/shard_map/solve_near/pallas_call | solution.py:263
  31.4 4.8 %solve.1.weights = f32[128,256]{1,0:T(8,128)S(1)} custom-call(f32[32,512]{1,0:T(8,128)S(1)} %add_add_fusion.refs_0_, f32[32,512]{1,0:T(8,128)S(1)} %collective-permute-done.7.refs_1_, f32[32,512]{1,0:T(8,128)S(1)} %collective-permute-done.9.refs_2_, f32[32,512]{1,0:T(8,128)S(1)} %collective-permute-done.10.refs_3_, ...), custom_call_target="tpu_custom_call" | custom-call | flops 5000000000 | bytes 1 | tf_op jit(solution)/shard_map/solve/pallas_call | solution.py:334
  36.2 1.5 %update.1 = f32[128,2048]{1,0:T(8,128)} custom-call(f32[128,256]{1,0:T(8,128)S(1)} %solve.1.weights, f32[128,2048]{1,0:T(8,128)S(1)} %copy-done, f32[128,256]{1,0:T(8,128)S(1)} %collective-permute-done.2.refs_0_, f32[128,768]{1,0:T(8,128)S(1)} %collective-permute-done.6.refs_1_, f32[128,256]{1,0:T(8,128)S(1)} %collective-permute-done.8.refs_2_, ...), custom_call_target="tpu_custom_call" | custom-call | flops 134217728 | bytes 3145728 | tf_op jit(solution)/shard_map/update/pallas_call | solution.py:375
  (29 shorter events, 0.2 us)
Async XLA Ops:
  0.0 3.7 %copy-start = (f32[128,2048]{1,0:T(8,128)S(1)}, f32[128,2048]{1,0:T(8,128)}, u32[]{:S(2)}) copy-start(f32[128,2048]{1,0:T(8,128)} %own_ens.1) | copy-start | bytes 3145732
  0.0 15.1 %copy-start.4 = (s32[512]{0:T(512)S(1)}, s32[512]{0:T(512)}, u32[]{:S(2)}) copy-start(s32[512]{0:T(512)} %param.11) | copy-start | bytes 6148
  0.0 15.1 %copy-start.3 = (f32[16384]{0:T(1024)S(1)}, f32[16384]{0:T(1024)}, u32[]{:S(2)}) copy-start(f32[16384]{0:T(1024)} %param.10) | copy-start | bytes 196612
  0.0 15.1 %copy-start.2 = (f32[16384]{0:T(1024)S(1)}, f32[16384]{0:T(1024)}, u32[]{:S(2)}) copy-start(f32[16384]{0:T(1024)} %param.9) | copy-start | bytes 196612
  0.0 15.1 %copy-start.1 = (f32[128,512]{1,0:T(8,128)S(1)}, f32[128,512]{1,0:T(8,128)}, u32[]{:S(2)}) copy-start(f32[128,512]{1,0:T(8,128)} %noise.1) | copy-start | bytes 786436
  3.1 3.1 %collective-permute-start = (f32[64,512]{1,0:T(8,128)S(1)}, f32[64,512]{1,0:T(8,128)S(1)}, u32[]{:S(2)}, u32[]{:S(2)}) collective-permute-start(f32[64,512]{1,0:T(8,128)S(1)} %get-tuple-element.27), channel_id=1, source_target_pairs={{0,1},{1,0},{2,3},{3,2},{4,5},{5,4},{6,7},{7,6},{8,9},{9,8},{10,11... | collective-permute-start | bytes 393224 | tf_op jit(solution)/shard_map/ppermute | solution.py:397
  3.7 6.7 %collective-permute-start.2 = (f32[128,256]{1,0:T(8,128)S(1)}, f32[128,256]{1,0:T(8,128)S(1)}, u32[]{:S(2)}, u32[]{:S(2)}) collective-permute-start(f32[128,256]{1,0:T(8,128)S(1)} %get-tuple-element.50), channel_id=1, source_target_pairs={{0,16},{1,17},{2,18},{3,19},{4,20},{5,21},{6,22},{7,23},{8,24},{9,... | collective-permute-start | bytes 393224 | tf_op jit(solution)/shard_map/ppermute | solution.py:397
  6.3 4.3 %collective-permute-start.1 = (f32[32,512]{1,0:T(8,128)S(1)}, f32[32,512]{1,0:T(8,128)S(1)}, u32[]{:S(2)}, u32[]{:S(2)}) collective-permute-start(f32[32,512]{1,0:T(8,128)S(1)} %constant_dynamic-slice_fusion), channel_id=1, source_target_pairs={{0,2},{1,3},{2,0},{3,1},{4,6},{5,7},{6,4},{7,5},{8,10},{9,11},{10,... | collective-permute-start | bytes 196616 | tf_op jit(solution)/shard_map/ppermute | solution.py:397
  8.0 12.1 %collective-permute-start.6 = (f32[128,768]{1,0:T(8,128)S(1)}, f32[128,768]{1,0:T(8,128)S(1)}, u32[]{:S(2)}, u32[]{:S(2)}) collective-permute-start(f32[128,768]{1,0:T(8,128)S(1)} %get-tuple-element.48), channel_id=1, source_target_pairs={{0,16},{1,17},{2,18},{3,19},{4,20},{5,21},{6,22},{7,23},{8,24},{9,... | collective-permute-start | bytes 1179656 | tf_op jit(solution)/shard_map/ppermute | solution.py:397
  10.6 7.1 %collective-permute-start.5 = (f32[32,512]{1,0:T(8,128)S(1)}, f32[32,512]{1,0:T(8,128)S(1)}, u32[]{:S(2)}, u32[]{:S(2)}) collective-permute-start(f32[32,512]{1,0:T(8,128)S(1)} %dynamic-slice_add_fusion), channel_id=1, source_target_pairs={{0,12},{1,13},{2,14},{3,15},{4,8},{5,9},{6,10},{7,11},{8,4},{9,5},... | collective-permute-start | bytes 196616 | tf_op jit(solution)/shard_map/ppermute | solution.py:397
  14.4 5.5 %collective-permute-start.4 = (f32[32,512]{1,0:T(8,128)S(1)}, f32[32,512]{1,0:T(8,128)S(1)}, u32[]{:S(2)}, u32[]{:S(2)}) collective-permute-start(f32[32,512]{1,0:T(8,128)S(1)} %dynamic-slice_add_fusion), channel_id=1, source_target_pairs={{0,8},{1,9},{2,10},{3,11},{4,12},{5,13},{6,14},{7,15},{8,0},{9,1},... | collective-permute-start | bytes 196616 | tf_op jit(solution)/shard_map/ppermute | solution.py:397
  14.4 5.5 %collective-permute-start.3 = (f32[32,512]{1,0:T(8,128)S(1)}, f32[32,512]{1,0:T(8,128)S(1)}, u32[]{:S(2)}, u32[]{:S(2)}) collective-permute-start(f32[32,512]{1,0:T(8,128)S(1)} %dynamic-slice_add_fusion), channel_id=1, source_target_pairs={{0,4},{1,5},{2,6},{3,7},{4,0},{5,1},{6,2},{7,3},{8,12},{9,13},{10,... | collective-permute-start | bytes 196616 | tf_op jit(solution)/shard_map/ppermute | solution.py:397
  15.8 9.2 %collective-permute-start.8 = (f32[128,256]{1,0:T(8,128)S(1)}, f32[128,256]{1,0:T(8,128)S(1)}, u32[]{:S(2)}, u32[]{:S(2)}) collective-permute-start(f32[128,256]{1,0:T(8,128)S(1)} %get-tuple-element.35), channel_id=1, source_target_pairs={{0,16},{1,17},{2,18},{3,19},{4,20},{5,21},{6,22},{7,23},{8,24},{9,... | collective-permute-start | bytes 393224 | tf_op jit(solution)/shard_map/ppermute | solution.py:397
  20.0 5.0 %collective-permute-start.7 = (f32[32,512]{1,0:T(8,128)S(1)}, f32[32,512]{1,0:T(8,128)S(1)}, u32[]{:S(2)}, u32[]{:S(2)}) collective-permute-start(f32[32,512]{1,0:T(8,128)S(1)} %add_add_fusion.refs_0_), channel_id=1, source_target_pairs={{0,2},{1,3},{2,0},{3,1},{4,6},{5,7},{6,4},{7,5},{8,10},{9,11},{10,... | collective-permute-start | bytes 196616 | tf_op jit(solution)/shard_map/ppermute | solution.py:397
  21.6 5.9 %collective-permute-start.10 = (f32[32,512]{1,0:T(8,128)S(1)}, f32[32,512]{1,0:T(8,128)S(1)}, u32[]{:S(2)}, u32[]{:S(2)}) collective-permute-start(f32[32,512]{1,0:T(8,128)S(1)} %add_add_fusion.refs_0_), channel_id=1, source_target_pairs={{0,18},{1,19},{2,16},{3,17},{4,22},{5,23},{6,20},{7,21},{8,26},{9,... | collective-permute-start | bytes 196616 | tf_op jit(solution)/shard_map/ppermute | solution.py:397
  23.0 5.0 %collective-permute-start.9 = (f32[32,512]{1,0:T(8,128)S(1)}, f32[32,512]{1,0:T(8,128)S(1)}, u32[]{:S(2)}, u32[]{:S(2)}) collective-permute-start(f32[32,512]{1,0:T(8,128)S(1)} %add_add_fusion.refs_0_), channel_id=1, source_target_pairs={{0,16},{1,17},{2,18},{3,19},{4,20},{5,21},{6,22},{7,23},{8,24},{9,... | collective-permute-start | bytes 196616 | tf_op jit(solution)/shard_map/ppermute | solution.py:397
  23.6 12.6 %collective-permute-start.15 = (f32[128,768]{1,0:T(8,128)S(1)}, f32[128,768]{1,0:T(8,128)S(1)}, u32[]{:S(2)}, u32[]{:S(2)}) collective-permute-start(f32[128,768]{1,0:T(8,128)S(1)} %get-tuple-element.46), channel_id=1, source_target_pairs={{0,16},{1,17},{2,18},{3,19},{4,20},{5,21},{6,22},{7,23},{8,24},{9,... | collective-permute-start | bytes 1179656 | tf_op jit(solution)/shard_map/ppermute | solution.py:397
  25.1 6.3 %collective-permute-start.11 = (f32[32,512]{1,0:T(8,128)S(1)}, f32[32,512]{1,0:T(8,128)S(1)}, u32[]{:S(2)}, u32[]{:S(2)}) collective-permute-start(f32[32,512]{1,0:T(8,128)S(1)} %add_add_fusion.refs_0_), channel_id=1, source_target_pairs={{0,1},{1,0},{2,3},{3,2},{4,5},{5,4},{6,7},{7,6},{8,9},{9,8},{10,11... | collective-permute-start | bytes 196616 | tf_op jit(solution)/shard_map/ppermute | solution.py:397
  25.1 6.3 %collective-permute-start.12 = (f32[32,512]{1,0:T(8,128)S(1)}, f32[32,512]{1,0:T(8,128)S(1)}, u32[]{:S(2)}, u32[]{:S(2)}) collective-permute-start(f32[32,512]{1,0:T(8,128)S(1)} %collective-permute-done.7.refs_1_), channel_id=1, source_target_pairs={{0,1},{1,0},{2,3},{3,2},{4,5},{5,4},{6,7},{7,6},{8,9},{9,8},{10,11... | collective-permute-start | bytes 196616 | tf_op jit(solution)/shard_map/ppermute | solution.py:397
  27.5 3.9 %collective-permute-start.14 = (f32[32,512]{1,0:T(8,128)S(1)}, f32[32,512]{1,0:T(8,128)S(1)}, u32[]{:S(2)}, u32[]{:S(2)}) collective-permute-start(f32[32,512]{1,0:T(8,128)S(1)} %collective-permute-done.10.refs_3_), channel_id=1, source_target_pairs={{0,1},{1,0},{2,3},{3,2},{4,5},{5,4},{6,7},{7,6},{8,9},{9,8},{10,11... | collective-permute-start | bytes 196616 | tf_op jit(solution)/shard_map/ppermute | solution.py:397
  28.1 3.3 %collective-permute-start.13 = (f32[32,512]{1,0:T(8,128)S(1)}, f32[32,512]{1,0:T(8,128)S(1)}, u32[]{:S(2)}, u32[]{:S(2)}) collective-permute-start(f32[32,512]{1,0:T(8,128)S(1)} %collective-permute-done.9.refs_2_), channel_id=1, source_target_pairs={{0,1},{1,0},{2,3},{3,2},{4,5},{5,4},{6,7},{7,6},{8,9},{9,8},{10,11... | collective-permute-start | bytes 196616 | tf_op jit(solution)/shard_map/ppermute | solution.py:397

commit v9 on v8

--- a/solution.py
+++ b/solution.py
@@ -11,11 +11,13 @@
 HIGHEST = lax.Precision.HIGHEST
 SUB, LANE = 8, 128
 BUF_ROWS = 2 * SUB * SUB + SUB
+FAR_ROWS = 4
 VMEM = pl.BlockSpec(memory_space=pltpu.VMEM)
 HBM = pl.BlockSpec(memory_space=pltpu.HBM)
 VMEM_LIMIT = 20 << 20
-PARTS = 8
-CUTS = (0, 1, 4, 5, 8)
+PARTS = 16
+CUTS = (0, 1, 7, 9, 16)
+STEP = 2
 
 
 def dot(a, b, dims, precision=HIGHEST):
@@ -100,11 +102,18 @@
                 old[i] - add_all(get(square + SUB * k + i) * outs[1][k] for k in range(SUB)) for i in range(SUB)
             ]
             m[j + 1] = jnp.where(here, 0.0, m[j + 1]) - add_all(side[k] * new[k] for k in range(SUB))
-        for i in range(j + 2, n):
-            m[i] = jnp.where(here, 0.0, m[i]) - add_all(across(m[i], at + k) * new[k] for k in range(SUB))
         done = new[0]
         for i in range(1, SUB):
             done = jnp.where(sub == i, new[i], done)
+        far = j + 3 if n - j - 3 >= FAR_ROWS else n
+        for i in range(j + 2, min(far, n)):
+            m[i] = jnp.where(here, 0.0, m[i]) - add_all(across(m[i], at + k) * new[k] for k in range(SUB))
+        if far < n:
+            blank = lambda count: [jnp.zeros((count, size), f32)] if count else []
+            rows = jnp.concatenate(blank(at) + [done] + blank(size - at - SUB), axis=0)
+            drop = dot3(jnp.concatenate(m[far:], axis=0), rows, ((1,), (0,)))
+            for i in range(far, n):
+                m[i] = jnp.where(here, 0.0, m[i]) - drop[SUB * (i - far) : SUB * (i - far + 1), :]
         keep = lane < at + SUB
         low.append(jnp.where(keep, row, 0.0))
         scaled.append(jnp.where(keep, done, 0.0))
@@ -357,9 +366,11 @@
     w_high, w_low = halves(weights[...])
     copies = []
     for part in range(parts):
-        for i in range(CUTS[part], CUTS[part + 1]):
-            cols = slice(i * width, (i + 1) * width)
-            at = slice((i - CUTS[part]) * width, (i - CUTS[part] + 1) * width)
+        first, end = CUTS[part : part + 2]
+        for i in range(first, end, STEP):
+            last = min(i + STEP, end)
+            cols = slice(i * width, last * width)
+            at = slice((i - first) * width, (last - first) * width)
             held = [own_ens[:, cols]] + [ref[:, at] for ref in others[part::parts]]
             high, low = halves(jnp.concatenate(held, axis=0))
             change = matmul(w_high, high) + (matmul(w_high, low) + matmul(w_low, high))

time: 37.9 us -> 37.5 us (0.989)
  starting transfers between devices: 18 us -> 17.1 us
  waiting for transfers between devices: 6.11 us -> 6.82 us
    ppermute x16, starting transfers between devices: 18 us -> 17.1 us  [swap(): return lax.ppermute(x, ('mem', 'par'), pairs)]
    ppermute x16, waiting for transfers between devices: 6.11 us -> 6.82 us  [swap(): return lax.ppermute(x, ('mem', 'par'), pairs)]
  transfers between devices with their start and end apart: 16 -> 16, of which waited for: 7 -> 5; matrix products, arithmetic and copies ran while one was open for 0% -> 0% of each run, Pallas kernels for 23% -> 23%
where the time goes in v9:
time: 37.5 us; the launch traced here: 37.3 us
  starting transfers between devices  17.1 us (46%)
  Pallas kernels  13.1 us (35%)
  waiting for transfers between devices  6.82 us (18%)
    ppermute x16, starting transfers between devices, swap(): return lax.ppermute(x, ('mem', 'par'), pairs)  17.1 us
    ppermute x16, waiting for transfers between devices, swap(): return lax.ppermute(x, ('mem', 'par'), pairs)  6.82 us
    pallas_call x1, Pallas kernels, solve(): pl.pallas_call(functools.partial(solve_kernel, places), out_shape=jax.Sha...  4.65 us
    pallas_call x1, Pallas kernels, solve_near(): pl.pallas_call(functools.partial(near_kernel, members, len(pieces)), out_...  3.11 us
    pallas_call x1, Pallas kernels, forward(): pl.pallas_call(functools.partial(forward_kernel, steps), out_shape=(half,...  3.1 us
    pallas_call x1, Pallas kernels, update(): pl.pallas_call(update_kernel, out_shape=jax.ShapeDtypeStruct((own, params...  1.55 us
  transfers between devices with their start and end apart: 16, of which 5 were waited for; matrix products, arithmetic and copies ran while one was open for 0% of the time, Pallas kernels for 23%

profile of v9, /device:TPU:0, one launch (start us, length us, event | category | flops | bytes accessed | tf_op | source)
XLA Modules:
  0.0 37.3 jit_solution(13996607897185597327)
XLA Ops:
  0.0 3.1 %forward.1 = (f32[64,512]{1,0:T(8,128)S(1)}, f32[64,512]{1,0:T(8,128)S(1)}) custom-call(f32[128,2048]{1,0:T(8,128)} %own_ens.1, f32[2048,512]{1,0:T(8,128)} %op.1), custom_call_target="tpu_custom_call" | custom-call | flops 268435456 | bytes 5242880 | tf_op jit(solution)/shard_map/forward/pallas_call | solution.py:187
  3.1 0.5 %collective-permute-start = (f32[64,512]{1,0:T(8,128)S(1)}, f32[64,512]{1,0:T(8,128)S(1)}, u32[]{:S(2)}, u32[]{:S(2)}) collective-permute-start(f32[64,512]{1,0:T(8,128)S(1)} %get-tuple-element.27), channel_id=1, source_target_pairs={{0,1},{1,0},{2,3},{3,2},{4,5},{5,4},{6,7},{7,6},{8,9},{9,8},{10,11... | collective-permute-start | bytes 393224 | tf_op jit(solution)/shard_map/ppermute | solution.py:408
  3.7 2.6 %collective-permute-start.2 = (f32[128,128]{1,0:T(8,128)S(1)}, f32[128,128]{1,0:T(8,128)S(1)}, u32[]{:S(2)}, u32[]{:S(2)}) collective-permute-start(f32[128,128]{1,0:T(8,128)S(1)} %slice.12), channel_id=1, source_target_pairs={{0,16},{1,17},{2,18},{3,19},{4,20},{5,21},{6,22},{7,23},{8,24},{9,... | collective-permute-start | bytes 196616 | tf_op jit(solution)/shard_map/ppermute | solution.py:408
  6.2 0.0 collective-permute-done
  6.3 1.6 %collective-permute-start.1 = (f32[32,512]{1,0:T(8,128)S(1)}, f32[32,512]{1,0:T(8,128)S(1)}, u32[]{:S(2)}, u32[]{:S(2)}) collective-permute-start(f32[32,512]{1,0:T(8,128)S(1)} %constant_dynamic-slice_fusion), channel_id=1, source_target_pairs={{0,2},{1,3},{2,0},{3,1},{4,6},{5,7},{6,4},{7,5},{8,10},{9,11},{10,... | collective-permute-start | bytes 196616 | tf_op jit(solution)/shard_map/ppermute | solution.py:408
  7.9 1.3 %collective-permute-start.6 = (f32[128,768]{1,0:T(8,128)S(1)}, f32[128,768]{1,0:T(8,128)S(1)}, u32[]{:S(2)}, u32[]{:S(2)}) collective-permute-start(f32[128,768]{1,0:T(8,128)S(1)} %slice.13), channel_id=1, source_target_pairs={{0,16},{1,17},{2,18},{3,19},{4,20},{5,21},{6,22},{7,23},{8,24},{9,... | collective-permute-start | bytes 1179656 | tf_op jit(solution)/shard_map/ppermute | solution.py:408
  9.2 1.4 %collective-permute-done.1 = f32[32,512]{1,0:T(8,128)S(1)} collective-permute-done((f32[32,512]{1,0:T(8,128)S(1)}, f32[32,512]{1,0:T(8,128)S(1)}, u32[]{:S(2)}, u32[]{:S(2)}) %collective-permute-start.1) | collective-permute-done | bytes 65568 | tf_op jit(solution)/shard_map/ppermute | solution.py:408
  10.6 3.7 %collective-permute-start.5 = (f32[32,512]{1,0:T(8,128)S(1)}, f32[32,512]{1,0:T(8,128)S(1)}, u32[]{:S(2)}, u32[]{:S(2)}) collective-permute-start(f32[32,512]{1,0:T(8,128)S(1)} %dynamic-slice_add_fusion), channel_id=1, source_target_pairs={{0,12},{1,13},{2,14},{3,15},{4,8},{5,9},{6,10},{7,11},{8,4},{9,5},... | collective-permute-start | bytes 196616 | tf_op jit(solution)/shard_map/ppermute | solution.py:408
  14.3 0.0 collective-permute-start.4
  14.3 0.8 %collective-permute-start.3 = (f32[32,512]{1,0:T(8,128)S(1)}, f32[32,512]{1,0:T(8,128)S(1)}, u32[]{:S(2)}, u32[]{:S(2)}) collective-permute-start(f32[32,512]{1,0:T(8,128)S(1)} %dynamic-slice_add_fusion), channel_id=1, source_target_pairs={{0,4},{1,5},{2,6},{3,7},{4,0},{5,1},{6,2},{7,3},{8,12},{9,13},{10,... | collective-permute-start | bytes 196616 | tf_op jit(solution)/shard_map/ppermute | solution.py:408
  15.1 0.7 %lookup.1 = (f32[128,512]{1,0:T(8,128)S(1)}, f32[8,512]{1,0:T(8,128)S(1)}) custom-call(s32[1,512]{1,0:T(1,128)S(1)} %bitcast.5, f32[128,128]{1,0:T(8,128)S(1)} %bitcast.3, f32[128,128]{1,0:T(8,128)S(1)} %bitcast.4, f32[128,512]{1,0:T(8,128)S(1)} %copy-done.1), custom_call_target="tpu_custom_call" | custom-call | flops 25769803776 | bytes 1048576 | tf_op jit(solution)/shard_map/lookup/pallas_call | solution.py:222
  15.8 1.3 %collective-permute-start.8 = (f32[128,256]{1,0:T(8,128)S(1)}, f32[128,256]{1,0:T(8,128)S(1)}, u32[]{:S(2)}, u32[]{:S(2)}) collective-permute-start(f32[128,256]{1,0:T(8,128)S(1)} %slice.14), channel_id=1, source_target_pairs={{0,16},{1,17},{2,18},{3,19},{4,20},{5,21},{6,22},{7,23},{8,24},{9,... | collective-permute-start | bytes 393224 | tf_op jit(solution)/shard_map/ppermute | solution.py:408
  17.1 2.5 %collective-permute-done.4 = f32[32,512]{1,0:T(8,128)S(1)} collective-permute-done((f32[32,512]{1,0:T(8,128)S(1)}, f32[32,512]{1,0:T(8,128)S(1)}, u32[]{:S(2)}, u32[]{:S(2)}) %collective-permute-start.4) | collective-permute-done | bytes 65568 | tf_op jit(solution)/shard_map/ppermute | solution.py:408
  19.7 0.3 collective-permute-done.6.refs_1_
  20.0 1.3 %collective-permute-start.7 = (f32[32,512]{1,0:T(8,128)S(1)}, f32[32,512]{1,0:T(8,128)S(1)}, u32[]{:S(2)}, u32[]{:S(2)}) collective-permute-start(f32[32,512]{1,0:T(8,128)S(1)} %add_add_fusion.refs_0_), channel_id=1, source_target_pairs={{0,2},{1,3},{2,0},{3,1},{4,6},{5,7},{6,4},{7,5},{8,10},{9,11},{10,... | collective-permute-start | bytes 196616 | tf_op jit(solution)/shard_map/ppermute | solution.py:408
  21.3 1.5 %collective-permute-start.10 = (f32[32,512]{1,0:T(8,128)S(1)}, f32[32,512]{1,0:T(8,128)S(1)}, u32[]{:S(2)}, u32[]{:S(2)}) collective-permute-start(f32[32,512]{1,0:T(8,128)S(1)} %add_add_fusion.refs_0_), channel_id=1, source_target_pairs={{0,18},{1,19},{2,16},{3,17},{4,22},{5,23},{6,20},{7,21},{8,26},{9,... | collective-permute-start | bytes 196616 | tf_op jit(solution)/shard_map/ppermute | solution.py:408
  22.8 0.8 %collective-permute-start.9 = (f32[32,512]{1,0:T(8,128)S(1)}, f32[32,512]{1,0:T(8,128)S(1)}, u32[]{:S(2)}, u32[]{:S(2)}) collective-permute-start(f32[32,512]{1,0:T(8,128)S(1)} %add_add_fusion.refs_0_), channel_id=1, source_target_pairs={{0,16},{1,17},{2,18},{3,19},{4,20},{5,21},{6,22},{7,23},{8,24},{9,... | collective-permute-start | bytes 196616 | tf_op jit(solution)/shard_map/ppermute | solution.py:408
  23.6 1.3 %collective-permute-start.15 = (f32[128,896]{1,0:T(8,128)S(1)}, f32[128,896]{1,0:T(8,128)S(1)}, u32[]{:S(2)}, u32[]{:S(2)}) collective-permute-start(f32[128,896]{1,0:T(8,128)S(1)} %slice.15), channel_id=1, source_target_pairs={{0,16},{1,17},{2,18},{3,19},{4,20},{5,21},{6,22},{7,23},{8,24},{9,... | collective-permute-start | bytes 1376264 | tf_op jit(solution)/shard_map/ppermute | solution.py:408
  24.9 0.5 %collective-permute-start.12 = (f32[32,512]{1,0:T(8,128)S(1)}, f32[32,512]{1,0:T(8,128)S(1)}, u32[]{:S(2)}, u32[]{:S(2)}) collective-permute-start(f32[32,512]{1,0:T(8,128)S(1)} %collective-permute-done.7.refs_1_), channel_id=1, source_target_pairs={{0,1},{1,0},{2,3},{3,2},{4,5},{5,4},{6,7},{7,6},{8,9},{9,8},{10,11... | collective-permute-start | bytes 196616 | tf_op jit(solution)/shard_map/ppermute | solution.py:408
  25.4 1.8 %collective-permute-done.10.refs_3_ = f32[32,512]{1,0:T(8,128)S(1)} collective-permute-done((f32[32,512]{1,0:T(8,128)S(1)}, f32[32,512]{1,0:T(8,128)S(1)}, u32[]{:S(2)}, u32[]{:S(2)}) %collective-permute-start.10) | collective-permute-done | bytes 65568 | tf_op jit(solution)/shard_map/ppermute | solution.py:408
  27.2 0.8 %collective-permute-done.9.refs_2_ = f32[32,512]{1,0:T(8,128)S(1)} collective-permute-done((f32[32,512]{1,0:T(8,128)S(1)}, f32[32,512]{1,0:T(8,128)S(1)}, u32[]{:S(2)}, u32[]{:S(2)}) %collective-permute-start.9) | collective-permute-done | bytes 65568 | tf_op jit(solution)/shard_map/ppermute | solution.py:408
  28.0 3.1 %solve_near.1 = (f32[128,128]{1,0:T(8,128)S(1)}, f32[128,512]{1,0:T(8,128)S(1)}, f32[8,512]{1,0:T(8,128)S(1)}) custom-call(f32[32,512]{1,0:T(8,128)S(1)} %add_add_fusion.refs_0_, f32[32,512]{1,0:T(8,128)S(1)} %collective-permute-done.7.refs_1_, f32[32,512]{1,0:T(8,128)S(1)} %collective-permute-done.9.refs_2_, f32[32,512]{1,0:T(8,128)S(1)} %collective-permute-done.10.refs_3_, ...), custom_call_target="tpu_custom_call" | custom-call | flops 5000000000 | bytes 1 | tf_op jit(solution)/shard_map/solve_near/pallas_call | solution.py:272
  31.1 4.6 %solve.1.weights = f32[128,256]{1,0:T(8,128)S(1)} custom-call(f32[32,512]{1,0:T(8,128)S(1)} %add_add_fusion.refs_0_, f32[32,512]{1,0:T(8,128)S(1)} %collective-permute-done.7.refs_1_, f32[32,512]{1,0:T(8,128)S(1)} %collective-permute-done.9.refs_2_, f32[32,512]{1,0:T(8,128)S(1)} %collective-permute-done.10.refs_3_, ...), custom_call_target="tpu_custom_call" | custom-call | flops 5000000000 | bytes 1 | tf_op jit(solution)/shard_map/solve/pallas_call | solution.py:343
  35.8 1.5 %update.1 = f32[128,2048]{1,0:T(8,128)} custom-call(f32[128,256]{1,0:T(8,128)S(1)} %solve.1.weights, f32[128,2048]{1,0:T(8,128)S(1)} %copy-done, f32[128,128]{1,0:T(8,128)S(1)} %collective-permute-done.2.refs_0_, f32[128,768]{1,0:T(8,128)S(1)} %collective-permute-done.6.refs_1_, f32[128,256]{1,0:T(8,128)S(1)} %collective-permute-done.8.refs_2_, ...), custom_call_target="tpu_custom_call" | custom-call | flops 134217728 | bytes 3145728 | tf_op jit(solution)/shard_map/update/pallas_call | solution.py:386
  (31 shorter events, 0.2 us)
Async XLA Ops:
  0.0 3.7 %copy-start = (f32[128,2048]{1,0:T(8,128)S(1)}, f32[128,2048]{1,0:T(8,128)}, u32[]{:S(2)}) copy-start(f32[128,2048]{1,0:T(8,128)} %own_ens.1) | copy-start | bytes 3145732
  0.0 15.1 %copy-start.4 = (s32[512]{0:T(512)S(1)}, s32[512]{0:T(512)}, u32[]{:S(2)}) copy-start(s32[512]{0:T(512)} %param.11) | copy-start | bytes 6148
  0.0 15.1 %copy-start.3 = (f32[16384]{0:T(1024)S(1)}, f32[16384]{0:T(1024)}, u32[]{:S(2)}) copy-start(f32[16384]{0:T(1024)} %param.10) | copy-start | bytes 196612
  0.0 15.1 %copy-start.2 = (f32[16384]{0:T(1024)S(1)}, f32[16384]{0:T(1024)}, u32[]{:S(2)}) copy-start(f32[16384]{0:T(1024)} %param.9) | copy-start | bytes 196612
  0.0 15.1 %copy-start.1 = (f32[128,512]{1,0:T(8,128)S(1)}, f32[128,512]{1,0:T(8,128)}, u32[]{:S(2)}) copy-start(f32[128,512]{1,0:T(8,128)} %noise.1) | copy-start | bytes 786436
  3.1 3.1 %collective-permute-start = (f32[64,512]{1,0:T(8,128)S(1)}, f32[64,512]{1,0:T(8,128)S(1)}, u32[]{:S(2)}, u32[]{:S(2)}) collective-permute-start(f32[64,512]{1,0:T(8,128)S(1)} %get-tuple-element.27), channel_id=1, source_target_pairs={{0,1},{1,0},{2,3},{3,2},{4,5},{5,4},{6,7},{7,6},{8,9},{9,8},{10,11... | collective-permute-start | bytes 393224 | tf_op jit(solution)/shard_map/ppermute | solution.py:408
  3.7 5.6 %collective-permute-start.2 = (f32[128,128]{1,0:T(8,128)S(1)}, f32[128,128]{1,0:T(8,128)S(1)}, u32[]{:S(2)}, u32[]{:S(2)}) collective-permute-start(f32[128,128]{1,0:T(8,128)S(1)} %slice.12), channel_id=1, source_target_pairs={{0,16},{1,17},{2,18},{3,19},{4,20},{5,21},{6,22},{7,23},{8,24},{9,... | collective-permute-start | bytes 196616 | tf_op jit(solution)/shard_map/ppermute | solution.py:408
  6.3 4.3 %collective-permute-start.1 = (f32[32,512]{1,0:T(8,128)S(1)}, f32[32,512]{1,0:T(8,128)S(1)}, u32[]{:S(2)}, u32[]{:S(2)}) collective-permute-start(f32[32,512]{1,0:T(8,128)S(1)} %constant_dynamic-slice_fusion), channel_id=1, source_target_pairs={{0,2},{1,3},{2,0},{3,1},{4,6},{5,7},{6,4},{7,5},{8,10},{9,11},{10,... | collective-permute-start | bytes 196616 | tf_op jit(solution)/shard_map/ppermute | solution.py:408
  7.9 12.1 %collective-permute-start.6 = (f32[128,768]{1,0:T(8,128)S(1)}, f32[128,768]{1,0:T(8,128)S(1)}, u32[]{:S(2)}, u32[]{:S(2)}) collective-permute-start(f32[128,768]{1,0:T(8,128)S(1)} %slice.13), channel_id=1, source_target_pairs={{0,16},{1,17},{2,18},{3,19},{4,20},{5,21},{6,22},{7,23},{8,24},{9,... | collective-permute-start | bytes 1179656 | tf_op jit(solution)/shard_map/ppermute | solution.py:408
  10.6 6.5 %collective-permute-start.5 = (f32[32,512]{1,0:T(8,128)S(1)}, f32[32,512]{1,0:T(8,128)S(1)}, u32[]{:S(2)}, u32[]{:S(2)}) collective-permute-start(f32[32,512]{1,0:T(8,128)S(1)} %dynamic-slice_add_fusion), channel_id=1, source_target_pairs={{0,12},{1,13},{2,14},{3,15},{4,8},{5,9},{6,10},{7,11},{8,4},{9,5},... | collective-permute-start | bytes 196616 | tf_op jit(solution)/shard_map/ppermute | solution.py:408
  14.3 5.4 %collective-permute-start.4 = (f32[32,512]{1,0:T(8,128)S(1)}, f32[32,512]{1,0:T(8,128)S(1)}, u32[]{:S(2)}, u32[]{:S(2)}) collective-permute-start(f32[32,512]{1,0:T(8,128)S(1)} %dynamic-slice_add_fusion), channel_id=1, source_target_pairs={{0,8},{1,9},{2,10},{3,11},{4,12},{5,13},{6,14},{7,15},{8,0},{9,1},... | collective-permute-start | bytes 196616 | tf_op jit(solution)/shard_map/ppermute | solution.py:408
  14.3 5.4 %collective-permute-start.3 = (f32[32,512]{1,0:T(8,128)S(1)}, f32[32,512]{1,0:T(8,128)S(1)}, u32[]{:S(2)}, u32[]{:S(2)}) collective-permute-start(f32[32,512]{1,0:T(8,128)S(1)} %dynamic-slice_add_fusion), channel_id=1, source_target_pairs={{0,4},{1,5},{2,6},{3,7},{4,0},{5,1},{6,2},{7,3},{8,12},{9,13},{10,... | collective-permute-start | bytes 196616 | tf_op jit(solution)/shard_map/ppermute | solution.py:408
  15.8 9.1 %collective-permute-start.8 = (f32[128,256]{1,0:T(8,128)S(1)}, f32[128,256]{1,0:T(8,128)S(1)}, u32[]{:S(2)}, u32[]{:S(2)}) collective-permute-start(f32[128,256]{1,0:T(8,128)S(1)} %slice.14), channel_id=1, source_target_pairs={{0,16},{1,17},{2,18},{3,19},{4,20},{5,21},{6,22},{7,23},{8,24},{9,... | collective-permute-start | bytes 393224 | tf_op jit(solution)/shard_map/ppermute | solution.py:408
  20.0 4.9 %collective-permute-start.7 = (f32[32,512]{1,0:T(8,128)S(1)}, f32[32,512]{1,0:T(8,128)S(1)}, u32[]{:S(2)}, u32[]{:S(2)}) collective-permute-start(f32[32,512]{1,0:T(8,128)S(1)} %add_add_fusion.refs_0_), channel_id=1, source_target_pairs={{0,2},{1,3},{2,0},{3,1},{4,6},{5,7},{6,4},{7,5},{8,10},{9,11},{10,... | collective-permute-start | bytes 196616 | tf_op jit(solution)/shard_map/ppermute | solution.py:408
  21.3 5.9 %collective-permute-start.10 = (f32[32,512]{1,0:T(8,128)S(1)}, f32[32,512]{1,0:T(8,128)S(1)}, u32[]{:S(2)}, u32[]{:S(2)}) collective-permute-start(f32[32,512]{1,0:T(8,128)S(1)} %add_add_fusion.refs_0_), channel_id=1, source_target_pairs={{0,18},{1,19},{2,16},{3,17},{4,22},{5,23},{6,20},{7,21},{8,26},{9,... | collective-permute-start | bytes 196616 | tf_op jit(solution)/shard_map/ppermute | solution.py:408
  22.8 5.2 %collective-permute-start.9 = (f32[32,512]{1,0:T(8,128)S(1)}, f32[32,512]{1,0:T(8,128)S(1)}, u32[]{:S(2)}, u32[]{:S(2)}) collective-permute-start(f32[32,512]{1,0:T(8,128)S(1)} %add_add_fusion.refs_0_), channel_id=1, source_target_pairs={{0,16},{1,17},{2,18},{3,19},{4,20},{5,21},{6,22},{7,23},{8,24},{9,... | collective-permute-start | bytes 196616 | tf_op jit(solution)/shard_map/ppermute | solution.py:408
  23.6 12.2 %collective-permute-start.15 = (f32[128,896]{1,0:T(8,128)S(1)}, f32[128,896]{1,0:T(8,128)S(1)}, u32[]{:S(2)}, u32[]{:S(2)}) collective-permute-start(f32[128,896]{1,0:T(8,128)S(1)} %slice.15), channel_id=1, source_target_pairs={{0,16},{1,17},{2,18},{3,19},{4,20},{5,21},{6,22},{7,23},{8,24},{9,... | collective-permute-start | bytes 1376264 | tf_op jit(solution)/shard_map/ppermute | solution.py:408
  24.9 6.2 %collective-permute-start.11 = (f32[32,512]{1,0:T(8,128)S(1)}, f32[32,512]{1,0:T(8,128)S(1)}, u32[]{:S(2)}, u32[]{:S(2)}) collective-permute-start(f32[32,512]{1,0:T(8,128)S(1)} %add_add_fusion.refs_0_), channel_id=1, source_target_pairs={{0,1},{1,0},{2,3},{3,2},{4,5},{5,4},{6,7},{7,6},{8,9},{9,8},{10,11... | collective-permute-start | bytes 196616 | tf_op jit(solution)/shard_map/ppermute | solution.py:408
  24.9 6.2 %collective-permute-start.12 = (f32[32,512]{1,0:T(8,128)S(1)}, f32[32,512]{1,0:T(8,128)S(1)}, u32[]{:S(2)}, u32[]{:S(2)}) collective-permute-start(f32[32,512]{1,0:T(8,128)S(1)} %collective-permute-done.7.refs_1_), channel_id=1, source_target_pairs={{0,1},{1,0},{2,3},{3,2},{4,5},{5,4},{6,7},{7,6},{8,9},{9,8},{10,11... | collective-permute-start | bytes 196616 | tf_op jit(solution)/shard_map/ppermute | solution.py:408
  27.2 3.9 %collective-permute-start.14 = (f32[32,512]{1,0:T(8,128)S(1)}, f32[32,512]{1,0:T(8,128)S(1)}, u32[]{:S(2)}, u32[]{:S(2)}) collective-permute-start(f32[32,512]{1,0:T(8,128)S(1)} %collective-permute-done.10.refs_3_), channel_id=1, source_target_pairs={{0,1},{1,0},{2,3},{3,2},{4,5},{5,4},{6,7},{7,6},{8,9},{9,8},{10,11... | collective-permute-start | bytes 196616 | tf_op jit(solution)/shard_map/ppermute | solution.py:408
  28.0 3.1 %collective-permute-start.13 = (f32[32,512]{1,0:T(8,128)S(1)}, f32[32,512]{1,0:T(8,128)S(1)}, u32[]{:S(2)}, u32[]{:S(2)}) collective-permute-start(f32[32,512]{1,0:T(8,128)S(1)} %collective-permute-done.9.refs_2_), channel_id=1, source_target_pairs={{0,1},{1,0},{2,3},{3,2},{4,5},{5,4},{6,7},{7,6},{8,9},{9,8},{10,11... | collective-permute-start | bytes 196616 | tf_op jit(solution)/shard_map/ppermute | solution.py:408

commit v10 on v9

--- a/solution.py
+++ b/solution.py
@@ -16,7 +16,7 @@
 HBM = pl.BlockSpec(memory_space=pltpu.HBM)
 VMEM_LIMIT = 20 << 20
 PARTS = 16
-CUTS = (0, 1, 7, 9, 16)
+CUTS = (0, 1, 6, 9, 16)
 STEP = 2
 
 

time: 37.5 us -> 37.2 us (level)
  transfers between devices with their start and end apart: 16 -> 16, of which waited for: 5 -> 4; matrix products, arithmetic and copies ran while one was open for 0% -> 0% of each run, Pallas kernels for 23% -> 23%
where the time goes in v10:
time: 37.2 us; the launch traced here: 37.1 us
  starting transfers between devices  17.2 us (46%)
  Pallas kernels  13.1 us (35%)
  waiting for transfers between devices  6.5 us (17%)
    ppermute x16, starting transfers between devices, swap(): return lax.ppermute(x, ('mem', 'par'), pairs)  17.2 us
    ppermute x16, waiting for transfers between devices, swap(): return lax.ppermute(x, ('mem', 'par'), pairs)  6.5 us
    pallas_call x1, Pallas kernels, solve(): pl.pallas_call(functools.partial(solve_kernel, places), out_shape=jax.Sha...  4.65 us
    pallas_call x1, Pallas kernels, solve_near(): pl.pallas_call(functools.partial(near_kernel, members, len(pieces)), out_...  3.11 us
    pallas_call x1, Pallas kernels, forward(): pl.pallas_call(functools.partial(forward_kernel, steps), out_shape=(half,...  3.1 us
    pallas_call x1, Pallas kernels, update(): pl.pallas_call(update_kernel, out_shape=jax.ShapeDtypeStruct((own, params...  1.55 us
  transfers between devices with their start and end apart: 16, of which 4 were waited for; matrix products, arithmetic and copies ran while one was open for 0% of the time, Pallas kernels for 23%

profile of v10, /device:TPU:0, one launch (start us, length us, event | category | flops | bytes accessed | tf_op | source)
XLA Modules:
  0.0 37.1 jit_solution(15163122199554316229)
XLA Ops:
  0.0 3.1 %forward.1 = (f32[64,512]{1,0:T(8,128)S(1)}, f32[64,512]{1,0:T(8,128)S(1)}) custom-call(f32[128,2048]{1,0:T(8,128)} %own_ens.1, f32[2048,512]{1,0:T(8,128)} %op.1), custom_call_target="tpu_custom_call" | custom-call | flops 268435456 | bytes 5242880 | tf_op jit(solution)/shard_map/forward/pallas_call | solution.py:187
  3.1 0.5 %collective-permute-start = (f32[64,512]{1,0:T(8,128)S(1)}, f32[64,512]{1,0:T(8,128)S(1)}, u32[]{:S(2)}, u32[]{:S(2)}) collective-permute-start(f32[64,512]{1,0:T(8,128)S(1)} %get-tuple-element.27), channel_id=1, source_target_pairs={{0,1},{1,0},{2,3},{3,2},{4,5},{5,4},{6,7},{7,6},{8,9},{9,8},{10,11... | collective-permute-start | bytes 393224 | tf_op jit(solution)/shard_map/ppermute | solution.py:408
  3.7 2.6 %collective-permute-start.2 = (f32[128,128]{1,0:T(8,128)S(1)}, f32[128,128]{1,0:T(8,128)S(1)}, u32[]{:S(2)}, u32[]{:S(2)}) collective-permute-start(f32[128,128]{1,0:T(8,128)S(1)} %slice.12), channel_id=1, source_target_pairs={{0,16},{1,17},{2,18},{3,19},{4,20},{5,21},{6,22},{7,23},{8,24},{9,... | collective-permute-start | bytes 196616 | tf_op jit(solution)/shard_map/ppermute | solution.py:408
  6.2 0.0 collective-permute-done
  6.3 1.6 %collective-permute-start.1 = (f32[32,512]{1,0:T(8,128)S(1)}, f32[32,512]{1,0:T(8,128)S(1)}, u32[]{:S(2)}, u32[]{:S(2)}) collective-permute-start(f32[32,512]{1,0:T(8,128)S(1)} %constant_dynamic-slice_fusion), channel_id=1, source_target_pairs={{0,2},{1,3},{2,0},{3,1},{4,6},{5,7},{6,4},{7,5},{8,10},{9,11},{10,... | collective-permute-start | bytes 196616 | tf_op jit(solution)/shard_map/ppermute | solution.py:408
  7.9 1.3 %collective-permute-start.6 = (f32[128,640]{1,0:T(8,128)S(1)}, f32[128,640]{1,0:T(8,128)S(1)}, u32[]{:S(2)}, u32[]{:S(2)}) collective-permute-start(f32[128,640]{1,0:T(8,128)S(1)} %slice.13), channel_id=1, source_target_pairs={{0,16},{1,17},{2,18},{3,19},{4,20},{5,21},{6,22},{7,23},{8,24},{9,... | collective-permute-start | bytes 983048 | tf_op jit(solution)/shard_map/ppermute | solution.py:408
  9.2 0.0 collective-permute-done.2.refs_0_
  9.2 1.4 %collective-permute-done.1 = f32[32,512]{1,0:T(8,128)S(1)} collective-permute-done((f32[32,512]{1,0:T(8,128)S(1)}, f32[32,512]{1,0:T(8,128)S(1)}, u32[]{:S(2)}, u32[]{:S(2)}) %collective-permute-start.1) | collective-permute-done | bytes 65568 | tf_op jit(solution)/shard_map/ppermute | solution.py:408
  10.6 3.7 %collective-permute-start.5 = (f32[32,512]{1,0:T(8,128)S(1)}, f32[32,512]{1,0:T(8,128)S(1)}, u32[]{:S(2)}, u32[]{:S(2)}) collective-permute-start(f32[32,512]{1,0:T(8,128)S(1)} %dynamic-slice_add_fusion), channel_id=1, source_target_pairs={{0,12},{1,13},{2,14},{3,15},{4,8},{5,9},{6,10},{7,11},{8,4},{9,5},... | collective-permute-start | bytes 196616 | tf_op jit(solution)/shard_map/ppermute | solution.py:408
  14.3 0.8 %collective-permute-start.3 = (f32[32,512]{1,0:T(8,128)S(1)}, f32[32,512]{1,0:T(8,128)S(1)}, u32[]{:S(2)}, u32[]{:S(2)}) collective-permute-start(f32[32,512]{1,0:T(8,128)S(1)} %dynamic-slice_add_fusion), channel_id=1, source_target_pairs={{0,4},{1,5},{2,6},{3,7},{4,0},{5,1},{6,2},{7,3},{8,12},{9,13},{10,... | collective-permute-start | bytes 196616 | tf_op jit(solution)/shard_map/ppermute | solution.py:408
  15.1 0.7 %lookup.1 = (f32[128,512]{1,0:T(8,128)S(1)}, f32[8,512]{1,0:T(8,128)S(1)}) custom-call(s32[1,512]{1,0:T(1,128)S(1)} %bitcast.5, f32[128,128]{1,0:T(8,128)S(1)} %bitcast.3, f32[128,128]{1,0:T(8,128)S(1)} %bitcast.4, f32[128,512]{1,0:T(8,128)S(1)} %copy-done.1), custom_call_target="tpu_custom_call" | custom-call | flops 25769803776 | bytes 1048576 | tf_op jit(solution)/shard_map/lookup/pallas_call | solution.py:222
  15.8 1.3 %collective-permute-start.8 = (f32[128,384]{1,0:T(8,128)S(1)}, f32[128,384]{1,0:T(8,128)S(1)}, u32[]{:S(2)}, u32[]{:S(2)}) collective-permute-start(f32[128,384]{1,0:T(8,128)S(1)} %slice.14), channel_id=1, source_target_pairs={{0,16},{1,17},{2,18},{3,19},{4,20},{5,21},{6,22},{7,23},{8,24},{9,... | collective-permute-start | bytes 589832 | tf_op jit(solution)/shard_map/ppermute | solution.py:408
  17.1 2.5 %collective-permute-done.4 = f32[32,512]{1,0:T(8,128)S(1)} collective-permute-done((f32[32,512]{1,0:T(8,128)S(1)}, f32[32,512]{1,0:T(8,128)S(1)}, u32[]{:S(2)}, u32[]{:S(2)}) %collective-permute-start.4) | collective-permute-done | bytes 65568 | tf_op jit(solution)/shard_map/ppermute | solution.py:408
  19.7 1.6 %collective-permute-start.7 = (f32[32,512]{1,0:T(8,128)S(1)}, f32[32,512]{1,0:T(8,128)S(1)}, u32[]{:S(2)}, u32[]{:S(2)}) collective-permute-start(f32[32,512]{1,0:T(8,128)S(1)} %add_add_fusion.refs_0_), channel_id=1, source_target_pairs={{0,2},{1,3},{2,0},{3,1},{4,6},{5,7},{6,4},{7,5},{8,10},{9,11},{10,... | collective-permute-start | bytes 196616 | tf_op jit(solution)/shard_map/ppermute | solution.py:408
  21.3 1.2 %collective-permute-start.10 = (f32[32,512]{1,0:T(8,128)S(1)}, f32[32,512]{1,0:T(8,128)S(1)}, u32[]{:S(2)}, u32[]{:S(2)}) collective-permute-start(f32[32,512]{1,0:T(8,128)S(1)} %add_add_fusion.refs_0_), channel_id=1, source_target_pairs={{0,18},{1,19},{2,16},{3,17},{4,22},{5,23},{6,20},{7,21},{8,26},{9,... | collective-permute-start | bytes 196616 | tf_op jit(solution)/shard_map/ppermute | solution.py:408
  22.5 0.8 %collective-permute-start.9 = (f32[32,512]{1,0:T(8,128)S(1)}, f32[32,512]{1,0:T(8,128)S(1)}, u32[]{:S(2)}, u32[]{:S(2)}) collective-permute-start(f32[32,512]{1,0:T(8,128)S(1)} %add_add_fusion.refs_0_), channel_id=1, source_target_pairs={{0,16},{1,17},{2,18},{3,19},{4,20},{5,21},{6,22},{7,23},{8,24},{9,... | collective-permute-start | bytes 196616 | tf_op jit(solution)/shard_map/ppermute | solution.py:408
  23.3 1.3 %collective-permute-start.15 = (f32[128,896]{1,0:T(8,128)S(1)}, f32[128,896]{1,0:T(8,128)S(1)}, u32[]{:S(2)}, u32[]{:S(2)}) collective-permute-start(f32[128,896]{1,0:T(8,128)S(1)} %slice.15), channel_id=1, source_target_pairs={{0,16},{1,17},{2,18},{3,19},{4,20},{5,21},{6,22},{7,23},{8,24},{9,... | collective-permute-start | bytes 1376264 | tf_op jit(solution)/shard_map/ppermute | solution.py:408
  24.6 0.5 %collective-permute-start.12 = (f32[32,512]{1,0:T(8,128)S(1)}, f32[32,512]{1,0:T(8,128)S(1)}, u32[]{:S(2)}, u32[]{:S(2)}) collective-permute-start(f32[32,512]{1,0:T(8,128)S(1)} %collective-permute-done.7.refs_1_), channel_id=1, source_target_pairs={{0,1},{1,0},{2,3},{3,2},{4,5},{5,4},{6,7},{7,6},{8,9},{9,8},{10,11... | collective-permute-start | bytes 196616 | tf_op jit(solution)/shard_map/ppermute | solution.py:408
  25.1 2.1 %collective-permute-done.10.refs_3_ = f32[32,512]{1,0:T(8,128)S(1)} collective-permute-done((f32[32,512]{1,0:T(8,128)S(1)}, f32[32,512]{1,0:T(8,128)S(1)}, u32[]{:S(2)}, u32[]{:S(2)}) %collective-permute-start.10) | collective-permute-done | bytes 65568 | tf_op jit(solution)/shard_map/ppermute | solution.py:408
  27.2 0.4 %collective-permute-done.9.refs_2_ = f32[32,512]{1,0:T(8,128)S(1)} collective-permute-done((f32[32,512]{1,0:T(8,128)S(1)}, f32[32,512]{1,0:T(8,128)S(1)}, u32[]{:S(2)}, u32[]{:S(2)}) %collective-permute-start.9) | collective-permute-done | bytes 65568 | tf_op jit(solution)/shard_map/ppermute | solution.py:408
  27.7 0.1 collective-permute-start.13
  27.7 3.1 %solve_near.1 = (f32[128,128]{1,0:T(8,128)S(1)}, f32[128,512]{1,0:T(8,128)S(1)}, f32[8,512]{1,0:T(8,128)S(1)}) custom-call(f32[32,512]{1,0:T(8,128)S(1)} %add_add_fusion.refs_0_, f32[32,512]{1,0:T(8,128)S(1)} %collective-permute-done.7.refs_1_, f32[32,512]{1,0:T(8,128)S(1)} %collective-permute-done.9.refs_2_, f32[32,512]{1,0:T(8,128)S(1)} %collective-permute-done.10.refs_3_, ...), custom_call_target="tpu_custom_call" | custom-call | flops 5000000000 | bytes 1 | tf_op jit(solution)/shard_map/solve_near/pallas_call | solution.py:272
  30.9 4.7 %solve.1.weights = f32[128,256]{1,0:T(8,128)S(1)} custom-call(f32[32,512]{1,0:T(8,128)S(1)} %add_add_fusion.refs_0_, f32[32,512]{1,0:T(8,128)S(1)} %collective-permute-done.7.refs_1_, f32[32,512]{1,0:T(8,128)S(1)} %collective-permute-done.9.refs_2_, f32[32,512]{1,0:T(8,128)S(1)} %collective-permute-done.10.refs_3_, ...), custom_call_target="tpu_custom_call" | custom-call | flops 5000000000 | bytes 1 | tf_op jit(solution)/shard_map/solve/pallas_call | solution.py:343
  35.5 1.5 %update.1 = f32[128,2048]{1,0:T(8,128)} custom-call(f32[128,256]{1,0:T(8,128)S(1)} %solve.1.weights, f32[128,2048]{1,0:T(8,128)S(1)} %copy-done, f32[128,128]{1,0:T(8,128)S(1)} %collective-permute-done.2.refs_0_, f32[128,640]{1,0:T(8,128)S(1)} %collective-permute-done.6.refs_1_, f32[128,384]{1,0:T(8,128)S(1)} %collective-permute-done.8.refs_2_, ...), custom_call_target="tpu_custom_call" | custom-call | flops 134217728 | bytes 3145728 | tf_op jit(solution)/shard_map/update/pallas_call | solution.py:386
  (31 shorter events, 0.2 us)
Async XLA Ops:
  0.0 3.7 %copy-start = (f32[128,2048]{1,0:T(8,128)S(1)}, f32[128,2048]{1,0:T(8,128)}, u32[]{:S(2)}) copy-start(f32[128,2048]{1,0:T(8,128)} %own_ens.1) | copy-start | bytes 3145732
  0.0 15.1 %copy-start.4 = (s32[512]{0:T(512)S(1)}, s32[512]{0:T(512)}, u32[]{:S(2)}) copy-start(s32[512]{0:T(512)} %param.11) | copy-start | bytes 6148
  0.0 15.1 %copy-start.3 = (f32[16384]{0:T(1024)S(1)}, f32[16384]{0:T(1024)}, u32[]{:S(2)}) copy-start(f32[16384]{0:T(1024)} %param.10) | copy-start | bytes 196612
  0.0 15.1 %copy-start.2 = (f32[16384]{0:T(1024)S(1)}, f32[16384]{0:T(1024)}, u32[]{:S(2)}) copy-start(f32[16384]{0:T(1024)} %param.9) | copy-start | bytes 196612
  0.0 15.1 %copy-start.1 = (f32[128,512]{1,0:T(8,128)S(1)}, f32[128,512]{1,0:T(8,128)}, u32[]{:S(2)}) copy-start(f32[128,512]{1,0:T(8,128)} %noise.1) | copy-start | bytes 786436
  3.1 3.1 %collective-permute-start = (f32[64,512]{1,0:T(8,128)S(1)}, f32[64,512]{1,0:T(8,128)S(1)}, u32[]{:S(2)}, u32[]{:S(2)}) collective-permute-start(f32[64,512]{1,0:T(8,128)S(1)} %get-tuple-element.27), channel_id=1, source_target_pairs={{0,1},{1,0},{2,3},{3,2},{4,5},{5,4},{6,7},{7,6},{8,9},{9,8},{10,11... | collective-permute-start | bytes 393224 | tf_op jit(solution)/shard_map/ppermute | solution.py:408
  3.7 5.6 %collective-permute-start.2 = (f32[128,128]{1,0:T(8,128)S(1)}, f32[128,128]{1,0:T(8,128)S(1)}, u32[]{:S(2)}, u32[]{:S(2)}) collective-permute-start(f32[128,128]{1,0:T(8,128)S(1)} %slice.12), channel_id=1, source_target_pairs={{0,16},{1,17},{2,18},{3,19},{4,20},{5,21},{6,22},{7,23},{8,24},{9,... | collective-permute-start | bytes 196616 | tf_op jit(solution)/shard_map/ppermute | solution.py:408
  6.3 4.3 %collective-permute-start.1 = (f32[32,512]{1,0:T(8,128)S(1)}, f32[32,512]{1,0:T(8,128)S(1)}, u32[]{:S(2)}, u32[]{:S(2)}) collective-permute-start(f32[32,512]{1,0:T(8,128)S(1)} %constant_dynamic-slice_fusion), channel_id=1, source_target_pairs={{0,2},{1,3},{2,0},{3,1},{4,6},{5,7},{6,4},{7,5},{8,10},{9,11},{10,... | collective-permute-start | bytes 196616 | tf_op jit(solution)/shard_map/ppermute | solution.py:408
  7.9 11.8 %collective-permute-start.6 = (f32[128,640]{1,0:T(8,128)S(1)}, f32[128,640]{1,0:T(8,128)S(1)}, u32[]{:S(2)}, u32[]{:S(2)}) collective-permute-start(f32[128,640]{1,0:T(8,128)S(1)} %slice.13), channel_id=1, source_target_pairs={{0,16},{1,17},{2,18},{3,19},{4,20},{5,21},{6,22},{7,23},{8,24},{9,... | collective-permute-start | bytes 983048 | tf_op jit(solution)/shard_map/ppermute | solution.py:408
  10.6 6.5 %collective-permute-start.5 = (f32[32,512]{1,0:T(8,128)S(1)}, f32[32,512]{1,0:T(8,128)S(1)}, u32[]{:S(2)}, u32[]{:S(2)}) collective-permute-start(f32[32,512]{1,0:T(8,128)S(1)} %dynamic-slice_add_fusion), channel_id=1, source_target_pairs={{0,12},{1,13},{2,14},{3,15},{4,8},{5,9},{6,10},{7,11},{8,4},{9,5},... | collective-permute-start | bytes 196616 | tf_op jit(solution)/shard_map/ppermute | solution.py:408
  14.3 5.4 %collective-permute-start.4 = (f32[32,512]{1,0:T(8,128)S(1)}, f32[32,512]{1,0:T(8,128)S(1)}, u32[]{:S(2)}, u32[]{:S(2)}) collective-permute-start(f32[32,512]{1,0:T(8,128)S(1)} %dynamic-slice_add_fusion), channel_id=1, source_target_pairs={{0,8},{1,9},{2,10},{3,11},{4,12},{5,13},{6,14},{7,15},{8,0},{9,1},... | collective-permute-start | bytes 196616 | tf_op jit(solution)/shard_map/ppermute | solution.py:408
  14.3 5.4 %collective-permute-start.3 = (f32[32,512]{1,0:T(8,128)S(1)}, f32[32,512]{1,0:T(8,128)S(1)}, u32[]{:S(2)}, u32[]{:S(2)}) collective-permute-start(f32[32,512]{1,0:T(8,128)S(1)} %dynamic-slice_add_fusion), channel_id=1, source_target_pairs={{0,4},{1,5},{2,6},{3,7},{4,0},{5,1},{6,2},{7,3},{8,12},{9,13},{10,... | collective-permute-start | bytes 196616 | tf_op jit(solution)/shard_map/ppermute | solution.py:408
  15.8 8.8 %collective-permute-start.8 = (f32[128,384]{1,0:T(8,128)S(1)}, f32[128,384]{1,0:T(8,128)S(1)}, u32[]{:S(2)}, u32[]{:S(2)}) collective-permute-start(f32[128,384]{1,0:T(8,128)S(1)} %slice.14), channel_id=1, source_target_pairs={{0,16},{1,17},{2,18},{3,19},{4,20},{5,21},{6,22},{7,23},{8,24},{9,... | collective-permute-start | bytes 589832 | tf_op jit(solution)/shard_map/ppermute | solution.py:408
  19.7 4.9 %collective-permute-start.7 = (f32[32,512]{1,0:T(8,128)S(1)}, f32[32,512]{1,0:T(8,128)S(1)}, u32[]{:S(2)}, u32[]{:S(2)}) collective-permute-start(f32[32,512]{1,0:T(8,128)S(1)} %add_add_fusion.refs_0_), channel_id=1, source_target_pairs={{0,2},{1,3},{2,0},{3,1},{4,6},{5,7},{6,4},{7,5},{8,10},{9,11},{10,... | collective-permute-start | bytes 196616 | tf_op jit(solution)/shard_map/ppermute | solution.py:408
  21.3 5.9 %collective-permute-start.10 = (f32[32,512]{1,0:T(8,128)S(1)}, f32[32,512]{1,0:T(8,128)S(1)}, u32[]{:S(2)}, u32[]{:S(2)}) collective-permute-start(f32[32,512]{1,0:T(8,128)S(1)} %add_add_fusion.refs_0_), channel_id=1, source_target_pairs={{0,18},{1,19},{2,16},{3,17},{4,22},{5,23},{6,20},{7,21},{8,26},{9,... | collective-permute-start | bytes 196616 | tf_op jit(solution)/shard_map/ppermute | solution.py:408
  22.5 5.2 %collective-permute-start.9 = (f32[32,512]{1,0:T(8,128)S(1)}, f32[32,512]{1,0:T(8,128)S(1)}, u32[]{:S(2)}, u32[]{:S(2)}) collective-permute-start(f32[32,512]{1,0:T(8,128)S(1)} %add_add_fusion.refs_0_), channel_id=1, source_target_pairs={{0,16},{1,17},{2,18},{3,19},{4,20},{5,21},{6,22},{7,23},{8,24},{9,... | collective-permute-start | bytes 196616 | tf_op jit(solution)/shard_map/ppermute | solution.py:408
  23.3 12.3 %collective-permute-start.15 = (f32[128,896]{1,0:T(8,128)S(1)}, f32[128,896]{1,0:T(8,128)S(1)}, u32[]{:S(2)}, u32[]{:S(2)}) collective-permute-start(f32[128,896]{1,0:T(8,128)S(1)} %slice.15), channel_id=1, source_target_pairs={{0,16},{1,17},{2,18},{3,19},{4,20},{5,21},{6,22},{7,23},{8,24},{9,... | collective-permute-start | bytes 1376264 | tf_op jit(solution)/shard_map/ppermute | solution.py:408
  24.6 6.3 %collective-permute-start.11 = (f32[32,512]{1,0:T(8,128)S(1)}, f32[32,512]{1,0:T(8,128)S(1)}, u32[]{:S(2)}, u32[]{:S(2)}) collective-permute-start(f32[32,512]{1,0:T(8,128)S(1)} %add_add_fusion.refs_0_), channel_id=1, source_target_pairs={{0,1},{1,0},{2,3},{3,2},{4,5},{5,4},{6,7},{7,6},{8,9},{9,8},{10,11... | collective-permute-start | bytes 196616 | tf_op jit(solution)/shard_map/ppermute | solution.py:408
  24.6 6.3 %collective-permute-start.12 = (f32[32,512]{1,0:T(8,128)S(1)}, f32[32,512]{1,0:T(8,128)S(1)}, u32[]{:S(2)}, u32[]{:S(2)}) collective-permute-start(f32[32,512]{1,0:T(8,128)S(1)} %collective-permute-done.7.refs_1_), channel_id=1, source_target_pairs={{0,1},{1,0},{2,3},{3,2},{4,5},{5,4},{6,7},{7,6},{8,9},{9,8},{10,11... | collective-permute-start | bytes 196616 | tf_op jit(solution)/shard_map/ppermute | solution.py:408
  27.2 3.6 %collective-permute-start.14 = (f32[32,512]{1,0:T(8,128)S(1)}, f32[32,512]{1,0:T(8,128)S(1)}, u32[]{:S(2)}, u32[]{:S(2)}) collective-permute-start(f32[32,512]{1,0:T(8,128)S(1)} %collective-permute-done.10.refs_3_), channel_id=1, source_target_pairs={{0,1},{1,0},{2,3},{3,2},{4,5},{5,4},{6,7},{7,6},{8,9},{9,8},{10,11... | collective-permute-start | bytes 196616 | tf_op jit(solution)/shard_map/ppermute | solution.py:408
  27.7 3.2 %collective-permute-start.13 = (f32[32,512]{1,0:T(8,128)S(1)}, f32[32,512]{1,0:T(8,128)S(1)}, u32[]{:S(2)}, u32[]{:S(2)}) collective-permute-start(f32[32,512]{1,0:T(8,128)S(1)} %collective-permute-done.9.refs_2_), channel_id=1, source_target_pairs={{0,1},{1,0},{2,3},{3,2},{4,5},{5,4},{6,7},{7,6},{8,9},{9,8},{10,11... | collective-permute-start | bytes 196616 | tf_op jit(solution)/shard_map/ppermute | solution.py:408

commit v11 on v10

--- a/solution.py
+++ b/solution.py
@@ -17,7 +17,7 @@
 VMEM_LIMIT = 20 << 20
 PARTS = 16
 CUTS = (0, 1, 6, 9, 16)
-STEP = 2
+STEP = 4
 
 
 def dot(a, b, dims, precision=HIGHEST):
@@ -291,10 +291,11 @@
 
 
 def solve_kernel(places, *refs):
-    count = len(places)
-    pieces = refs[:count]
-    inverse, near, shift, target, root, weights = refs[count : count + 6]
-    fwd, gram, buf, low, scaled, second, far_z, right, out = refs[count + 6 :]
+    count = len(places) // 2
+    pieces = list(refs[:count])
+    far_rows, inverse, near, shift, target, root, weights = refs[count : count + 7]
+    fwd, gram, buf, low, scaled, second, far_z, right, out = refs[count + 7 :]
+    pieces += [far_rows.at[i * pieces[0].shape[0] : (i + 1) * pieces[0].shape[0], :] for i in range(count)]
     rows = pieces[0].shape[0]
     own, size = target.shape[0], near.shape[0]
     members = 2 * size
@@ -310,8 +311,7 @@
         if place[0] == 0:
             fwd[pl.ds(start(place), rows), :] = piece[...]
     scale = root[0:1, :]
-    for i, piece in enumerate(pieces[count // 2 :]):
-        far_z[i * rows : (i + 1) * rows, :] = (piece[...] - shift[0:1, :]) * scale
+    far_z[...] = (far_rows[...] - shift[0:1, :]) * scale
     residual = (target[...] - fwd[...]) * scale
     za, zb = near[...], far_z[...]
     side = dot3(zb, za, ((1,), (1,)))
@@ -337,13 +337,13 @@
     weights[...] = out[...].T
 
 
-def solve(pieces, places, inverse, near, shift, target, root):
+def solve(pieces, far_rows, places, inverse, near, shift, target, root):
     own, cols = target.shape
     size = near.shape[0]
     return pl.pallas_call(
         functools.partial(solve_kernel, places),
         out_shape=jax.ShapeDtypeStruct((own, 2 * size), f32),
-        in_specs=[VMEM] * (len(pieces) + 5),
+        in_specs=[VMEM] * (len(pieces) + 6),
         out_specs=VMEM,
         scratch_shapes=[pltpu.VMEM((own, cols), f32)]
         + solve_scratch(size)
@@ -356,7 +356,7 @@
         cost_estimate=pl.CostEstimate(flops=5_000_000_000, bytes_accessed=1, transcendentals=0),
         compiler_params=pltpu.CompilerParams(vmem_limit_bytes=VMEM_LIMIT),
         name="solve",
-    )(*pieces, inverse, near, shift, target, root)
+    )(*pieces, far_rows, inverse, near, shift, target, root)
 
 
 def update_kernel(weights, own_ens, *refs):
@@ -433,10 +433,10 @@
     last, _ = lax.optimization_barrier((last, total))
     last = [swap(last, far, 0) for far in range(1, n_mem)]
     inverse, near, shift = solve_near(pieces, root, ensemble.shape[0] * n_mem)
-    mine, pieces[1], third = lax.optimization_barrier((pieces[0], pieces[1], third))
-    pieces += [swap(piece, 0, 1) for piece in [mine] + pieces[1:]]
+    third, pieces[1] = lax.optimization_barrier((third, pieces[1]))
+    far_rows = swap(jnp.concatenate(pieces, axis=0), 0, 1)
     places += [(far, dy, 1) for far, dy, _ in places]
-    weights = solve(pieces, places, inverse, near, shift, target, root)
+    weights = solve(pieces, far_rows, places, inverse, near, shift, target, root)
     return update(weights, ensemble, [part for far in zip(first, second, third, last) for part in far])
 
 

time: 37.2 us -> 37.3 us (level)
  waiting for transfers between devices: 6.5 us -> 7.01 us
  starting transfers between devices: 17.2 us -> 16.7 us
    ppermute x16 -> x13, waiting for transfers between devices: 6.5 us -> 7.01 us  [swap(): return lax.ppermute(x, ('mem', 'par'), pairs)]
    ppermute x16 -> x13, starting transfers between devices: 17.2 us -> 16.7 us  [swap(): return lax.ppermute(x, ('mem', 'par'), pairs)]
  transfers between devices with their start and end apart: 16 -> 13, of which waited for: 4 -> 4; matrix products, arithmetic and copies ran while one was open for 0% -> 0% of each run, Pallas kernels for 23% -> 23%
where the time goes in v11:
time: 37.3 us; the launch traced here: 37.1 us
  starting transfers between devices  16.7 us (45%)
  Pallas kernels  13.1 us (35%)
  waiting for transfers between devices  7.01 us (19%)
    ppermute x13, starting transfers between devices, swap(): return lax.ppermute(x, ('mem', 'par'), pairs)  16.7 us
    ppermute x13, waiting for transfers between devices, swap(): return lax.ppermute(x, ('mem', 'par'), pairs)  7.01 us
    pallas_call x1, Pallas kernels, solve(): pl.pallas_call(functools.partial(solve_kernel, places), out_shape=jax.Sha...  4.63 us
    pallas_call x1, Pallas kernels, solve_near(): pl.pallas_call(functools.partial(near_kernel, members, len(pieces)), out_...  3.11 us
    pallas_call x1, Pallas kernels, forward(): pl.pallas_call(functools.partial(forward_kernel, steps), out_shape=(half,...  3.1 us
    pallas_call x1, Pallas kernels, update(): pl.pallas_call(update_kernel, out_shape=jax.ShapeDtypeStruct((own, params...  1.55 us
  transfers between devices with their start and end apart: 13, of which 4 were waited for; matrix products, arithmetic and copies ran while one was open for 0% of the time, Pallas kernels for 23%

profile of v11, /device:TPU:0, one launch (start us, length us, event | category | flops | bytes accessed | tf_op | source)
XLA Modules:
  0.0 37.1 jit_solution(9476063567690042322)
XLA Ops:
  0.0 3.1 %forward.1 = (f32[64,512]{1,0:T(8,128)S(1)}, f32[64,512]{1,0:T(8,128)S(1)}) custom-call(f32[128,2048]{1,0:T(8,128)} %own_ens.1, f32[2048,512]{1,0:T(8,128)} %op.1), custom_call_target="tpu_custom_call" | custom-call | flops 268435456 | bytes 5242880 | tf_op jit(solution)/shard_map/forward/pallas_call | solution.py:187
  3.1 0.5 %collective-permute-start = (f32[64,512]{1,0:T(8,128)S(1)}, f32[64,512]{1,0:T(8,128)S(1)}, u32[]{:S(2)}, u32[]{:S(2)}) collective-permute-start(f32[64,512]{1,0:T(8,128)S(1)} %get-tuple-element.26), channel_id=1, source_target_pairs={{0,1},{1,0},{2,3},{3,2},{4,5},{5,4},{6,7},{7,6},{8,9},{9,8},{10,11... | collective-permute-start | bytes 393224 | tf_op jit(solution)/shard_map/ppermute | solution.py:408
  3.7 2.6 %collective-permute-start.2 = (f32[128,128]{1,0:T(8,128)S(1)}, f32[128,128]{1,0:T(8,128)S(1)}, u32[]{:S(2)}, u32[]{:S(2)}) collective-permute-start(f32[128,128]{1,0:T(8,128)S(1)} %slice.12), channel_id=1, source_target_pairs={{0,16},{1,17},{2,18},{3,19},{4,20},{5,21},{6,22},{7,23},{8,24},{9,... | collective-permute-start | bytes 196616 | tf_op jit(solution)/shard_map/ppermute | solution.py:408
  6.2 0.0 collective-permute-done
  6.3 1.6 %collective-permute-start.1 = (f32[32,512]{1,0:T(8,128)S(1)}, f32[32,512]{1,0:T(8,128)S(1)}, u32[]{:S(2)}, u32[]{:S(2)}) collective-permute-start(f32[32,512]{1,0:T(8,128)S(1)} %constant_dynamic-slice_fusion), channel_id=1, source_target_pairs={{0,2},{1,3},{2,0},{3,1},{4,6},{5,7},{6,4},{7,5},{8,10},{9,11},{10,... | collective-permute-start | bytes 196616 | tf_op jit(solution)/shard_map/ppermute | solution.py:408
  7.9 1.3 %collective-permute-start.6 = (f32[128,640]{1,0:T(8,128)S(1)}, f32[128,640]{1,0:T(8,128)S(1)}, u32[]{:S(2)}, u32[]{:S(2)}) collective-permute-start(f32[128,640]{1,0:T(8,128)S(1)} %slice.13), channel_id=1, source_target_pairs={{0,16},{1,17},{2,18},{3,19},{4,20},{5,21},{6,22},{7,23},{8,24},{9,... | collective-permute-start | bytes 983048 | tf_op jit(solution)/shard_map/ppermute | solution.py:408
  9.2 1.4 %collective-permute-done.1 = f32[32,512]{1,0:T(8,128)S(1)} collective-permute-done((f32[32,512]{1,0:T(8,128)S(1)}, f32[32,512]{1,0:T(8,128)S(1)}, u32[]{:S(2)}, u32[]{:S(2)}) %collective-permute-start.1) | collective-permute-done | bytes 65568 | tf_op jit(solution)/shard_map/ppermute | solution.py:408
  10.6 3.7 %collective-permute-start.5 = (f32[32,512]{1,0:T(8,128)S(1)}, f32[32,512]{1,0:T(8,128)S(1)}, u32[]{:S(2)}, u32[]{:S(2)}) collective-permute-start(f32[32,512]{1,0:T(8,128)S(1)} %dynamic-slice_add_fusion), channel_id=1, source_target_pairs={{0,12},{1,13},{2,14},{3,15},{4,8},{5,9},{6,10},{7,11},{8,4},{9,5},... | collective-permute-start | bytes 196616 | tf_op jit(solution)/shard_map/ppermute | solution.py:408
  14.3 0.8 %collective-permute-start.3 = (f32[32,512]{1,0:T(8,128)S(1)}, f32[32,512]{1,0:T(8,128)S(1)}, u32[]{:S(2)}, u32[]{:S(2)}) collective-permute-start(f32[32,512]{1,0:T(8,128)S(1)} %dynamic-slice_add_fusion), channel_id=1, source_target_pairs={{0,4},{1,5},{2,6},{3,7},{4,0},{5,1},{6,2},{7,3},{8,12},{9,13},{10,... | collective-permute-start | bytes 196616 | tf_op jit(solution)/shard_map/ppermute | solution.py:408
  15.1 0.7 %lookup.1 = (f32[128,512]{1,0:T(8,128)S(1)}, f32[8,512]{1,0:T(8,128)S(1)}) custom-call(s32[1,512]{1,0:T(1,128)S(1)} %bitcast.5, f32[128,128]{1,0:T(8,128)S(1)} %bitcast.3, f32[128,128]{1,0:T(8,128)S(1)} %bitcast.4, f32[128,512]{1,0:T(8,128)S(1)} %copy-done.1), custom_call_target="tpu_custom_call" | custom-call | flops 25769803776 | bytes 1048576 | tf_op jit(solution)/shard_map/lookup/pallas_call | solution.py:222
  15.8 1.3 %collective-permute-start.7 = (f32[128,384]{1,0:T(8,128)S(1)}, f32[128,384]{1,0:T(8,128)S(1)}, u32[]{:S(2)}, u32[]{:S(2)}) collective-permute-start(f32[128,384]{1,0:T(8,128)S(1)} %slice.14), channel_id=1, source_target_pairs={{0,16},{1,17},{2,18},{3,19},{4,20},{5,21},{6,22},{7,23},{8,24},{9,... | collective-permute-start | bytes 589832 | tf_op jit(solution)/shard_map/ppermute | solution.py:408
  17.1 2.5 %collective-permute-done.4 = f32[32,512]{1,0:T(8,128)S(1)} collective-permute-done((f32[32,512]{1,0:T(8,128)S(1)}, f32[32,512]{1,0:T(8,128)S(1)}, u32[]{:S(2)}, u32[]{:S(2)}) %collective-permute-start.4) | collective-permute-done | bytes 65568 | tf_op jit(solution)/shard_map/ppermute | solution.py:408
  19.7 0.0 collective-permute-done.3
  19.7 0.0 collective-permute-done.6.refs_1_
  19.7 1.6 %collective-permute-start.8 = (f32[32,512]{1,0:T(8,128)S(1)}, f32[32,512]{1,0:T(8,128)S(1)}, u32[]{:S(2)}, u32[]{:S(2)}) collective-permute-start(f32[32,512]{1,0:T(8,128)S(1)} %add_add_fusion.refs_0_), channel_id=1, source_target_pairs={{0,2},{1,3},{2,0},{3,1},{4,6},{5,7},{6,4},{7,5},{8,10},{9,11},{10,... | collective-permute-start | bytes 196616 | tf_op jit(solution)/shard_map/ppermute | solution.py:408
  21.3 1.2 %collective-permute-start.10 = (f32[32,512]{1,0:T(8,128)S(1)}, f32[32,512]{1,0:T(8,128)S(1)}, u32[]{:S(2)}, u32[]{:S(2)}) collective-permute-start(f32[32,512]{1,0:T(8,128)S(1)} %add_add_fusion.refs_0_), channel_id=1, source_target_pairs={{0,18},{1,19},{2,16},{3,17},{4,22},{5,23},{6,20},{7,21},{8,26},{9,... | collective-permute-start | bytes 196616 | tf_op jit(solution)/shard_map/ppermute | solution.py:408
  22.5 0.8 %collective-permute-start.9 = (f32[32,512]{1,0:T(8,128)S(1)}, f32[32,512]{1,0:T(8,128)S(1)}, u32[]{:S(2)}, u32[]{:S(2)}) collective-permute-start(f32[32,512]{1,0:T(8,128)S(1)} %add_add_fusion.refs_0_), channel_id=1, source_target_pairs={{0,16},{1,17},{2,18},{3,19},{4,20},{5,21},{6,22},{7,23},{8,24},{9,... | collective-permute-start | bytes 196616 | tf_op jit(solution)/shard_map/ppermute | solution.py:408
  23.3 1.3 %collective-permute-start.12 = (f32[128,896]{1,0:T(8,128)S(1)}, f32[128,896]{1,0:T(8,128)S(1)}, u32[]{:S(2)}, u32[]{:S(2)}) collective-permute-start(f32[128,896]{1,0:T(8,128)S(1)} %slice.15), channel_id=1, source_target_pairs={{0,16},{1,17},{2,18},{3,19},{4,20},{5,21},{6,22},{7,23},{8,24},{9,... | collective-permute-start | bytes 1376264 | tf_op jit(solution)/shard_map/ppermute | solution.py:408
  24.6 2.6 %collective-permute-done.10.refs_3_ = f32[32,512]{1,0:T(8,128)S(1)} collective-permute-done((f32[32,512]{1,0:T(8,128)S(1)}, f32[32,512]{1,0:T(8,128)S(1)}, u32[]{:S(2)}, u32[]{:S(2)}) %collective-permute-start.10) | collective-permute-done | bytes 65568 | tf_op jit(solution)/shard_map/ppermute | solution.py:408
  27.2 0.4 %collective-permute-done.9.refs_2_ = f32[32,512]{1,0:T(8,128)S(1)} collective-permute-done((f32[32,512]{1,0:T(8,128)S(1)}, f32[32,512]{1,0:T(8,128)S(1)}, u32[]{:S(2)}, u32[]{:S(2)}) %collective-permute-start.9) | collective-permute-done | bytes 65568 | tf_op jit(solution)/shard_map/ppermute | solution.py:408
  27.7 0.1 collective-permute-start.11
  27.8 3.1 %solve_near.1 = (f32[128,128]{1,0:T(8,128)S(1)}, f32[128,512]{1,0:T(8,128)S(1)}, f32[8,512]{1,0:T(8,128)S(1)}) custom-call(f32[32,512]{1,0:T(8,128)S(1)} %add_add_fusion.refs_0_, f32[32,512]{1,0:T(8,128)S(1)} %collective-permute-done.8.refs_1_, f32[32,512]{1,0:T(8,128)S(1)} %collective-permute-done.9.refs_2_, f32[32,512]{1,0:T(8,128)S(1)} %collective-permute-done.10.refs_3_, ...), custom_call_target="tpu_custom_call" | custom-call | flops 5000000000 | bytes 1 | tf_op jit(solution)/shard_map/solve_near/pallas_call | solution.py:272
  30.9 4.6 %solve.1.weights = f32[128,256]{1,0:T(8,128)S(1)} custom-call(f32[32,512]{1,0:T(8,128)S(1)} %add_add_fusion.refs_0_, f32[32,512]{1,0:T(8,128)S(1)} %collective-permute-done.8.refs_1_, f32[32,512]{1,0:T(8,128)S(1)} %collective-permute-done.9.refs_2_, f32[32,512]{1,0:T(8,128)S(1)} %collective-permute-done.10.refs_3_, ...), custom_call_target="tpu_custom_call" | custom-call | flops 5000000000 | bytes 1 | tf_op jit(solution)/shard_map/solve/pallas_call | solution.py:343
  35.5 1.5 %update.1 = f32[128,2048]{1,0:T(8,128)} custom-call(f32[128,256]{1,0:T(8,128)S(1)} %solve.1.weights, f32[128,2048]{1,0:T(8,128)S(1)} %copy-done, f32[128,128]{1,0:T(8,128)S(1)} %collective-permute-done.2.refs_0_, f32[128,640]{1,0:T(8,128)S(1)} %collective-permute-done.6.refs_1_, f32[128,384]{1,0:T(8,128)S(1)} %collective-permute-done.7.refs_2_, ...), custom_call_target="tpu_custom_call" | custom-call | flops 134217728 | bytes 3145728 | tf_op jit(solution)/shard_map/update/pallas_call | solution.py:386
  (26 shorter events, 0.2 us)
Async XLA Ops:
  0.0 3.7 %copy-start = (f32[128,2048]{1,0:T(8,128)S(1)}, f32[128,2048]{1,0:T(8,128)}, u32[]{:S(2)}) copy-start(f32[128,2048]{1,0:T(8,128)} %own_ens.1) | copy-start | bytes 3145732
  0.0 15.1 %copy-start.4 = (s32[512]{0:T(512)S(1)}, s32[512]{0:T(512)}, u32[]{:S(2)}) copy-start(s32[512]{0:T(512)} %param.11) | copy-start | bytes 6148
  0.0 15.1 %copy-start.3 = (f32[16384]{0:T(1024)S(1)}, f32[16384]{0:T(1024)}, u32[]{:S(2)}) copy-start(f32[16384]{0:T(1024)} %param.10) | copy-start | bytes 196612
  0.0 15.1 %copy-start.2 = (f32[16384]{0:T(1024)S(1)}, f32[16384]{0:T(1024)}, u32[]{:S(2)}) copy-start(f32[16384]{0:T(1024)} %param.9) | copy-start | bytes 196612
  0.0 15.1 %copy-start.1 = (f32[128,512]{1,0:T(8,128)S(1)}, f32[128,512]{1,0:T(8,128)}, u32[]{:S(2)}) copy-start(f32[128,512]{1,0:T(8,128)} %noise.1) | copy-start | bytes 786436
  3.1 3.1 %collective-permute-start = (f32[64,512]{1,0:T(8,128)S(1)}, f32[64,512]{1,0:T(8,128)S(1)}, u32[]{:S(2)}, u32[]{:S(2)}) collective-permute-start(f32[64,512]{1,0:T(8,128)S(1)} %get-tuple-element.26), channel_id=1, source_target_pairs={{0,1},{1,0},{2,3},{3,2},{4,5},{5,4},{6,7},{7,6},{8,9},{9,8},{10,11... | collective-permute-start | bytes 393224 | tf_op jit(solution)/shard_map/ppermute | solution.py:408
  3.7 5.6 %collective-permute-start.2 = (f32[128,128]{1,0:T(8,128)S(1)}, f32[128,128]{1,0:T(8,128)S(1)}, u32[]{:S(2)}, u32[]{:S(2)}) collective-permute-start(f32[128,128]{1,0:T(8,128)S(1)} %slice.12), channel_id=1, source_target_pairs={{0,16},{1,17},{2,18},{3,19},{4,20},{5,21},{6,22},{7,23},{8,24},{9,... | collective-permute-start | bytes 196616 | tf_op jit(solution)/shard_map/ppermute | solution.py:408
  6.3 4.3 %collective-permute-start.1 = (f32[32,512]{1,0:T(8,128)S(1)}, f32[32,512]{1,0:T(8,128)S(1)}, u32[]{:S(2)}, u32[]{:S(2)}) collective-permute-start(f32[32,512]{1,0:T(8,128)S(1)} %constant_dynamic-slice_fusion), channel_id=1, source_target_pairs={{0,2},{1,3},{2,0},{3,1},{4,6},{5,7},{6,4},{7,5},{8,10},{9,11},{10,... | collective-permute-start | bytes 196616 | tf_op jit(solution)/shard_map/ppermute | solution.py:408
  7.9 11.8 %collective-permute-start.6 = (f32[128,640]{1,0:T(8,128)S(1)}, f32[128,640]{1,0:T(8,128)S(1)}, u32[]{:S(2)}, u32[]{:S(2)}) collective-permute-start(f32[128,640]{1,0:T(8,128)S(1)} %slice.13), channel_id=1, source_target_pairs={{0,16},{1,17},{2,18},{3,19},{4,20},{5,21},{6,22},{7,23},{8,24},{9,... | collective-permute-start | bytes 983048 | tf_op jit(solution)/shard_map/ppermute | solution.py:408
  10.6 6.5 %collective-permute-start.5 = (f32[32,512]{1,0:T(8,128)S(1)}, f32[32,512]{1,0:T(8,128)S(1)}, u32[]{:S(2)}, u32[]{:S(2)}) collective-permute-start(f32[32,512]{1,0:T(8,128)S(1)} %dynamic-slice_add_fusion), channel_id=1, source_target_pairs={{0,12},{1,13},{2,14},{3,15},{4,8},{5,9},{6,10},{7,11},{8,4},{9,5},... | collective-permute-start | bytes 196616 | tf_op jit(solution)/shard_map/ppermute | solution.py:408
  14.3 5.4 %collective-permute-start.4 = (f32[32,512]{1,0:T(8,128)S(1)}, f32[32,512]{1,0:T(8,128)S(1)}, u32[]{:S(2)}, u32[]{:S(2)}) collective-permute-start(f32[32,512]{1,0:T(8,128)S(1)} %dynamic-slice_add_fusion), channel_id=1, source_target_pairs={{0,8},{1,9},{2,10},{3,11},{4,12},{5,13},{6,14},{7,15},{8,0},{9,1},... | collective-permute-start | bytes 196616 | tf_op jit(solution)/shard_map/ppermute | solution.py:408
  14.3 5.4 %collective-permute-start.3 = (f32[32,512]{1,0:T(8,128)S(1)}, f32[32,512]{1,0:T(8,128)S(1)}, u32[]{:S(2)}, u32[]{:S(2)}) collective-permute-start(f32[32,512]{1,0:T(8,128)S(1)} %dynamic-slice_add_fusion), channel_id=1, source_target_pairs={{0,4},{1,5},{2,6},{3,7},{4,0},{5,1},{6,2},{7,3},{8,12},{9,13},{10,... | collective-permute-start | bytes 196616 | tf_op jit(solution)/shard_map/ppermute | solution.py:408
  15.8 8.8 %collective-permute-start.7 = (f32[128,384]{1,0:T(8,128)S(1)}, f32[128,384]{1,0:T(8,128)S(1)}, u32[]{:S(2)}, u32[]{:S(2)}) collective-permute-start(f32[128,384]{1,0:T(8,128)S(1)} %slice.14), channel_id=1, source_target_pairs={{0,16},{1,17},{2,18},{3,19},{4,20},{5,21},{6,22},{7,23},{8,24},{9,... | collective-permute-start | bytes 589832 | tf_op jit(solution)/shard_map/ppermute | solution.py:408
  19.7 4.9 %collective-permute-start.8 = (f32[32,512]{1,0:T(8,128)S(1)}, f32[32,512]{1,0:T(8,128)S(1)}, u32[]{:S(2)}, u32[]{:S(2)}) collective-permute-start(f32[32,512]{1,0:T(8,128)S(1)} %add_add_fusion.refs_0_), channel_id=1, source_target_pairs={{0,2},{1,3},{2,0},{3,1},{4,6},{5,7},{6,4},{7,5},{8,10},{9,11},{10,... | collective-permute-start | bytes 196616 | tf_op jit(solution)/shard_map/ppermute | solution.py:408
  21.3 5.9 %collective-permute-start.10 = (f32[32,512]{1,0:T(8,128)S(1)}, f32[32,512]{1,0:T(8,128)S(1)}, u32[]{:S(2)}, u32[]{:S(2)}) collective-permute-start(f32[32,512]{1,0:T(8,128)S(1)} %add_add_fusion.refs_0_), channel_id=1, source_target_pairs={{0,18},{1,19},{2,16},{3,17},{4,22},{5,23},{6,20},{7,21},{8,26},{9,... | collective-permute-start | bytes 196616 | tf_op jit(solution)/shard_map/ppermute | solution.py:408
  22.5 5.2 %collective-permute-start.9 = (f32[32,512]{1,0:T(8,128)S(1)}, f32[32,512]{1,0:T(8,128)S(1)}, u32[]{:S(2)}, u32[]{:S(2)}) collective-permute-start(f32[32,512]{1,0:T(8,128)S(1)} %add_add_fusion.refs_0_), channel_id=1, source_target_pairs={{0,16},{1,17},{2,18},{3,19},{4,20},{5,21},{6,22},{7,23},{8,24},{9,... | collective-permute-start | bytes 196616 | tf_op jit(solution)/shard_map/ppermute | solution.py:408
  23.3 12.2 %collective-permute-start.12 = (f32[128,896]{1,0:T(8,128)S(1)}, f32[128,896]{1,0:T(8,128)S(1)}, u32[]{:S(2)}, u32[]{:S(2)}) collective-permute-start(f32[128,896]{1,0:T(8,128)S(1)} %slice.15), channel_id=1, source_target_pairs={{0,16},{1,17},{2,18},{3,19},{4,20},{5,21},{6,22},{7,23},{8,24},{9,... | collective-permute-start | bytes 1376264 | tf_op jit(solution)/shard_map/ppermute | solution.py:408
  27.7 3.2 %collective-permute-start.11 = (f32[128,512]{1,0:T(8,128)S(1)}, f32[128,512]{1,0:T(8,128)S(1)}, u32[]{:S(2)}, u32[]{:S(2)}) collective-permute-start(f32[128,512]{1,0:T(8,128)S(1)} %pad_maximum_fusion), channel_id=1, source_target_pairs={{0,1},{1,0},{2,3},{3,2},{4,5},{5,4},{6,7},{7,6},{8,9},{9,8},{10,11... | collective-permute-start | bytes 786440 | tf_op jit(solution)/shard_map/ppermute | solution.py:408
